TPU v7x, 128 devices: a whole 4x4x4 slice. The times are simulated.
128 devices in a mesh: lat: 8 (over x, core), lon: 16 (over y, z).
Axes of the slice: x: 4, y: 4, z: 4, core: 2. Of those that a mesh axis runs over, the one named last changes fastest.
Arguments:
- model_state: bfloat16 [256, 2048, 256], P('lat', 'lon'), may hold values from -6 to 6
- tangent_slope: bfloat16 [256, 2048, 256], P('lat', 'lon'), may hold values from 0.19921875 to 1.1953125
- conv_weight: bfloat16 [3, 3, 256, 256], replicated, may hold values from -0.125 to 0.125
- weight_in: bfloat16 [256, 512], replicated, may hold values from -0.375 to 0.375
- bias_in: float32 [512], replicated, may hold values from -3 to 3
- weight_mid: bfloat16 [512, 512], replicated, may hold values from -0.25 to 0.25
- bias_mid: float32 [512], replicated, may hold values from -3 to 3
- weight_out: bfloat16 [512, 384], replicated, may hold values from -0.25 to 0.25
- bias_out: float32 [384], replicated, may hold values from -3 to 3
- obs_tile: int32 [65536, 1], P(('lat', 'lon')), may hold values from 0 to 127; in each aligned block of 512 rows (0 to 511, 512 to 1023, ...) at most 8 rows name the same one
- obs_cell: int32 [65536], P(('lat', 'lon')), may hold values from 0 to 3966, as said below
- obs_frac: float32 [65536, 2], P(('lat', 'lon')), may hold values from 0 to 1
- radiance: bfloat16 [65536, 384], P(('lat', 'lon')), may hold values from -6 to 6
- inv_error: float32 [384], replicated, may hold values from 0.5 to 2
Outputs:
- departures: float32 [65536, 384], P(('lat', 'lon'))
- gradient: float32 [256, 2048, 256], P('lat', 'lon')
Inputs may be any that keep to these rules, and one draw needn't show every extreme that they name: `obs_tile`: among the rows of one device, at most 8 name the same tile. `obs_cell`: row k // 128 is at most 30 and column k % 128 at most 126.
All inputs are finite; a program needn't handle non-finite values.
Results may differ from a plain program's by a relative error of at most 0.0078.
Values may be sent and summed in bfloat16 or wider, within the bound.
No kernel may reach another device: no remote copies, remote signals or barrier semaphores. Data moves between devices by JAX's collectives and lax.ppermute only.
A program may use at most 64 MiB of HBM per device.

v0:
```python
import functools

import jax
import jax.numpy as jnp
from jax import lax
from jax.experimental import pallas as pl
from jax.experimental.pallas import tpu as pltpu
from jax.sharding import PartitionSpec as P

F32 = jnp.float32
BF16 = jnp.bfloat16
META = 128
FIELDS = 6
VMEM_LIMIT = 40 * 1024 * 1024


def dot_nt(left, right):
    return lax.dot_general(left, right, (((1,), (1,)), ((), ())), preferred_element_type=F32)


def dot_nn(left, right):
    return jnp.dot(left, right, preferred_element_type=F32)


def iota(shape, dim):
    return lax.broadcasted_iota(jnp.int32, shape, dim)


def kernel_call(body, outs, scratch=(), flops=0, moved=0, name=None):
    return pl.pallas_call(
        body,
        out_shape=outs,
        scratch_shapes=list(scratch),
        name=name,
        compiler_params=pltpu.CompilerParams(vmem_limit_bytes=VMEM_LIMIT),
        cost_estimate=pl.CostEstimate(flops=flops, bytes_accessed=moved, transcendentals=0),
    )


def dispatch_kernel(capacity, tile_ref, cell_ref, frac_ref, radiance_ref, box_ref, slot_ref):
    slots, width = box_ref.shape
    devices = slots // capacity
    count = tile_ref.shape[1]
    channels = width - META
    tile = tile_ref[...]
    match = (iota((devices, count), 0) == tile).astype(F32)
    earlier = (iota((count, count), 0) < iota((count, count), 1)).astype(F32).astype(BF16)
    before = dot_nn(match.astype(BF16), earlier)
    position = jnp.sum(before * match, axis=0, keepdims=True)
    slot = tile * capacity + position.astype(jnp.int32)
    slot_ref[...] = slot
    place = (iota((slots, count), 0) == slot).astype(F32).astype(BF16)
    box_ref[:, :channels] = dot_nn(place, radiance_ref[...]).astype(BF16)
    cell = cell_ref[...]
    low, side = frac_ref[0:1, :], frac_ref[1:2, :]
    fields = (
        (cell >> 7).astype(F32),
        (cell & 127).astype(F32),
        (1.0 - low) * (1.0 - side),
        (1.0 - low) * side,
        low * (1.0 - side),
        low * side,
    )
    number = iota((META, count), 0)
    meta = jnp.zeros((META, count), F32)
    for index, field in enumerate(fields):
        meta = jnp.where(number == index, field, meta)
    box_ref[:, channels:] = dot_nt(place, meta.astype(BF16)).astype(BF16)


def fill_row(shifted, row, center, left, right):
    columns = center.shape[0]
    place = iota(center.shape, 0)
    where = pl.ds(row * columns, columns)
    shifted[1, where, :] = center.astype(BF16)
    shifted[0, where, :] = jnp.where(place == 0, left, pltpu.roll(center, 1, 0)).astype(BF16)
    shifted[2, where, :] = jnp.where(
        place == columns - 1, right, pltpu.roll(center, columns - 1, 0)
    ).astype(BF16)


def fill(shifted, field_ref, left_ref, right_ref, north_ref, south_ref):
    rows, columns, _ = field_ref.shape
    left = left_ref[...].astype(F32)
    right = right_ref[...].astype(F32)
    for row in range(rows):
        fill_row(
            shifted,
            row + 1,
            field_ref[row].astype(F32),
            left[row : row + 1],
            right[row : row + 1],
        )
    for row, edge_ref in ((0, north_ref), (rows + 1, south_ref)):
        corners = edge_ref[columns : columns + 16, :].astype(F32)
        fill_row(
            shifted, row, edge_ref[:columns, :].astype(F32), corners[0:1], corners[1:2]
        )


def convolve_rows(shifted, weight_ref, start, count, columns, mirror):
    total = None
    for row_step in range(3):
        for col_step in range(3):
            window = shifted[
                col_step, pl.ds(pl.multiple_of(start + row_step * columns, columns), count), :
            ]
            if mirror:
                term = dot_nt(window, weight_ref[2 - row_step, 2 - col_step])
            else:
                term = dot_nn(window, weight_ref[row_step, col_step])
            total = term if total is None else total + term
    return total


CHUNK = 512


def forecast_kernel(
    state_ref, slope_ref, left_ref, right_ref, north_ref, south_ref, weight_ref, out_ref, shifted
):
    rows, columns, channels = state_ref.shape
    fill(shifted, state_ref, left_ref, right_ref, north_ref, south_ref)
    per = CHUNK // columns

    def step(index, carry):
        start = index * CHUNK
        response = convolve_rows(shifted, weight_ref, start, CHUNK, columns, False)
        which = pl.ds(index * per, per)
        state = state_ref[which].reshape(CHUNK, channels).astype(F32)
        slope = slope_ref[which].reshape(CHUNK, channels).astype(F32)
        out_ref[pl.ds(pl.multiple_of(start, CHUNK), CHUNK), :] = (
            state + slope * response
        ).astype(BF16)
        return carry

    lax.fori_loop(0, rows * columns // CHUNK, step, 0)


def gradient_kernel(
    pulled_ref, spread_ref, left_ref, right_ref, north_ref, south_ref, weight_ref, out_ref, shifted
):
    rows, columns, channels = pulled_ref.shape
    fill(shifted, pulled_ref, left_ref, right_ref, north_ref, south_ref)

    def step(index, carry):
        start = index * CHUNK
        response = convolve_rows(shifted, weight_ref, start, CHUNK, columns, True)
        which = pl.ds(pl.multiple_of(start, CHUNK), CHUNK)
        out_ref[which, :] = spread_ref[which, :] + response
        return carry

    lax.fori_loop(0, rows * columns // CHUNK, step, 0)


def sigmoid(value):
    return 0.5 + 0.5 * jnp.tanh(0.5 * value)


def sample_kernel(
    columns,
    box_ref,
    grid_ref,
    weight_in_ref,
    bias_in_ref,
    weight_mid_ref,
    bias_mid_ref,
    weight_out_ref,
    bias_out_ref,
    inv_error_ref,
    departures_ref,
    scaled_ref,
    slope_first_ref,
    slope_second_ref,
    sampled,
):
    slots, width = box_ref.shape
    cells = grid_ref.shape[0]
    channels = width - META
    pick = (iota((META, FIELDS * columns), 0) == iota((META, FIELDS * columns), 1) // columns)
    wide = dot_nn(box_ref[:, channels:], pick.astype(F32).astype(BF16))
    row, column, w00, w01, w10, w11 = (
        wide[:, index * columns : (index + 1) * columns] for index in range(FIELDS)
    )
    lane = iota((slots, columns), 1).astype(F32)
    here, beside = lane == column, lane == column + 1.0
    upper = (jnp.where(here, w00, 0.0) + jnp.where(beside, w01, 0.0)).astype(BF16)
    lower = (jnp.where(here, w10, 0.0) + jnp.where(beside, w11, 0.0)).astype(BF16)
    row_low = row.astype(BF16)
    row_high = (row + 1.0).astype(BF16)
    zero = jnp.zeros((slots, columns), BF16)
    per = 8
    for block in range(cells // columns // per):
        parts = []
        for index in range(per):
            at = jnp.asarray(block * per + index, BF16)
            parts.append(jnp.where(row_low == at, upper, jnp.where(row_high == at, lower, zero)))
        first = block * per * columns
        term = dot_nn(
            jnp.concatenate(parts, axis=1), grid_ref[first : first + per * columns, :]
        )
        if block == 0:
            sampled[...] = term
        else:
            sampled[...] += term
    inv_error = inv_error_ref[...]
    step = 256
    for start in range(0, slots, step):
        rows = slice(start, start + step)
        pre_first = dot_nn(sampled[rows, :].astype(BF16), weight_in_ref[...]) + bias_in_ref[...]
        gate = sigmoid(pre_first)
        act = pre_first * gate
        slope_first_ref[rows, :] = gate + act * (1.0 - gate)
        pre_second = dot_nn(act.astype(BF16), weight_mid_ref[...]) + bias_mid_ref[...]
        gate = sigmoid(pre_second)
        act = pre_second * gate
        slope_second_ref[rows, :] = gate + act * (1.0 - gate)
        evolved = dot_nn(act.astype(BF16), weight_out_ref[...]) + bias_out_ref[...]
        departures = (evolved - box_ref[rows, :channels].astype(F32)) * inv_error
        departures_ref[rows, :] = departures.astype(BF16)
        scaled_ref[rows, :] = (departures * inv_error).astype(BF16)


def spread_kernel(
    columns,
    box_ref,
    scaled_ref,
    slope_first_ref,
    slope_second_ref,
    weight_in_ref,
    weight_mid_ref,
    weight_out_ref,
    tangent_ref,
    spread_ref,
    pulled_ref,
    west_ref,
    east_ref,
    adjoint,
):
    slots, width = box_ref.shape
    cells = spread_ref.shape[0]
    channels = width - META
    step = 256
    for start in range(0, slots, step):
        rows = slice(start, start + step)
        back = (dot_nt(scaled_ref[rows, :], weight_out_ref[...]) * slope_second_ref[rows, :]).astype(BF16)
        back = (dot_nt(back, weight_mid_ref[...]) * slope_first_ref[rows, :]).astype(BF16)
        adjoint[rows, :] = dot_nt(back, weight_in_ref[...]).astype(BF16)
    pick = (iota((16, META), 0) == iota((16, META), 1)).astype(F32).astype(BF16)
    turned = dot_nt(pick, box_ref[:, channels:])
    row, column, w00, w01, w10, w11 = (turned[index : index + 1, :] for index in range(FIELDS))
    place = iota((columns, slots), 0).astype(F32)
    here, beside = place == column, place == column + 1.0
    upper = (jnp.where(here, w00, 0.0) + jnp.where(beside, w01, 0.0)).astype(BF16)
    lower = (jnp.where(here, w10, 0.0) + jnp.where(beside, w11, 0.0)).astype(BF16)
    row_low = jnp.broadcast_to(row, (columns, slots)).astype(BF16)
    row_high = jnp.broadcast_to(row + 1.0, (columns, slots)).astype(BF16)
    zero = jnp.zeros((columns, slots), BF16)
    per = 4
    for block in range(cells // columns // per):
        parts = []
        for index in range(per):
            at = jnp.asarray(block * per + index, BF16)
            parts.append(jnp.where(row_low == at, upper, jnp.where(row_high == at, lower, zero)))
        first = block * per * columns
        which = slice(first, first + per * columns)
        spread = dot_nn(jnp.concatenate(parts, axis=0), adjoint[...])
        spread_ref[which, :] = spread
        pulled = tangent_ref[which, :].astype(F32) * spread
        pulled_ref[which, :] = pulled.astype(BF16)
        for index in range(per):
            at = block * per + index
            first = index * columns
            west_ref[at : at + 1, :] = pulled[first : first + 1, :]
            east_ref[at : at + 1, :] = pulled[first + columns - 1 : first + columns, :]


def departures_kernel(slot_ref, box_ref, out_ref):
    slots = box_ref.shape[0]
    count = slot_ref.shape[1]
    turned = jnp.broadcast_to(slot_ref[...].astype(F32), (128, count)).T
    lane = iota((count, 128), 1).astype(F32)
    parts = [(lane + float(first) == turned).astype(F32).astype(BF16) for first in range(0, slots, 128)]
    out_ref[...] = dot_nn(jnp.concatenate(parts, axis=1), box_ref[...])


def halo(west, east, top, bottom):
    lon, lat = lax.axis_size("lon"), lax.axis_size("lat")
    onward = [(i, (i + 1) % lon) for i in range(lon)]
    left = lax.ppermute(east, "lon", onward)
    right = lax.ppermute(west, "lon", [(target, source) for source, target in onward])
    down = [(i, i + 1) for i in range(lat - 1)]
    up = [(target, source) for source, target in down]
    filler = jnp.zeros((14, top.shape[1]), top.dtype)
    north = lax.ppermute(jnp.concatenate([bottom, left[-1:], right[-1:], filler]), "lat", down)
    south = lax.ppermute(jnp.concatenate([top, left[:1], right[:1], filler]), "lat", up)
    return left, right, north, south


def body(
    model_state,
    tangent_slope,
    conv_weight,
    weight_in,
    bias_in,
    weight_mid,
    bias_mid,
    weight_out,
    bias_out,
    obs_tile,
    obs_cell,
    obs_frac,
    radiance,
    inv_error,
):
    rows, columns, channels = model_state.shape
    cells = rows * columns
    devices = lax.axis_size("lat") * lax.axis_size("lon")
    count, bands = radiance.shape
    capacity = 2 * count // devices
    slots = devices * capacity
    hidden = weight_in.shape[1]
    sds = jax.ShapeDtypeStruct

    def exchange(box):
        return lax.all_to_all(
            box.reshape(devices, capacity, -1), ("lat", "lon"), split_axis=0, concat_axis=0, tiled=True
        ).reshape(slots, -1)

    box, slot = kernel_call(
        functools.partial(dispatch_kernel, capacity),
        (sds((slots, bands + META), BF16), sds((1, count), jnp.int32)),
        flops=2 * slots * count * (bands + META),
        moved=2 * slots * (bands + META),
        name="dispatch",
    )(obs_tile.reshape(1, count), obs_cell.reshape(1, count), obs_frac.T, radiance)
    arrived = exchange(box)

    conv_flops = 2 * 9 * cells * channels * channels
    shifted = pltpu.VMEM((3, (rows + 2) * columns, channels), BF16)
    beside = halo(model_state[:, 0], model_state[:, -1], model_state[0], model_state[-1])
    forecast = kernel_call(
        forecast_kernel,
        sds((cells, channels), BF16),
        (shifted,),
        flops=conv_flops,
        moved=6 * cells * channels,
        name="forecast",
    )(model_state, tangent_slope, *beside, conv_weight)

    network_flops = 2 * slots * (channels * hidden + hidden * hidden + hidden * bands)
    departures_box, scaled, slope_first, slope_second = kernel_call(
        functools.partial(sample_kernel, columns),
        (
            sds((slots, bands), BF16),
            sds((slots, bands), BF16),
            sds((slots, hidden), F32),
            sds((slots, hidden), F32),
        ),
        (pltpu.VMEM((slots, channels), F32),),
        flops=network_flops + 2 * slots * cells * channels,
        moved=2 * cells * channels + 8 * slots * hidden,
        name="sample",
    )(
        arrived,
        forecast,
        weight_in,
        bias_in.reshape(1, -1),
        weight_mid,
        bias_mid.reshape(1, -1),
        weight_out,
        bias_out.reshape(1, -1),
        inv_error.reshape(1, -1),
    )
    returned = exchange(departures_box)

    spread, pulled, west, east = kernel_call(
        functools.partial(spread_kernel, columns),
        (
            sds((cells, channels), F32),
            sds((cells, channels), BF16),
            sds((rows, channels), F32),
            sds((rows, channels), F32),
        ),
        (pltpu.VMEM((slots, channels), BF16),),
        flops=network_flops + 2 * slots * cells * channels,
        moved=8 * cells * channels + 8 * slots * hidden,
        name="spread",
    )(
        arrived,
        scaled,
        slope_first,
        slope_second,
        weight_in,
        weight_mid,
        weight_out,
        tangent_slope.reshape(cells, channels),
    )
    beside = halo(
        west.astype(BF16), east.astype(BF16), pulled[:columns], pulled[cells - columns :]
    )
    gradient = kernel_call(
        gradient_kernel,
        sds((cells, channels), F32),
        (shifted,),
        flops=conv_flops,
        moved=10 * cells * channels,
        name="gradient",
    )(pulled.reshape(rows, columns, channels), spread, *beside, conv_weight)

    departures = kernel_call(
        departures_kernel,
        sds((count, bands), F32),
        flops=2 * slots * count * bands,
        moved=4 * count * bands,
        name="departures",
    )(slot, returned)
    return departures, gradient.reshape(rows, columns, channels)


def solution(mesh):
    in_specs = (
        P("lat", "lon", None),
        P("lat", "lon", None),
        P(),
        P(),
        P(),
        P(),
        P(),
        P(),
        P(),
        P(("lat", "lon"), None),
        P(("lat", "lon")),
        P(("lat", "lon"), None),
        P(("lat", "lon"), None),
        P(),
    )
    out_specs = (P(("lat", "lon"), None), P("lat", "lon", None))
    return jax.shard_map(body, mesh=mesh, in_specs=in_specs, out_specs=out_specs, check_vma=False)
```

profile of v0, /device:TPU:1, one launch (start us, length us, event | category | flops | bytes accessed | tf_op | source)
XLA Modules:
  0.0 118.6 jit_solution(6864379041314645030)
XLA Ops:
  0.6 1.0 fusion.1
  1.7 0.0 copy-start
  1.7 2.5 %collective-permute-start = (bf16[32,256]{1,0:T(8,128)(2,1)S(1)}, bf16[32,256]{1,0:T(8,128)(2,1)S(1)}, u32[]{:S(2)}, u32[]{:S(2)}) collective-permute-start(bf16[32,256]{1,0:T(8,128)(2,1)S(1)} %bitcast.32), channel_id=1, source_target_pairs={{0,1},{1,2},{2,3},{3,4},{4,5},{5,6},{6,7},{7,8},{8,9},{9,10},{10,1... | collective-permute-start | bytes 49160 | tf_op jit(solution)/shard_map/ppermute | solution.py:290
  4.2 4.7 %collective-permute-start.1 = (bf16[32,256]{1,0:T(8,128)(2,1)S(1)}, bf16[32,256]{1,0:T(8,128)(2,1)S(1)}, u32[]{:S(2)}, u32[]{:S(2)}) collective-permute-start(bf16[32,256]{1,0:T(8,128)(2,1)S(1)} %bitcast.33), channel_id=1, source_target_pairs={{1,0},{2,1},{3,2},{4,3},{5,4},{6,5},{7,6},{8,7},{9,8},{10,9},{11,1... | collective-permute-start | bytes 49160 | tf_op jit(solution)/shard_map/ppermute | solution.py:291
  8.9 1.0 copy-done.7
  9.9 0.7 copy-done.12
  10.6 0.7 copy-done.13
  11.3 0.7 copy-done.14
  11.9 2.2 %dispatch.1 = (bf16[1024,512]{1,0:T(8,128)(2,1)}, s32[1,512]{1,0:T(1,128)S(1)}) custom-call(s32[1,512]{1,0:T(1,128)S(1)} %bitcast.28, s32[1,512]{1,0:T(1,128)S(1)} %bitcast.29, f32[2,512]{1,0:T(2,128)S(1)} %bitcast.27, bf16[512,384]{1,0:T(8,128)(2,1)S(1)} %copy-done.7), custom_call_target="tpu_custom_call" | custom-call | flops 536870912 | bytes 1048576 | tf_op jit(solution)/shard_map/dispatch/pallas_call | solution.py:330
  14.1 6.4 %all-to-all-start = ((bf16[128,8,512]{2,1,0:T(8,128)(2,1)}), bf16[128,8,512]{2,1,0:T(8,128)(2,1)S(1)}, u32[]{:S(2)}, u32[]{:S(2)}) async-start(bf16[128,8,512]{2,1,0:T(8,128)(2,1)} %bitcast.3), calls=%async_computation | async-start | bytes 2097152 | tf_op jit(solution)/shard_map/all_to_all | solution.py:326
  20.5 0.0 copy-done
  20.6 0.1 pad.15.clone
  20.7 0.0 collective-permute-done.left_ref
  20.7 0.0 collective-permute-done.1.right_ref
  20.7 0.1 maximum_maximum_fusion.1
  20.8 3.0 %collective-permute-start.3 = (bf16[144,256]{1,0:T(8,128)(2,1)S(1)}, bf16[144,256]{1,0:T(8,128)(2,1)S(1)}, u32[]{:S(2)}, u32[]{:S(2)}) collective-permute-start(bf16[144,256]{1,0:T(8,128)(2,1)S(1)} %get-tuple-element.38), channel_id=1, source_target_pairs={{16,0},{32,16},{48,32},{64,48},{80,64},{96,80},{112,96},{17,1},{33... | collective-permute-start | bytes 221192 | tf_op jit(solution)/shard_map/ppermute | solution.py:296
  23.8 2.6 %collective-permute-start.2 = (bf16[144,256]{1,0:T(8,128)(2,1)S(1)}, bf16[144,256]{1,0:T(8,128)(2,1)S(1)}, u32[]{:S(2)}, u32[]{:S(2)}) collective-permute-start(bf16[144,256]{1,0:T(8,128)(2,1)S(1)} %get-tuple-element.39), channel_id=1, source_target_pairs={{0,16},{16,32},{32,48},{48,64},{64,80},{80,96},{96,112},{1,17},{17... | collective-permute-start | bytes 221192 | tf_op jit(solution)/shard_map/ppermute | solution.py:295
  26.4 0.0 copy-done.28
  26.4 0.0 copy-done.29
  26.4 0.0 copy-start.15
  26.4 8.1 %collective-permute-done.3.south_ref = bf16[144,256]{1,0:T(8,128)(2,1)S(1)} collective-permute-done((bf16[144,256]{1,0:T(8,128)(2,1)S(1)}, bf16[144,256]{1,0:T(8,128)(2,1)S(1)}, u32[]{:S(2)}, u32[]{:S(2)}) %collective-permute-start.3) | collective-permute-done | bytes 73760 | tf_op jit(solution)/shard_map/ppermute | solution.py:296
  34.5 0.0 copy-done.26
  34.5 0.0 collective-permute-done.2.north_ref
  34.5 1.6 %copy-done.1 = bf16[32,128,256]{2,1,0:T(8,128)(2,1)S(1)} copy-done((bf16[32,128,256]{2,1,0:T(8,128)(2,1)S(1)}, bf16[32,128,256]{2,1,0:T(8,128)(2,1)}, u32[]{:S(2)}) %copy-start.1) | copy-done | bytes 2097176
  36.1 1.3 %copy-done.3 = bf16[3,3,256,256]{3,2,1,0:T(8,128)(2,1)S(1)} copy-done((bf16[3,3,256,256]{3,2,1,0:T(8,128)(2,1)S(1)}, bf16[3,3,256,256]{3,2,1,0:T(8,128)(2,1)}, u32[]{:S(2)}) %copy-start.3) | copy-done | bytes 1179672
  37.4 7.2 %forecast.1.grid_ref = bf16[4096,256]{1,0:T(8,128)(2,1)S(1)} custom-call(bf16[32,128,256]{2,1,0:T(8,128)(2,1)S(1)} %copy-done, bf16[32,128,256]{2,1,0:T(8,128)(2,1)S(1)} %copy-done.1, bf16[32,256]{1,0:T(8,128)(2,1)S(1)} %collective-permute-done.left_ref, bf16[32,256]{1,0:T(8,128)(2,1)S(1)} %collective-permute-done.1.right_ref, ...), custom_call_target="tpu_custom_call" | custom-call | flops 4831838208 | bytes 6291456 | tf_op jit(solution)/shard_map/forecast/pallas_call | solution.py:342
  44.6 0.0 copy-start.24
  44.6 1.3 %copy-done.24 = bf16[4096,256]{1,0:T(8,128)(2,1)} copy-done((bf16[4096,256]{1,0:T(8,128)(2,1)}, bf16[4096,256]{1,0:T(8,128)(2,1)S(1)}, u32[]{:S(2)}) %copy-start.24) | copy-done | bytes 2097176
  45.9 0.0 all-to-all-done
  45.9 0.0 copy-done.15
  45.9 1.0 copy-done.5
  46.9 1.0 copy-done.8
  47.9 0.9 copy-done.10
  48.9 0.7 copy-done.16
  49.6 1.6 %copy-done.25 = bf16[4096,256]{1,0:T(8,128)(2,1)S(1)} copy-done((bf16[4096,256]{1,0:T(8,128)(2,1)S(1)}, bf16[4096,256]{1,0:T(8,128)(2,1)}, u32[]{:S(2)}) %copy-start.25) | copy-done | bytes 2097176
  51.2 7.8 %sample.1 = (bf16[1024,384]{1,0:T(8,128)(2,1)}, bf16[1024,384]{1,0:T(8,128)(2,1)S(1)}, f32[1024,512]{1,0:T(8,128)S(1)}, f32[1024,512]{1,0:T(8,128)S(1)}) custom-call(bf16[1024,512]{1,0:T(8,128)(2,1)S(1)} %bitcast.23, bf16[4096,256]{1,0:T(8,128)(2,1)S(1)} %copy-done.25, bf16[256,512]{1,0:T(8,128)(2,1)S(1)} %copy-done.10, f32[1,512]{1,0:T(1,128)S(1)} %bitcast.30, ...), custom_call_target="tpu_custom_call" | custom-call | flops 3355443200 | bytes 6291456 | tf_op jit(solution)/shard_map/sample/pallas_call | solution.py:352
  59.0 1.3 %copy-done.18 = f32[1024,512]{1,0:T(8,128)} copy-done((f32[1024,512]{1,0:T(8,128)}, f32[1024,512]{1,0:T(8,128)S(1)}, u32[]{:S(2)}) %copy-start.18) | copy-done | bytes 2097176
  60.3 1.3 %copy-done.20 = f32[1024,512]{1,0:T(8,128)} copy-done((f32[1024,512]{1,0:T(8,128)}, f32[1024,512]{1,0:T(8,128)S(1)}, u32[]{:S(2)}) %copy-start.20) | copy-done | bytes 2097176
  61.6 0.9 copy-done.22
  62.5 8.7 %all-to-all-start.1 = ((bf16[128,8,384]{2,1,0:T(8,128)(2,1)}), bf16[128,8,384]{2,1,0:T(8,128)(2,1)S(1)}, u32[]{:S(2)}, u32[]{:S(2)}) async-start(bf16[128,8,384]{2,1,0:T(8,128)(2,1)} %bitcast.11), calls=%async_computation.1 | async-start | bytes 1572864 | tf_op jit(solution)/shard_map/all_to_all | solution.py:326
  71.3 0.0 copy-done.9
  71.3 0.0 copy-start.2
  71.3 1.6 %copy-done.2 = bf16[32,128,256]{2,1,0:T(8,128)(2,1)S(1)} copy-done((bf16[32,128,256]{2,1,0:T(8,128)(2,1)S(1)}, bf16[32,128,256]{2,1,0:T(8,128)(2,1)}, u32[]{:S(2)}) %copy-start.2) | copy-done | bytes 2097176
  72.9 1.0 copy-done.6
  73.9 0.9 copy-done.11
  74.9 1.6 %copy-done.19 = f32[1024,512]{1,0:T(8,128)S(1)} copy-done((f32[1024,512]{1,0:T(8,128)S(1)}, f32[1024,512]{1,0:T(8,128)}, u32[]{:S(2)}) %copy-start.19) | copy-done | bytes 2097176
  76.5 1.6 %copy-done.21 = f32[1024,512]{1,0:T(8,128)S(1)} copy-done((f32[1024,512]{1,0:T(8,128)S(1)}, f32[1024,512]{1,0:T(8,128)}, u32[]{:S(2)}) %copy-start.21) | copy-done | bytes 2097176
  78.1 1.1 copy-done.23
  79.2 6.4 %spread.1 = (f32[4096,256]{1,0:T(8,128)}, bf16[4096,256]{1,0:T(8,128)(2,1)S(1)}, f32[32,256]{1,0:T(8,128)S(1)}, f32[32,256]{1,0:T(8,128)S(1)}) custom-call(bf16[1024,512]{1,0:T(8,128)(2,1)S(1)} %bitcast.24, bf16[1024,384]{1,0:T(8,128)(2,1)S(1)} %copy-done.23, f32[1024,512]{1,0:T(8,128)S(1)} %copy-done.19, f32[1024,512]{1,0:T(8,128)S(1)} %copy-done.21, ...), custom_call_target="tpu_custom_call" | custom-call | flops 3355443200 | bytes 12582912 | tf_op jit(solution)/shard_map/spread/pallas_call | solution.py:377
  85.6 5.6 %collective-permute-start.5 = (bf16[32,256]{1,0:T(8,128)(2,1)S(1)}, bf16[32,256]{1,0:T(8,128)(2,1)S(1)}, u32[]{:S(2)}, u32[]{:S(2)}) collective-permute-start(bf16[32,256]{1,0:T(8,128)(2,1)S(1)} %convert_element_type.7), channel_id=1, source_target_pairs={{1,0},{2,1},{3,2},{4,3},{5,4},{6,5},{7,6},{8,7},{9,8},{10,9},{11,1... | collective-permute-start | bytes 49160 | tf_op jit(solution)/shard_map/ppermute | solution.py:291
  91.2 0.0 collective-permute-start.4
  91.3 0.9 collective-permute-done.5.right_ref
  92.1 5.0 %collective-permute-done.4.left_ref = bf16[32,256]{1,0:T(8,128)(2,1)S(1)} collective-permute-done((bf16[32,256]{1,0:T(8,128)(2,1)S(1)}, bf16[32,256]{1,0:T(8,128)(2,1)S(1)}, u32[]{:S(2)}, u32[]{:S(2)}) %collective-permute-start.4) | collective-permute-done | bytes 16416 | tf_op jit(solution)/shard_map/ppermute | solution.py:290
  97.2 0.0 copy-done.27
  97.2 0.1 maximum_maximum_fusion.3
  97.3 3.7 %collective-permute-start.7 = (bf16[144,256]{1,0:T(8,128)(2,1)S(1)}, bf16[144,256]{1,0:T(8,128)(2,1)S(1)}, u32[]{:S(2)}, u32[]{:S(2)}) collective-permute-start(bf16[144,256]{1,0:T(8,128)(2,1)S(1)} %get-tuple-element.36), channel_id=1, source_target_pairs={{16,0},{32,16},{48,32},{64,48},{80,64},{96,80},{112,96},{17,1},{33... | collective-permute-start | bytes 221192 | tf_op jit(solution)/shard_map/ppermute | solution.py:296
  101.0 3.0 %collective-permute-start.6 = (bf16[144,256]{1,0:T(8,128)(2,1)S(1)}, bf16[144,256]{1,0:T(8,128)(2,1)S(1)}, u32[]{:S(2)}, u32[]{:S(2)}) collective-permute-start(bf16[144,256]{1,0:T(8,128)(2,1)S(1)} %get-tuple-element.37), channel_id=1, source_target_pairs={{0,16},{16,32},{32,48},{48,64},{64,80},{80,96},{96,112},{1,17},{17... | collective-permute-start | bytes 221192 | tf_op jit(solution)/shard_map/ppermute | solution.py:295
  104.0 0.1 collective-permute-done.7.south_ref
  104.1 1.3 %collective-permute-done.6.north_ref = bf16[144,256]{1,0:T(8,128)(2,1)S(1)} collective-permute-done((bf16[144,256]{1,0:T(8,128)(2,1)S(1)}, bf16[144,256]{1,0:T(8,128)(2,1)S(1)}, u32[]{:S(2)}, u32[]{:S(2)}) %collective-permute-start.6) | collective-permute-done | bytes 73760 | tf_op jit(solution)/shard_map/ppermute | solution.py:295
  105.4 0.0 copy-done.4
  105.4 2.2 %copy-done.17 = f32[4096,256]{1,0:T(8,128)S(1)} copy-done((f32[4096,256]{1,0:T(8,128)S(1)}, f32[4096,256]{1,0:T(8,128)}, u32[]{:S(2)}) %copy-start.17) | copy-done | bytes 4194328
  107.6 9.4 %gradient.1 = f32[4096,256]{1,0:T(8,128)} custom-call(bf16[32,128,256]{2,1,0:T(8,128)(2,1)S(1)} %bitcast.25, f32[4096,256]{1,0:T(8,128)S(1)} %copy-done.17, bf16[32,256]{1,0:T(8,128)(2,1)S(1)} %collective-permute-done.4.left_ref, bf16[32,256]{1,0:T(8,128)(2,1)S(1)} %collective-permute-done.5.right_ref, ...), custom_call_target="tpu_custom_call" | custom-call | flops 4831838208 | bytes 10485760 | tf_op jit(solution)/shard_map/gradient/pallas_call | solution.py:402
  117.0 0.0 all-to-all-done.1
  117.0 1.6 %departures.1 = f32[512,384]{1,0:T(8,128)} custom-call(s32[1,512]{1,0:T(1,128)S(1)} %get-tuple-element.12.slot_ref, bf16[1024,384]{1,0:T(8,128)(2,1)S(1)} %bitcast.22), custom_call_target="tpu_custom_call" | custom-call | flops 402653184 | bytes 786432 | tf_op jit(solution)/shard_map/departures/pallas_call | solution.py:411
  (39 shorter events, 0.1 us)
Async XLA Ops:
  1.7 18.9 %copy-start = (bf16[32,128,256]{2,1,0:T(8,128)(2,1)S(1)}, bf16[32,128,256]{2,1,0:T(8,128)(2,1)}, u32[]{:S(2)}) copy-start(bf16[32,128,256]{2,1,0:T(8,128)(2,1)} %state_ref.1) | copy-start | bytes 6291460
  1.7 19.0 %collective-permute-start = (bf16[32,256]{1,0:T(8,128)(2,1)S(1)}, bf16[32,256]{1,0:T(8,128)(2,1)S(1)}, u32[]{:S(2)}, u32[]{:S(2)}) collective-permute-start(bf16[32,256]{1,0:T(8,128)(2,1)S(1)} %bitcast.32), channel_id=1, source_target_pairs={{0,1},{1,2},{2,3},{3,4},{4,5},{5,6},{6,7},{7,8},{8,9},{9,10},{10,1... | collective-permute-start | bytes 49160 | tf_op jit(solution)/shard_map/ppermute | solution.py:290
  4.2 16.5 %collective-permute-start.1 = (bf16[32,256]{1,0:T(8,128)(2,1)S(1)}, bf16[32,256]{1,0:T(8,128)(2,1)S(1)}, u32[]{:S(2)}, u32[]{:S(2)}) collective-permute-start(bf16[32,256]{1,0:T(8,128)(2,1)S(1)} %bitcast.33), channel_id=1, source_target_pairs={{1,0},{2,1},{3,2},{4,3},{5,4},{6,5},{7,6},{8,7},{9,8},{10,9},{11,1... | collective-permute-start | bytes 49160 | tf_op jit(solution)/shard_map/ppermute | solution.py:291
  8.9 1.0 copy-start.7
  9.9 0.7 copy-start.12
  10.6 0.7 copy-start.13
  11.3 0.7 copy-start.14
  11.9 14.4 %copy-start.28 = (f32[384]{0:T(512)S(1)}, f32[384]{0:T(512)}, u32[]{:S(2)}) copy-start(f32[384]{0:T(512)} %param.22) | copy-start | bytes 4612
  11.9 14.5 %copy-start.29 = (f32[384]{0:T(512)S(1)}, f32[384]{0:T(512)}, u32[]{:S(2)}) copy-start(f32[384]{0:T(512)} %param.27) | copy-start | bytes 4612
  14.1 31.8 %all-to-all-start = ((bf16[128,8,512]{2,1,0:T(8,128)(2,1)}), bf16[128,8,512]{2,1,0:T(8,128)(2,1)S(1)}, u32[]{:S(2)}, u32[]{:S(2)}) async-start(bf16[128,8,512]{2,1,0:T(8,128)(2,1)} %bitcast.3), calls=%async_computation | async-start | bytes 2097152 | tf_op jit(solution)/shard_map/all_to_all | solution.py:326
  20.7 13.9 %copy-start.26 = (bf16[144]{0:T(256)(128)(2,1)}, bf16[144]{0:T(256)(128)(2,1)S(1)}, u32[]{:S(2)}) copy-start(bf16[144]{0:T(256)(128)(2,1)S(1)} %pad.15.clone) | copy-start | bytes 868
  20.8 13.7 %collective-permute-start.3 = (bf16[144,256]{1,0:T(8,128)(2,1)S(1)}, bf16[144,256]{1,0:T(8,128)(2,1)S(1)}, u32[]{:S(2)}, u32[]{:S(2)}) collective-permute-start(bf16[144,256]{1,0:T(8,128)(2,1)S(1)} %get-tuple-element.38), channel_id=1, source_target_pairs={{16,0},{32,16},{48,32},{64,48},{80,64},{96,80},{112,96},{17,1},{33... | collective-permute-start | bytes 221192 | tf_op jit(solution)/shard_map/ppermute | solution.py:296
  23.8 10.8 %collective-permute-start.2 = (bf16[144,256]{1,0:T(8,128)(2,1)S(1)}, bf16[144,256]{1,0:T(8,128)(2,1)S(1)}, u32[]{:S(2)}, u32[]{:S(2)}) collective-permute-start(bf16[144,256]{1,0:T(8,128)(2,1)S(1)} %get-tuple-element.39), channel_id=1, source_target_pairs={{0,16},{16,32},{32,48},{48,64},{64,80},{80,96},{96,112},{1,17},{17... | collective-permute-start | bytes 221192 | tf_op jit(solution)/shard_map/ppermute | solution.py:295
  26.4 19.5 %copy-start.15 = (f32[512]{0:T(512)S(1)}, f32[512]{0:T(512)}, u32[]{:S(2)}) copy-start(f32[512]{0:T(512)} %param.18) | copy-start | bytes 6148
  34.5 1.6 %copy-start.1 = (bf16[32,128,256]{2,1,0:T(8,128)(2,1)S(1)}, bf16[32,128,256]{2,1,0:T(8,128)(2,1)}, u32[]{:S(2)}) copy-start(bf16[32,128,256]{2,1,0:T(8,128)(2,1)} %slope_ref.1) | copy-start | bytes 6291460
  36.1 1.3 %copy-start.3 = (bf16[3,3,256,256]{3,2,1,0:T(8,128)(2,1)S(1)}, bf16[3,3,256,256]{3,2,1,0:T(8,128)(2,1)}, u32[]{:S(2)}) copy-start(bf16[3,3,256,256]{3,2,1,0:T(8,128)(2,1)} %weight_ref.3) | copy-start | bytes 3538948
  44.6 1.3 %copy-start.24 = (bf16[4096,256]{1,0:T(8,128)(2,1)}, bf16[4096,256]{1,0:T(8,128)(2,1)S(1)}, u32[]{:S(2)}) copy-start(bf16[4096,256]{1,0:T(8,128)(2,1)S(1)} %forecast.1.grid_ref) | copy-start | bytes 6291460
  45.9 1.0 copy-start.5
  46.9 1.0 copy-start.8
  47.9 0.9 copy-start.10
  48.9 0.7 copy-start.16
  49.6 1.6 %copy-start.25 = (bf16[4096,256]{1,0:T(8,128)(2,1)S(1)}, bf16[4096,256]{1,0:T(8,128)(2,1)}, u32[]{:S(2)}) copy-start(bf16[4096,256]{1,0:T(8,128)(2,1)} %copy-done.24) | copy-start | bytes 6291460
  51.2 20.1 %copy-start.9 = (bf16[512,384]{1,0:T(8,128)(2,1)S(1)}, bf16[512,384]{1,0:T(8,128)(2,1)}, u32[]{:S(2)}) copy-start(bf16[512,384]{1,0:T(8,128)(2,1)} %weight_out_ref.3) | copy-start | bytes 1179652
  59.0 1.3 %copy-start.18 = (f32[1024,512]{1,0:T(8,128)}, f32[1024,512]{1,0:T(8,128)S(1)}, u32[]{:S(2)}) copy-start(f32[1024,512]{1,0:T(8,128)S(1)} %get-tuple-element.16.slope_first_ref) | copy-start | bytes 6291460
  60.3 1.3 %copy-start.20 = (f32[1024,512]{1,0:T(8,128)}, f32[1024,512]{1,0:T(8,128)S(1)}, u32[]{:S(2)}) copy-start(f32[1024,512]{1,0:T(8,128)S(1)} %get-tuple-element.17.slope_second_ref) | copy-start | bytes 6291460
  61.6 0.9 copy-start.22
  62.5 54.4 %all-to-all-start.1 = ((bf16[128,8,384]{2,1,0:T(8,128)(2,1)}), bf16[128,8,384]{2,1,0:T(8,128)(2,1)S(1)}, u32[]{:S(2)}, u32[]{:S(2)}) async-start(bf16[128,8,384]{2,1,0:T(8,128)(2,1)} %bitcast.11), calls=%async_computation.1 | async-start | bytes 1572864 | tf_op jit(solution)/shard_map/all_to_all | solution.py:326
  71.3 1.6 %copy-start.2 = (bf16[32,128,256]{2,1,0:T(8,128)(2,1)S(1)}, bf16[32,128,256]{2,1,0:T(8,128)(2,1)}, u32[]{:S(2)}) copy-start(bf16[32,128,256]{2,1,0:T(8,128)(2,1)} %slope_ref.1) | copy-start | bytes 6291460
  72.9 1.0 copy-start.6
  73.9 0.9 copy-start.11
  74.9 1.6 %copy-start.19 = (f32[1024,512]{1,0:T(8,128)S(1)}, f32[1024,512]{1,0:T(8,128)}, u32[]{:S(2)}) copy-start(f32[1024,512]{1,0:T(8,128)} %copy-done.18) | copy-start | bytes 6291460
  76.5 1.6 %copy-start.21 = (f32[1024,512]{1,0:T(8,128)S(1)}, f32[1024,512]{1,0:T(8,128)}, u32[]{:S(2)}) copy-start(f32[1024,512]{1,0:T(8,128)} %copy-done.20) | copy-start | bytes 6291460
  78.1 1.1 copy-start.23
  79.2 18.0 %copy-start.27 = (bf16[144]{0:T(256)(128)(2,1)S(1)}, bf16[144]{0:T(256)(128)(2,1)}, u32[]{:S(2)}) copy-start(bf16[144]{0:T(256)(128)(2,1)} %copy-done.26) | copy-start | bytes 868
  79.2 26.2 %copy-start.4 = (bf16[3,3,256,256]{3,2,1,0:T(8,128)(2,1)S(1)}, bf16[3,3,256,256]{3,2,1,0:T(8,128)(2,1)}, u32[]{:S(2)}) copy-start(bf16[3,3,256,256]{3,2,1,0:T(8,128)(2,1)} %weight_ref.3) | copy-start | bytes 3538948
  85.6 6.5 %collective-permute-start.5 = (bf16[32,256]{1,0:T(8,128)(2,1)S(1)}, bf16[32,256]{1,0:T(8,128)(2,1)S(1)}, u32[]{:S(2)}, u32[]{:S(2)}) collective-permute-start(bf16[32,256]{1,0:T(8,128)(2,1)S(1)} %convert_element_type.7), channel_id=1, source_target_pairs={{1,0},{2,1},{3,2},{4,3},{5,4},{6,5},{7,6},{8,7},{9,8},{10,9},{11,1... | collective-permute-start | bytes 49160 | tf_op jit(solution)/shard_map/ppermute | solution.py:291
  91.2 5.9 %collective-permute-start.4 = (bf16[32,256]{1,0:T(8,128)(2,1)S(1)}, bf16[32,256]{1,0:T(8,128)(2,1)S(1)}, u32[]{:S(2)}, u32[]{:S(2)}) collective-permute-start(bf16[32,256]{1,0:T(8,128)(2,1)S(1)} %convert_element_type.6), channel_id=1, source_target_pairs={{0,1},{1,2},{2,3},{3,4},{4,5},{5,6},{6,7},{7,8},{8,9},{9,10},{10,1... | collective-permute-start | bytes 49160 | tf_op jit(solution)/shard_map/ppermute | solution.py:290
  97.3 6.8 %collective-permute-start.7 = (bf16[144,256]{1,0:T(8,128)(2,1)S(1)}, bf16[144,256]{1,0:T(8,128)(2,1)S(1)}, u32[]{:S(2)}, u32[]{:S(2)}) collective-permute-start(bf16[144,256]{1,0:T(8,128)(2,1)S(1)} %get-tuple-element.36), channel_id=1, source_target_pairs={{16,0},{32,16},{48,32},{64,48},{80,64},{96,80},{112,96},{17,1},{33... | collective-permute-start | bytes 221192 | tf_op jit(solution)/shard_map/ppermute | solution.py:296
  101.0 4.4 %collective-permute-start.6 = (bf16[144,256]{1,0:T(8,128)(2,1)S(1)}, bf16[144,256]{1,0:T(8,128)(2,1)S(1)}, u32[]{:S(2)}, u32[]{:S(2)}) collective-permute-start(bf16[144,256]{1,0:T(8,128)(2,1)S(1)} %get-tuple-element.37), channel_id=1, source_target_pairs={{0,16},{16,32},{32,48},{48,64},{64,80},{80,96},{96,112},{1,17},{17... | collective-permute-start | bytes 221192 | tf_op jit(solution)/shard_map/ppermute | solution.py:295
  105.4 2.2 %copy-start.17 = (f32[4096,256]{1,0:T(8,128)S(1)}, f32[4096,256]{1,0:T(8,128)}, u32[]{:S(2)}) copy-start(f32[4096,256]{1,0:T(8,128)} %get-tuple-element.19.spread_ref) | copy-start | bytes 12582916
where the time goes:
time: 120 us; the launch traced here: 119 us
  starting transfers between devices  40.2 us (34%)
  Pallas kernels  34.6 us (29%)
  local copies, waits for them, and re-layouts  27.3 us (23%)
  waiting for transfers between devices  15.4 us (13%)
    unnamed x62, local copies, waits for them, and re-layouts  26.1 us
    all_to_all x2, starting transfers between devices, exchange(): lax.all_to_all(box.reshape(devices, capacity, -1), ('lat', 'lon'), split_...  15.1 us
    ppermute x2, starting transfers between devices, halo(): lax.ppermute(west, 'lon', [(target, source) for source, target in onward])  10.3 us
    pallas_call x1, Pallas kernels, body(): kernel_call(gradient_kernel, sds((cells, channels), F32), (shifted,), flo...  9.4 us
    ppermute x2, waiting for transfers between devices, halo(): lax.ppermute(jnp.concatenate([top, left[:1], right[:1], filler]), 'lat', up)  8.2 us
    pallas_call x1, Pallas kernels, body(): kernel_call(functools.partial(sample_kernel, columns), (sds((slots, bands...  7.82 us
    pallas_call x1, Pallas kernels, body(): kernel_call(forecast_kernel, sds((cells, channels), BF16), (shifted,), fl...  7.16 us
    ppermute x2, starting transfers between devices, halo(): lax.ppermute(jnp.concatenate([top, left[:1], right[:1], filler]), 'lat', up)  6.68 us
  transfers between devices with their start and end apart: 10, of which 5 were waited for; matrix products, arithmetic and copies ran while one was open for 0% of the time, Pallas kernels for 21%

commit v1 on v0

v1 whole, which is shorter than its diff:
```python
import functools

import jax
import jax.numpy as jnp
from jax import lax
from jax.experimental import pallas as pl
from jax.experimental.pallas import tpu as pltpu
from jax.sharding import PartitionSpec as P

F32 = jnp.float32
BF16 = jnp.bfloat16
META = 128
FIELDS = 6


def dot_nt(left, right):
    return lax.dot_general(left, right, (((1,), (1,)), ((), ())), preferred_element_type=F32)


def dot_nn(left, right):
    return jnp.dot(left, right, preferred_element_type=F32)


def iota(shape, dim):
    return lax.broadcasted_iota(jnp.int32, shape, dim)


def kernel_call(body, outs, out_spaces, in_spaces, scratch=(), flops=0, moved=0, limit=24, name=None):
    return pl.pallas_call(
        body,
        out_shape=outs,
        in_specs=[pl.BlockSpec(memory_space=space) for space in in_spaces],
        out_specs=[pl.BlockSpec(memory_space=space) for space in out_spaces],
        scratch_shapes=list(scratch),
        name=name,
        compiler_params=pltpu.CompilerParams(vmem_limit_bytes=limit * 1024 * 1024),
        cost_estimate=pl.CostEstimate(flops=flops, bytes_accessed=moved, transcendentals=0),
    )


HBM = pltpu.HBM
VMEM = pltpu.VMEM


def copies(semaphores, *pairs):
    started = []
    for index, (source, target) in enumerate(pairs):
        copy = pltpu.make_async_copy(source, target, semaphores.at[index])
        copy.start()
        started.append(copy)
    return started


def dispatch_kernel(
    capacity,
    tile_hbm,
    cell_hbm,
    frac_hbm,
    radiance_hbm,
    box_ref,
    slot_ref,
    tile_ref,
    cell_ref,
    frac_ref,
    radiance_ref,
    semaphores,
):
    waiting = copies(
        semaphores,
        (tile_hbm, tile_ref),
        (cell_hbm, cell_ref),
        (frac_hbm, frac_ref),
        (radiance_hbm, radiance_ref),
    )
    slots, width = box_ref.shape
    devices = slots // capacity
    count = tile_ref.shape[1]
    channels = width - META
    earlier = (iota((count, count), 0) < iota((count, count), 1)).astype(F32).astype(BF16)
    for copy in waiting[:3]:
        copy.wait()
    tile = tile_ref[...]
    match = (iota((devices, count), 0) == tile).astype(F32)
    before = dot_nn(match.astype(BF16), earlier)
    position = jnp.sum(before * match, axis=0, keepdims=True)
    slot = tile * capacity + position.astype(jnp.int32)
    slot_ref[...] = slot
    place = (iota((slots, count), 0) == slot).astype(F32).astype(BF16)
    cell = cell_ref[...]
    low, side = frac_ref[0:1, :], frac_ref[1:2, :]
    fields = (
        (cell >> 7).astype(F32),
        (cell & 127).astype(F32),
        (1.0 - low) * (1.0 - side),
        (1.0 - low) * side,
        low * (1.0 - side),
        low * side,
    )
    number = iota((META, count), 0)
    meta = jnp.zeros((META, count), F32)
    for index, field in enumerate(fields):
        meta = jnp.where(number == index, field, meta)
    box_ref[:, channels:] = dot_nt(place, meta.astype(BF16)).astype(BF16)
    waiting[3].wait()
    box_ref[:, :channels] = dot_nn(place, radiance_ref[...]).astype(BF16)


CHUNK = 512


def fill_row(shifted, row, center, left, right):
    columns = center.shape[0]
    place = iota(center.shape, 0)
    where = pl.ds(row * columns, columns)
    shifted[1, where, :] = center.astype(BF16)
    shifted[0, where, :] = jnp.where(place == 0, left, pltpu.roll(center, 1, 0)).astype(BF16)
    shifted[2, where, :] = jnp.where(
        place == columns - 1, right, pltpu.roll(center, columns - 1, 0)
    ).astype(BF16)


def fill(shifted, field_ref, left_ref, right_ref, north_ref, south_ref):
    rows, columns, _ = field_ref.shape
    left = left_ref[...].astype(F32)
    right = right_ref[...].astype(F32)
    for row in range(rows):
        fill_row(
            shifted,
            row + 1,
            field_ref[row].astype(F32),
            left[row : row + 1],
            right[row : row + 1],
        )
    for row, edge_ref, at in ((0, north_ref, 15), (rows + 1, south_ref, 0)):
        corners = edge_ref[columns:, :].astype(F32)
        fill_row(
            shifted,
            row,
            edge_ref[:columns, :].astype(F32),
            corners[at : at + 1],
            corners[16 + at : 17 + at],
        )


def convolve_rows(shifted, weight_ref, start, count, columns):
    total = None
    for row_step in range(3):
        for col_step in range(3):
            window = shifted[
                col_step, pl.ds(pl.multiple_of(start + row_step * columns, columns), count), :
            ]
            term = dot_nn(window, weight_ref[row_step, col_step])
            total = term if total is None else total + term
    return total


def forecast_kernel(
    state_hbm,
    slope_hbm,
    weight_hbm,
    left_ref,
    right_ref,
    north_ref,
    south_ref,
    out_hbm,
    mirrored_ref,
    sides_ref,
    state_ref,
    slope_ref,
    weight_ref,
    out_ref,
    shifted,
    semaphores,
    out_semaphores,
):
    waiting = copies(
        semaphores, (state_hbm, state_ref), (weight_hbm, weight_ref), (slope_hbm, slope_ref)
    )
    rows, columns, channels = state_ref.shape
    waiting[0].wait()
    fill(shifted, state_ref, left_ref, right_ref, north_ref, south_ref)
    waiting[1].wait()
    waiting[2].wait()
    per = CHUNK // columns

    def out_copy(index):
        which = pl.ds(pl.multiple_of(index * CHUNK, CHUNK), CHUNK)
        return pltpu.make_async_copy(
            out_ref.at[which, :], out_hbm.at[which, :], out_semaphores.at[index]
        )

    def step(index, carry):
        start = index * CHUNK
        response = convolve_rows(shifted, weight_ref, start, CHUNK, columns)
        which = pl.ds(index * per, per)
        state = state_ref[which].reshape(CHUNK, channels).astype(F32)
        slope = slope_ref[which].reshape(CHUNK, channels).astype(F32)
        out_ref[pl.ds(pl.multiple_of(start, CHUNK), CHUNK), :] = (
            state + slope * response
        ).astype(BF16)
        out_copy(index).start()
        return carry

    steps = rows * columns // CHUNK
    lax.fori_loop(0, steps, step, 0)
    for row_step in range(3):
        for col_step in range(3):
            mirrored_ref[row_step, col_step] = (
                weight_ref[2 - row_step, 2 - col_step].astype(F32).T.astype(BF16)
            )
    for row in range(rows):
        sides_ref[0, row : row + 1, :] = slope_ref[row, 0:16, :].astype(F32)[0:1]
        sides_ref[1, row : row + 1, :] = slope_ref[row, columns - 16 : columns, :].astype(F32)[15:16]
    for index in range(steps):
        out_copy(index).wait()


def gradient_kernel(
    pulled_ref,
    spread_ref,
    weight_hbm,
    left_ref,
    right_ref,
    north_ref,
    south_ref,
    out_hbm,
    weight_ref,
    out_ref,
    shifted,
    semaphores,
    out_semaphores,
):
    waiting = copies(semaphores, (weight_hbm, weight_ref))
    rows, columns, channels = pulled_ref.shape
    fill(shifted, pulled_ref, left_ref, right_ref, north_ref, south_ref)
    waiting[0].wait()

    def out_copy(index):
        which = pl.ds(pl.multiple_of(index * CHUNK, CHUNK), CHUNK)
        return pltpu.make_async_copy(
            out_ref.at[which, :], out_hbm.at[which, :], out_semaphores.at[index]
        )

    def step(index, carry):
        start = index * CHUNK
        response = convolve_rows(shifted, weight_ref, start, CHUNK, columns)
        which = pl.ds(pl.multiple_of(start, CHUNK), CHUNK)
        out_ref[which, :] = spread_ref[which, :] + response
        out_copy(index).start()
        return carry

    steps = rows * columns // CHUNK
    lax.fori_loop(0, steps, step, 0)
    for index in range(steps):
        out_copy(index).wait()


def sigmoid(value):
    return 0.5 + 0.5 * jnp.tanh(0.5 * value)


def blend(row_low, row_high, upper, lower, at):
    at = jnp.asarray(at, BF16)
    zero = jnp.zeros(upper.shape, BF16)
    return jnp.where(row_low == at, upper, jnp.where(row_high == at, lower, zero))


def turned_weights(fields, columns):
    slots = fields.shape[1]
    row, column, w00, w01, w10, w11 = (fields[index : index + 1, :] for index in range(FIELDS))
    place = iota((columns, slots), 0).astype(F32)
    here, beside = place == column, place == column + 1.0
    upper = (jnp.where(here, w00, 0.0) + jnp.where(beside, w01, 0.0)).astype(BF16)
    lower = (jnp.where(here, w10, 0.0) + jnp.where(beside, w11, 0.0)).astype(BF16)
    row_low = jnp.broadcast_to(row, (columns, slots)).astype(BF16)
    row_high = jnp.broadcast_to(row + 1.0, (columns, slots)).astype(BF16)
    return row_low, row_high, upper, lower


def observe_kernel(
    columns,
    box_ref,
    grid_hbm,
    weight_in_hbm,
    weight_mid_hbm,
    weight_out_hbm,
    vectors_hbm,
    slope_hbm,
    sides_hbm,
    departures_hbm,
    adjoint_hbm,
    fields_hbm,
    west_ref,
    east_ref,
    top_ref,
    bottom_ref,
    grid_ref,
    weight_in_ref,
    weight_mid_ref,
    weight_out_ref,
    vectors_ref,
    ends_ref,
    sides_ref,
    sampled,
    departures_ref,
    adjoint,
    fields_ref,
    semaphores,
    out_semaphores,
):
    slots, width = box_ref.shape
    cells, grid_channels = grid_ref.shape
    channels = width - META
    hidden = weight_in_ref.shape[1]
    rows = cells // columns
    waiting = copies(
        semaphores,
        (grid_hbm, grid_ref),
        (weight_in_hbm, weight_in_ref),
        (vectors_hbm, vectors_ref),
        (weight_mid_hbm, weight_mid_ref),
        (weight_out_hbm, weight_out_ref),
        (slope_hbm.at[pl.ds(0, columns), :], ends_ref.at[0]),
        (slope_hbm.at[pl.ds(cells - columns, columns), :], ends_ref.at[1]),
        (sides_hbm, sides_ref),
    )
    pick = (iota((16, META), 0) == iota((16, META), 1)).astype(F32).astype(BF16)
    fields_ref[...] = dot_nt(pick, box_ref[:, channels:])
    fields_out = pltpu.make_async_copy(fields_ref, fields_hbm, out_semaphores.at[0])
    fields_out.start()
    pick = iota((META, FIELDS * columns), 0) == iota((META, FIELDS * columns), 1) // columns
    wide = dot_nn(box_ref[:, channels:], pick.astype(F32).astype(BF16))
    row, column, w00, w01, w10, w11 = (
        wide[:, index * columns : (index + 1) * columns] for index in range(FIELDS)
    )
    lane = iota((slots, columns), 1).astype(F32)
    here, beside = lane == column, lane == column + 1.0
    upper = (jnp.where(here, w00, 0.0) + jnp.where(beside, w01, 0.0)).astype(BF16)
    lower = (jnp.where(here, w10, 0.0) + jnp.where(beside, w11, 0.0)).astype(BF16)
    row_low = row.astype(BF16)
    row_high = (row + 1.0).astype(BF16)
    per = 8
    waiting[0].wait()
    for block in range(rows // per):
        parts = [
            blend(row_low, row_high, upper, lower, block * per + index) for index in range(per)
        ]
        first = block * per * columns
        term = dot_nn(jnp.concatenate(parts, axis=1), grid_ref[first : first + per * columns, :])
        if block == 0:
            sampled[...] = term
        else:
            sampled[...] += term
    for copy in waiting[1:]:
        copy.wait()
    bias_in = vectors_ref[:, :hidden]
    bias_mid = vectors_ref[:, hidden : 2 * hidden]
    bias_out = vectors_ref[:, 2 * hidden : 2 * hidden + channels]
    inv_error = vectors_ref[:, 2 * hidden + channels :]
    step = 256
    for start in range(0, slots, step):
        part = slice(start, start + step)
        pre = dot_nn(sampled[part, :].astype(BF16), weight_in_ref[...]) + bias_in
        gate = sigmoid(pre)
        act = pre * gate
        slope_first = gate + act * (1.0 - gate)
        pre = dot_nn(act.astype(BF16), weight_mid_ref[...]) + bias_mid
        gate = sigmoid(pre)
        act = pre * gate
        slope_second = gate + act * (1.0 - gate)
        evolved = dot_nn(act.astype(BF16), weight_out_ref[...]) + bias_out
        departures = (evolved - box_ref[part, :channels].astype(F32)) * inv_error
        departures_ref[part, :] = departures.astype(BF16)
        back = (departures * inv_error).astype(BF16)
        back = (dot_nt(back, weight_out_ref[...]) * slope_second).astype(BF16)
        back = (dot_nt(back, weight_mid_ref[...]) * slope_first).astype(BF16)
        adjoint[part, :] = dot_nt(back, weight_in_ref[...]).astype(BF16)
    results = [
        pltpu.make_async_copy(departures_ref, departures_hbm, out_semaphores.at[1]),
        pltpu.make_async_copy(adjoint, adjoint_hbm, out_semaphores.at[2]),
    ]
    for copy in results:
        copy.start()
    fields = fields_ref[...]
    around = turned_weights(fields, columns)
    for at, index, edge_ref in ((0, 0, top_ref), (rows - 1, 1, bottom_ref)):
        spread = dot_nn(blend(*around, at), adjoint[...])
        edge_ref[...] = (ends_ref[index].astype(F32) * spread).astype(BF16)
    row, column, w00, w01, w10, w11 = (fields[index : index + 1, :] for index in range(FIELDS))
    place = iota((rows, slots), 0).astype(F32)
    here, below = place == row, place == row + 1.0
    zero = jnp.zeros((rows, slots), F32)
    for at, index, edge_ref, high, low in (
        (0.0, 0, west_ref, w00, w10),
        (columns - 2.0, 1, east_ref, w01, w11),
    ):
        chosen = column == at
        weights = jnp.where(
            here & chosen, high, jnp.where(below & chosen, low, zero)
        ).astype(BF16)
        edge_ref[...] = (sides_ref[index] * dot_nn(weights, adjoint[...])).astype(BF16)
    fields_out.wait()
    for copy in results:
        copy.wait()


def spread_kernel(
    columns,
    adjoint_hbm,
    fields_hbm,
    slope_hbm,
    spread_ref,
    pulled_ref,
    adjoint,
    fields_ref,
    slope_ref,
    semaphores,
):
    waiting = copies(
        semaphores, (fields_hbm, fields_ref), (adjoint_hbm, adjoint), (slope_hbm, slope_ref)
    )
    cells = spread_ref.shape[0]
    waiting[0].wait()
    around = turned_weights(fields_ref[...], columns)
    waiting[1].wait()
    waiting[2].wait()
    per = 4
    for block in range(cells // columns // per):
        parts = [blend(*around, block * per + index) for index in range(per)]
        first = block * per * columns
        which = slice(first, first + per * columns)
        spread = dot_nn(jnp.concatenate(parts, axis=0), adjoint[...])
        spread_ref[which, :] = spread
        pulled_ref[which, :] = (slope_ref[which, :].astype(F32) * spread).astype(BF16)


def departures_kernel(slot_ref, box_ref, out_ref):
    slots = box_ref.shape[0]
    count = slot_ref.shape[1]
    turned = jnp.broadcast_to(slot_ref[...].astype(F32), (128, count)).T
    lane = iota((count, 128), 1).astype(F32)
    parts = [(lane + float(first) == turned).astype(F32).astype(BF16) for first in range(0, slots, 128)]
    out_ref[...] = dot_nn(jnp.concatenate(parts, axis=1), box_ref[...])


def halo(west, east, top, bottom):
    lon, lat = lax.axis_size("lon"), lax.axis_size("lat")
    onward = [(i, (i + 1) % lon) for i in range(lon)]
    left = lax.ppermute(east, "lon", onward)
    right = lax.ppermute(west, "lon", [(target, source) for source, target in onward])
    down = [(i, i + 1) for i in range(lat - 1)]
    up = [(target, source) for source, target in down]
    north = lax.ppermute(jnp.concatenate([bottom, left[-16:], right[-16:]]), "lat", down)
    south = lax.ppermute(jnp.concatenate([top, left[:16], right[:16]]), "lat", up)
    return left, right, north, south


def body(
    model_state,
    tangent_slope,
    conv_weight,
    weight_in,
    bias_in,
    weight_mid,
    bias_mid,
    weight_out,
    bias_out,
    obs_tile,
    obs_cell,
    obs_frac,
    radiance,
    inv_error,
):
    rows, columns, channels = model_state.shape
    cells = rows * columns
    devices = lax.axis_size("lat") * lax.axis_size("lon")
    count, bands = radiance.shape
    capacity = 2 * count // devices
    slots = devices * capacity
    hidden = weight_in.shape[1]
    sds = jax.ShapeDtypeStruct
    dma = pltpu.SemaphoreType.DMA

    def exchange(box):
        return lax.all_to_all(
            box.reshape(devices, capacity, -1), ("lat", "lon"), split_axis=0, concat_axis=0, tiled=True
        ).reshape(slots, -1)

    box, slot = kernel_call(
        functools.partial(dispatch_kernel, capacity),
        (sds((slots, bands + META), BF16), sds((1, count), jnp.int32)),
        (VMEM, VMEM),
        (HBM,) * 4,
        (
            pltpu.VMEM((1, count), jnp.int32),
            pltpu.VMEM((1, count), jnp.int32),
            pltpu.VMEM((2, count), F32),
            pltpu.VMEM((count, bands), BF16),
            dma((4,)),
        ),
        flops=2 * slots * count * (bands + META),
        moved=2 * slots * (bands + META),
        name="dispatch",
    )(obs_tile.reshape(1, count), obs_cell.reshape(1, count), obs_frac.T, radiance)
    box, model_state = lax.optimization_barrier((box, model_state))
    arrived = exchange(box)

    conv_flops = 2 * 9 * cells * channels * channels
    conv_scratch = (
        pltpu.VMEM((3, (rows + 2) * columns, channels), BF16),
    )
    steps = cells // CHUNK
    beside = halo(model_state[:, 0], model_state[:, -1], model_state[0], model_state[-1])
    forecast, mirrored, sides = kernel_call(
        forecast_kernel,
        (
            sds((cells, channels), BF16),
            sds(conv_weight.shape, BF16),
            sds((2, rows, channels), F32),
        ),
        (HBM, VMEM, VMEM),
        (HBM,) * 3 + (VMEM,) * 4,
        (
            pltpu.VMEM((rows, columns, channels), BF16),
            pltpu.VMEM((rows, columns, channels), BF16),
            pltpu.VMEM(conv_weight.shape, BF16),
            pltpu.VMEM((cells, channels), BF16),
            *conv_scratch,
            dma((3,)),
            dma((steps,)),
        ),
        flops=conv_flops,
        moved=6 * cells * channels,
        name="forecast",
    )(model_state, tangent_slope, conv_weight, *beside)

    flat_slope = tangent_slope.reshape(cells, channels)
    vectors = jnp.concatenate([bias_in, bias_mid, bias_out, inv_error]).reshape(1, -1)
    network_flops = 2 * slots * (channels * hidden + hidden * hidden + hidden * bands)
    departures_box, adjoint, fields, west, east, top, bottom = kernel_call(
        functools.partial(observe_kernel, columns),
        (
            sds((slots, bands), BF16),
            sds((slots, channels), BF16),
            sds((16, slots), F32),
            sds((rows, channels), BF16),
            sds((rows, channels), BF16),
            sds((columns, channels), BF16),
            sds((columns, channels), BF16),
        ),
        (HBM,) * 3 + (VMEM,) * 4,
        (VMEM,) + (HBM,) * 7,
        (
            pltpu.VMEM((cells, channels), BF16),
            pltpu.VMEM(weight_in.shape, BF16),
            pltpu.VMEM(weight_mid.shape, BF16),
            pltpu.VMEM(weight_out.shape, BF16),
            pltpu.VMEM(vectors.shape, F32),
            pltpu.VMEM((2, columns, channels), BF16),
            pltpu.VMEM((2, rows, channels), F32),
            pltpu.VMEM((slots, channels), F32),
            pltpu.VMEM((slots, bands), BF16),
            pltpu.VMEM((slots, channels), BF16),
            pltpu.VMEM((16, slots), F32),
            dma((8,)),
            dma((3,)),
        ),
        flops=2 * network_flops + 2 * slots * cells * channels,
        moved=2 * cells * channels,
        limit=32,
        name="observe",
    )(arrived, forecast, weight_in, weight_mid, weight_out, vectors, flat_slope, sides)
    returned = exchange(departures_box)

    beside = halo(west, east, top, bottom)
    spread, pulled = kernel_call(
        functools.partial(spread_kernel, columns),
        (sds((cells, channels), F32), sds((cells, channels), BF16)),
        (VMEM, VMEM),
        (HBM,) * 3,
        (
            pltpu.VMEM((slots, channels), BF16),
            pltpu.VMEM((16, slots), F32),
            pltpu.VMEM((cells, channels), BF16),
            dma((3,)),
        ),
        flops=2 * slots * cells * channels,
        moved=2 * cells * channels,
        name="spread",
    )(adjoint, fields, flat_slope)
    gradient, = kernel_call(
        gradient_kernel,
        (sds((cells, channels), F32),),
        (HBM,),
        (VMEM, VMEM, HBM) + (VMEM,) * 4,
        (
            pltpu.VMEM(conv_weight.shape, BF16),
            pltpu.VMEM((cells, channels), F32),
            *conv_scratch,
            dma((1,)),
            dma((steps,)),
        ),
        flops=conv_flops,
        moved=4 * cells * channels,
        name="gradient",
    )(pulled.reshape(rows, columns, channels), spread, mirrored, *beside)

    departures, = kernel_call(
        departures_kernel,
        (sds((count, bands), F32),),
        (VMEM,),
        (VMEM, VMEM),
        flops=2 * slots * count * bands,
        moved=4 * count * bands,
        name="departures",
    )(slot, returned)
    return departures, gradient.reshape(rows, columns, channels)


def solution(mesh):
    in_specs = (
        P("lat", "lon", None),
        P("lat", "lon", None),
        P(),
        P(),
        P(),
        P(),
        P(),
        P(),
        P(),
        P(("lat", "lon"), None),
        P(("lat", "lon")),
        P(("lat", "lon"), None),
        P(("lat", "lon"), None),
        P(),
    )
    out_specs = (P(("lat", "lon"), None), P("lat", "lon", None))
    return jax.shard_map(body, mesh=mesh, in_specs=in_specs, out_specs=out_specs, check_vma=False)
```

time: 120 us -> 116 us (0.967)
  the two profiles are of different devices: /device:TPU:1 before, /device:TPU:19 now
where the time goes in v1:
time: 116 us; the launch traced here: 115 us
  starting transfers between devices  40.2 us (35%)
  Pallas kernels  35.1 us (30%)
  waiting for transfers between devices  19.9 us (17%)
  local copies, waits for them, and re-layouts  19.3 us (17%)
    all_to_all x2, starting transfers between devices, exchange(): lax.all_to_all(box.reshape(devices, capacity, -1), ('lat', 'lon'), split_...  20.8 us
    unnamed x54, local copies, waits for them, and re-layouts  18.1 us
    ppermute x2, waiting for transfers between devices, halo(): lax.ppermute(west, 'lon', [(target, source) for source, target in onward])  14.7 us
    pallas_call x1, Pallas kernels, body(): kernel_call(functools.partial(observe_kernel, columns), (sds((slots, band...  12.1 us
    ppermute x2, starting transfers between devices, halo(): lax.ppermute(jnp.concatenate([bottom, left[-16:], right[-16:]]), 'lat', d...  8.72 us
    pallas_call x1, Pallas kernels, body(): kernel_call(forecast_kernel, (sds((cells, channels), BF16), sds(conv_weig...  8.55 us
    pallas_call x1, Pallas kernels, body(): kernel_call(gradient_kernel, (sds((cells, channels), F32),), (HBM,), (VME...  8.26 us
    ppermute x2, starting transfers between devices, halo(): lax.ppermute(west, 'lon', [(target, source) for source, target in onward])  6.62 us
  transfers between devices with their start and end apart: 10, of which 4 were waited for; matrix products, arithmetic and copies ran while one was open for 1% of the time, Pallas kernels for 17%

profile of v1, /device:TPU:19, one launch (start us, length us, event | category | flops | bytes accessed | tf_op | source)
XLA Modules:
  0.0 115.5 jit_solution(11583862662252569433)
XLA Ops:
  0.6 0.0 copy-start
  0.6 0.0 copy-start.7
  0.7 1.1 copy-done.7
  1.8 0.7 copy-done.10
  2.5 0.7 copy-done.11
  3.2 0.7 copy-done.12
  3.8 1.6 %dispatch.1 = (bf16[1024,512]{1,0:T(8,128)(2,1)S(1)}, s32[1,512]{1,0:T(1,128)S(1)}) custom-call(s32[1,512]{1,0:T(1,128)S(1)} %bitcast.24, s32[1,512]{1,0:T(1,128)S(1)} %bitcast.25, f32[2,512]{1,0:T(2,128)S(1)} %bitcast.23, bf16[512,384]{1,0:T(8,128)(2,1)S(1)} %copy-done.7), custom_call_target="tpu_custom_call" | custom-call | flops 536870912 | bytes 1048576 | tf_op jit(solution)/shard_map/dispatch/pallas_call | solution.py:489
  5.5 0.0 copy-start.1
  5.5 1.0 copy-done.1
  6.5 10.6 %all-to-all-start = ((bf16[128,8,512]{2,1,0:T(8,128)(2,1)}), bf16[128,8,512]{2,1,0:T(8,128)(2,1)S(1)}, u32[]{:S(2)}, u32[]{:S(2)}) async-start(bf16[128,8,512]{2,1,0:T(8,128)(2,1)} %bitcast.20), calls=%async_computation | async-start | bytes 2097152 | tf_op jit(solution)/shard_map/all_to_all | solution.py:485
  17.1 0.0 copy-done
  17.1 0.0 copy-start.23
  17.1 0.0 copy-start.24
  17.1 0.0 copy-start.25
  17.1 0.0 copy-start.26
  17.2 0.0 copy-start.2
  17.2 0.0 copy-start.5
  17.2 1.2 %copy.16 = bf16[32,128,256]{2,0,1:T(8,128)(2,1)S(1)} copy(bf16[32,128,256]{2,1,0:T(8,128)(2,1)S(1)} %copy-done) | data formatting | bytes 4194304 | tf_op jit(solution)/shard_map/optimization_barrier | solution.py:505
  18.4 3.2 %collective-permute-start.1 = (bf16[32,256]{1,0:T(8,128)(2,1)S(1)}, bf16[32,256]{1,0:T(8,128)(2,1)S(1)}, u32[]{:S(2)}, u32[]{:S(2)}) collective-permute-start(bf16[32,256]{1,0:T(8,128)(2,1)S(1)} %get-tuple-element.36), channel_id=1, source_target_pairs={{1,0},{2,1},{3,2},{4,3},{5,4},{6,5},{7,6},{8,7},{9,8},{10,9},{11,1... | collective-permute-start | bytes 49160 | tf_op jit(solution)/shard_map/ppermute | solution.py:450
  21.6 0.0 collective-permute-start
  21.6 8.1 %collective-permute-done.1.right_ref = bf16[32,256]{1,0:T(8,128)(2,1)S(1)} collective-permute-done((bf16[32,256]{1,0:T(8,128)(2,1)S(1)}, bf16[32,256]{1,0:T(8,128)(2,1)S(1)}, u32[]{:S(2)}, u32[]{:S(2)}) %collective-permute-start.1) | collective-permute-done | bytes 16416 | tf_op jit(solution)/shard_map/ppermute | solution.py:450
  29.7 1.6 %collective-permute-done.left_ref = bf16[32,256]{1,0:T(8,128)(2,1)S(1)} collective-permute-done((bf16[32,256]{1,0:T(8,128)(2,1)S(1)}, bf16[32,256]{1,0:T(8,128)(2,1)S(1)}, u32[]{:S(2)}, u32[]{:S(2)}) %collective-permute-start) | collective-permute-done | bytes 16416 | tf_op jit(solution)/shard_map/ppermute | solution.py:449
  31.3 4.5 %collective-permute-start.2 = (bf16[160,256]{1,0:T(8,128)(2,1)S(1)}, bf16[160,256]{1,0:T(8,128)(2,1)S(1)}, u32[]{:S(2)}, u32[]{:S(2)}) collective-permute-start(bf16[160,256]{1,0:T(8,128)(2,1)S(1)} %pad_maximum_fusion), channel_id=1, source_target_pairs={{0,16},{16,32},{32,48},{48,64},{64,80},{80,96},{96,112},{1,17},{17... | collective-permute-start | bytes 245768 | tf_op jit(solution)/shard_map/ppermute | solution.py:453
  35.9 2.1 %collective-permute-start.3 = (bf16[160,256]{1,0:T(8,128)(2,1)S(1)}, bf16[160,256]{1,0:T(8,128)(2,1)S(1)}, u32[]{:S(2)}, u32[]{:S(2)}) collective-permute-start(bf16[160,256]{1,0:T(8,128)(2,1)S(1)} %pad_maximum_fusion.1), channel_id=1, source_target_pairs={{16,0},{32,16},{48,32},{64,48},{80,64},{96,80},{112,96},{17,1},{33... | collective-permute-start | bytes 245768 | tf_op jit(solution)/shard_map/ppermute | solution.py:454
  38.0 0.0 copy-done.23
  38.0 0.0 copy-done.24
  38.0 0.0 copy-done.25
  38.0 0.0 copy-done.26
  38.1 0.0 copy-start.8
  38.1 0.0 collective-permute-done.2.north_ref
  38.1 3.6 %collective-permute-done.3.south_ref = bf16[160,256]{1,0:T(8,128)(2,1)S(1)} collective-permute-done((bf16[160,256]{1,0:T(8,128)(2,1)S(1)}, bf16[160,256]{1,0:T(8,128)(2,1)S(1)}, u32[]{:S(2)}, u32[]{:S(2)}) %collective-permute-start.3) | collective-permute-done | bytes 81952 | tf_op jit(solution)/shard_map/ppermute | solution.py:454
  41.6 0.0 copy-done.2
  41.6 0.0 copy-done.5
  41.6 8.5 %forecast.1 = (bf16[4096,256]{1,0:T(8,128)(2,1)S(1)}, bf16[3,3,256,256]{3,2,1,0:T(8,128)(2,1)S(1)}, f32[2,32,256]{2,1,0:T(8,128)S(1)}) custom-call(bf16[32,128,256]{2,1,0:T(8,128)(2,1)S(1)} %copy-done, bf16[32,128,256]{2,1,0:T(8,128)(2,1)S(1)} %copy-done.2, bf16[3,3,256,256]{3,2,1,0:T(8,128)(2,1)S(1)} %copy-done.5, ...), custom_call_target="tpu_custom_call" | custom-call | flops 4831838208 | bytes 6291456 | tf_op jit(solution)/shard_map/forecast/pallas_call | solution.py:514
  50.2 1.0 copy-done.13
  51.2 1.3 %copy-done.15 = bf16[4096,256]{1,0:T(8,128)(2,1)} copy-done((bf16[4096,256]{1,0:T(8,128)(2,1)}, bf16[4096,256]{1,0:T(8,128)(2,1)S(1)}, u32[]{:S(2)}) %copy-start.15) | copy-done | bytes 2097176
  52.6 0.6 copy-done.21
  53.2 0.0 all-to-all-done
  53.2 1.6 %copy-done.3 = bf16[32,128,256]{2,1,0:T(8,128)(2,1)S(1)} copy-done((bf16[32,128,256]{2,1,0:T(8,128)(2,1)S(1)}, bf16[32,128,256]{2,1,0:T(8,128)(2,1)}, u32[]{:S(2)}) %copy-start.3) | copy-done | bytes 2097176
  54.8 1.0 copy-done.6
  55.8 0.9 copy-done.9
  56.8 1.6 %copy-done.16 = bf16[4096,256]{1,0:T(8,128)(2,1)S(1)} copy-done((bf16[4096,256]{1,0:T(8,128)(2,1)S(1)}, bf16[4096,256]{1,0:T(8,128)(2,1)}, u32[]{:S(2)}) %copy-start.16) | copy-done | bytes 2097176
  58.4 0.8 copy-done.22
  59.2 12.1 %observe.1 = (bf16[1024,384]{1,0:T(8,128)(2,1)}, bf16[1024,256]{1,0:T(8,128)(2,1)S(1)}, f32[16,1024]{1,0:T(8,128)S(1)}, bf16[32,256]{1,0:T(8,128)(2,1)S(1)}, bf1...) custom-call(bf16[1024,512]{1,0:T(8,128)(2,1)S(1)} %bitcast.19, ...), custom_call_target="tpu_custom_call" | custom-call | flops 4563402752 | bytes 2097152 | tf_op jit(solution)/shard_map/observe/pallas_call | solution.py:540
  71.3 0.0 copy-start.17
  71.3 0.8 copy-done.17
  72.1 0.6 copy-done.19
  72.7 0.0 collective-permute-start.4
  72.7 10.2 %all-to-all-start.1 = ((bf16[128,8,384]{2,1,0:T(8,128)(2,1)}), bf16[128,8,384]{2,1,0:T(8,128)(2,1)S(1)}, u32[]{:S(2)}, u32[]{:S(2)}) async-start(bf16[128,8,384]{2,1,0:T(8,128)(2,1)} %bitcast.10), calls=%async_computation.1 | async-start | bytes 1572864 | tf_op jit(solution)/shard_map/all_to_all | solution.py:485
  82.9 3.4 %collective-permute-start.5 = (bf16[32,256]{1,0:T(8,128)(2,1)S(1)}, bf16[32,256]{1,0:T(8,128)(2,1)S(1)}, u32[]{:S(2)}, u32[]{:S(2)}) collective-permute-start(bf16[32,256]{1,0:T(8,128)(2,1)S(1)} %get-tuple-element.31), channel_id=1, source_target_pairs={{1,0},{2,1},{3,2},{4,3},{5,4},{6,5},{7,6},{8,7},{9,8},{10,9},{11,1... | collective-permute-start | bytes 49160 | tf_op jit(solution)/shard_map/ppermute | solution.py:450
  86.3 0.0 collective-permute-done.4.left_ref
  86.3 6.6 %collective-permute-done.5.right_ref = bf16[32,256]{1,0:T(8,128)(2,1)S(1)} collective-permute-done((bf16[32,256]{1,0:T(8,128)(2,1)S(1)}, bf16[32,256]{1,0:T(8,128)(2,1)S(1)}, u32[]{:S(2)}, u32[]{:S(2)}) %collective-permute-start.5) | collective-permute-done | bytes 16416 | tf_op jit(solution)/shard_map/ppermute | solution.py:450
  92.9 4.2 %collective-permute-start.6 = (bf16[160,256]{1,0:T(8,128)(2,1)S(1)}, bf16[160,256]{1,0:T(8,128)(2,1)S(1)}, u32[]{:S(2)}, u32[]{:S(2)}) collective-permute-start(bf16[160,256]{1,0:T(8,128)(2,1)S(1)} %pad_maximum_fusion.2), channel_id=1, source_target_pairs={{0,16},{16,32},{32,48},{48,64},{64,80},{80,96},{96,112},{1,17},{17... | collective-permute-start | bytes 245768 | tf_op jit(solution)/shard_map/ppermute | solution.py:453
  97.1 1.9 %collective-permute-start.7 = (bf16[160,256]{1,0:T(8,128)(2,1)S(1)}, bf16[160,256]{1,0:T(8,128)(2,1)S(1)}, u32[]{:S(2)}, u32[]{:S(2)}) collective-permute-start(bf16[160,256]{1,0:T(8,128)(2,1)S(1)} %pad_maximum_fusion.3), channel_id=1, source_target_pairs={{16,0},{32,16},{48,32},{64,48},{80,64},{96,80},{112,96},{17,1},{33... | collective-permute-start | bytes 245768 | tf_op jit(solution)/shard_map/ppermute | solution.py:454
  99.1 0.0 copy-start.4
  99.1 1.6 %copy-done.4 = bf16[32,128,256]{2,1,0:T(8,128)(2,1)S(1)} copy-done((bf16[32,128,256]{2,1,0:T(8,128)(2,1)S(1)}, bf16[32,128,256]{2,1,0:T(8,128)(2,1)}, u32[]{:S(2)}) %copy-start.4) | copy-done | bytes 2097176
  100.7 1.0 copy-done.18
  101.7 0.8 copy-done.20
  102.5 3.0 %spread.1 = (f32[4096,256]{1,0:T(8,128)S(1)}, bf16[4096,256]{1,0:T(8,128)(2,1)S(1)}) custom-call(bf16[1024,256]{1,0:T(8,128)(2,1)S(1)} %copy-done.18, f32[16,1024]{1,0:T(8,128)S(1)} %copy-done.20, bf16[4096,256]{1,0:T(8,128)(2,1)S(1)} %bitcast.22), custom_call_target="tpu_custom_call" | custom-call | flops 2147483648 | bytes 2097152 | tf_op jit(solution)/shard_map/spread/pallas_call | solution.py:576
  105.5 0.0 collective-permute-done.6.north_ref
  105.5 0.0 collective-permute-done.7.south_ref
  105.6 8.3 %gradient.1 = f32[4096,256]{1,0:T(8,128)} custom-call(bf16[32,128,256]{2,1,0:T(8,128)(2,1)S(1)} %bitcast.26, f32[4096,256]{1,0:T(8,128)S(1)} %get-tuple-element.28.spread_ref, bf16[3,3,256,256]{3,2,1,0:T(8,128)(2,1)S(1)} %copy-done.14, bf16[32,256]{1,0:T(8,128)(2,1)S(1)} %collective-permute-done.4.left_ref, ...), custom_call_target="tpu_custom_call" | custom-call | flops 4831838208 | bytes 4194304 | tf_op jit(solution)/shard_map/gradient/pallas_call | solution.py:591
  113.8 0.0 all-to-all-done.1
  113.8 1.6 %departures.1 = f32[512,384]{1,0:T(8,128)} custom-call(s32[1,512]{1,0:T(1,128)S(1)} %get-tuple-element.18.slot_ref, bf16[1024,384]{1,0:T(8,128)(2,1)S(1)} %bitcast.18), custom_call_target="tpu_custom_call" | custom-call | flops 402653184 | bytes 786432 | tf_op jit(solution)/shard_map/departures/pallas_call | solution.py:608
  (29 shorter events, 0.1 us)
Async XLA Ops:
  0.6 16.5 %copy-start = (bf16[32,128,256]{2,1,0:T(8,128)(2,1)S(1)}, bf16[32,128,256]{2,1,0:T(8,128)(2,1)}, u32[]{:S(2)}) copy-start(bf16[32,128,256]{2,1,0:T(8,128)(2,1)} %state_hbm) | copy-start | bytes 6291460
  0.6 1.1 copy-start.7
  1.8 0.7 copy-start.10
  2.5 0.7 copy-start.11
  3.2 0.7 copy-start.12
  5.5 1.0 copy-start.1
  6.5 46.7 %all-to-all-start = ((bf16[128,8,512]{2,1,0:T(8,128)(2,1)}), bf16[128,8,512]{2,1,0:T(8,128)(2,1)S(1)}, u32[]{:S(2)}, u32[]{:S(2)}) async-start(bf16[128,8,512]{2,1,0:T(8,128)(2,1)} %bitcast.20), calls=%async_computation | async-start | bytes 2097152 | tf_op jit(solution)/shard_map/all_to_all | solution.py:485
  17.1 20.9 %copy-start.23 = (f32[384]{0:T(512)S(1)}, f32[384]{0:T(512)}, u32[]{:S(2)}) copy-start(f32[384]{0:T(512)} %param.27) | copy-start | bytes 4612
  17.1 20.9 %copy-start.24 = (f32[384]{0:T(512)S(1)}, f32[384]{0:T(512)}, u32[]{:S(2)}) copy-start(f32[384]{0:T(512)} %param.22) | copy-start | bytes 4612
  17.1 20.9 %copy-start.25 = (f32[512]{0:T(512)S(1)}, f32[512]{0:T(512)}, u32[]{:S(2)}) copy-start(f32[512]{0:T(512)} %param.20) | copy-start | bytes 6148
  17.1 20.9 %copy-start.26 = (f32[512]{0:T(512)S(1)}, f32[512]{0:T(512)}, u32[]{:S(2)}) copy-start(f32[512]{0:T(512)} %param.18) | copy-start | bytes 6148
  17.2 24.5 %copy-start.2 = (bf16[32,128,256]{2,1,0:T(8,128)(2,1)S(1)}, bf16[32,128,256]{2,1,0:T(8,128)(2,1)}, u32[]{:S(2)}) copy-start(bf16[32,128,256]{2,1,0:T(8,128)(2,1)} %slope_hbm.1) | copy-start | bytes 6291460
  17.2 24.5 %copy-start.5 = (bf16[3,3,256,256]{3,2,1,0:T(8,128)(2,1)S(1)}, bf16[3,3,256,256]{3,2,1,0:T(8,128)(2,1)}, u32[]{:S(2)}) copy-start(bf16[3,3,256,256]{3,2,1,0:T(8,128)(2,1)} %weight_hbm.1) | copy-start | bytes 3538948
  18.4 11.3 %collective-permute-start.1 = (bf16[32,256]{1,0:T(8,128)(2,1)S(1)}, bf16[32,256]{1,0:T(8,128)(2,1)S(1)}, u32[]{:S(2)}, u32[]{:S(2)}) collective-permute-start(bf16[32,256]{1,0:T(8,128)(2,1)S(1)} %get-tuple-element.36), channel_id=1, source_target_pairs={{1,0},{2,1},{3,2},{4,3},{5,4},{6,5},{7,6},{8,7},{9,8},{10,9},{11,1... | collective-permute-start | bytes 49160 | tf_op jit(solution)/shard_map/ppermute | solution.py:450
  21.6 9.7 %collective-permute-start = (bf16[32,256]{1,0:T(8,128)(2,1)S(1)}, bf16[32,256]{1,0:T(8,128)(2,1)S(1)}, u32[]{:S(2)}, u32[]{:S(2)}) collective-permute-start(bf16[32,256]{1,0:T(8,128)(2,1)S(1)} %get-tuple-element.37), channel_id=1, source_target_pairs={{0,1},{1,2},{2,3},{3,4},{4,5},{5,6},{6,7},{7,8},{8,9},{9,10},{10,1... | collective-permute-start | bytes 49160 | tf_op jit(solution)/shard_map/ppermute | solution.py:449
  31.3 6.8 %collective-permute-start.2 = (bf16[160,256]{1,0:T(8,128)(2,1)S(1)}, bf16[160,256]{1,0:T(8,128)(2,1)S(1)}, u32[]{:S(2)}, u32[]{:S(2)}) collective-permute-start(bf16[160,256]{1,0:T(8,128)(2,1)S(1)} %pad_maximum_fusion), channel_id=1, source_target_pairs={{0,16},{16,32},{32,48},{48,64},{64,80},{80,96},{96,112},{1,17},{17... | collective-permute-start | bytes 245768 | tf_op jit(solution)/shard_map/ppermute | solution.py:453
  35.9 5.8 %collective-permute-start.3 = (bf16[160,256]{1,0:T(8,128)(2,1)S(1)}, bf16[160,256]{1,0:T(8,128)(2,1)S(1)}, u32[]{:S(2)}, u32[]{:S(2)}) collective-permute-start(bf16[160,256]{1,0:T(8,128)(2,1)S(1)} %pad_maximum_fusion.1), channel_id=1, source_target_pairs={{16,0},{32,16},{48,32},{64,48},{80,64},{96,80},{112,96},{17,1},{33... | collective-permute-start | bytes 245768 | tf_op jit(solution)/shard_map/ppermute | solution.py:454
  38.1 15.1 %copy-start.8 = (bf16[512,384]{1,0:T(8,128)(2,1)S(1)}, bf16[512,384]{1,0:T(8,128)(2,1)}, u32[]{:S(2)}) copy-start(bf16[512,384]{1,0:T(8,128)(2,1)} %weight_out_hbm.1) | copy-start | bytes 1179652
  50.2 1.0 copy-start.13
  51.2 1.3 %copy-start.15 = (bf16[4096,256]{1,0:T(8,128)(2,1)}, bf16[4096,256]{1,0:T(8,128)(2,1)S(1)}, u32[]{:S(2)}) copy-start(bf16[4096,256]{1,0:T(8,128)(2,1)S(1)} %get-tuple-element.22.grid_hbm) | copy-start | bytes 6291460
  52.6 0.6 copy-start.21
  53.2 1.6 %copy-start.3 = (bf16[32,128,256]{2,1,0:T(8,128)(2,1)S(1)}, bf16[32,128,256]{2,1,0:T(8,128)(2,1)}, u32[]{:S(2)}) copy-start(bf16[32,128,256]{2,1,0:T(8,128)(2,1)} %slope_hbm.1) | copy-start | bytes 6291460
  54.8 1.0 copy-start.6
  55.8 0.9 copy-start.9
  56.8 1.6 %copy-start.16 = (bf16[4096,256]{1,0:T(8,128)(2,1)S(1)}, bf16[4096,256]{1,0:T(8,128)(2,1)}, u32[]{:S(2)}) copy-start(bf16[4096,256]{1,0:T(8,128)(2,1)} %copy-done.15) | copy-start | bytes 6291460
  58.4 0.8 copy-start.22
  71.3 0.8 copy-start.17
  72.1 0.6 copy-start.19
  72.7 13.6 %collective-permute-start.4 = (bf16[32,256]{1,0:T(8,128)(2,1)S(1)}, bf16[32,256]{1,0:T(8,128)(2,1)S(1)}, u32[]{:S(2)}, u32[]{:S(2)}) collective-permute-start(bf16[32,256]{1,0:T(8,128)(2,1)S(1)} %get-tuple-element.30), channel_id=1, source_target_pairs={{0,1},{1,2},{2,3},{3,4},{4,5},{5,6},{6,7},{7,8},{8,9},{9,10},{10,1... | collective-permute-start | bytes 49160 | tf_op jit(solution)/shard_map/ppermute | solution.py:449
  72.7 41.1 %all-to-all-start.1 = ((bf16[128,8,384]{2,1,0:T(8,128)(2,1)}), bf16[128,8,384]{2,1,0:T(8,128)(2,1)S(1)}, u32[]{:S(2)}, u32[]{:S(2)}) async-start(bf16[128,8,384]{2,1,0:T(8,128)(2,1)} %bitcast.10), calls=%async_computation.1 | async-start | bytes 1572864 | tf_op jit(solution)/shard_map/all_to_all | solution.py:485
  82.9 10.0 %collective-permute-start.5 = (bf16[32,256]{1,0:T(8,128)(2,1)S(1)}, bf16[32,256]{1,0:T(8,128)(2,1)S(1)}, u32[]{:S(2)}, u32[]{:S(2)}) collective-permute-start(bf16[32,256]{1,0:T(8,128)(2,1)S(1)} %get-tuple-element.31), channel_id=1, source_target_pairs={{1,0},{2,1},{3,2},{4,3},{5,4},{6,5},{7,6},{8,7},{9,8},{10,9},{11,1... | collective-permute-start | bytes 49160 | tf_op jit(solution)/shard_map/ppermute | solution.py:450
  92.9 12.6 %collective-permute-start.6 = (bf16[160,256]{1,0:T(8,128)(2,1)S(1)}, bf16[160,256]{1,0:T(8,128)(2,1)S(1)}, u32[]{:S(2)}, u32[]{:S(2)}) collective-permute-start(bf16[160,256]{1,0:T(8,128)(2,1)S(1)} %pad_maximum_fusion.2), channel_id=1, source_target_pairs={{0,16},{16,32},{32,48},{48,64},{64,80},{80,96},{96,112},{1,17},{17... | collective-permute-start | bytes 245768 | tf_op jit(solution)/shard_map/ppermute | solution.py:453
  97.1 8.4 %collective-permute-start.7 = (bf16[160,256]{1,0:T(8,128)(2,1)S(1)}, bf16[160,256]{1,0:T(8,128)(2,1)S(1)}, u32[]{:S(2)}, u32[]{:S(2)}) collective-permute-start(bf16[160,256]{1,0:T(8,128)(2,1)S(1)} %pad_maximum_fusion.3), channel_id=1, source_target_pairs={{16,0},{32,16},{48,32},{64,48},{80,64},{96,80},{112,96},{17,1},{33... | collective-permute-start | bytes 245768 | tf_op jit(solution)/shard_map/ppermute | solution.py:454
  99.1 1.6 %copy-start.4 = (bf16[32,128,256]{2,1,0:T(8,128)(2,1)S(1)}, bf16[32,128,256]{2,1,0:T(8,128)(2,1)}, u32[]{:S(2)}) copy-start(bf16[32,128,256]{2,1,0:T(8,128)(2,1)} %slope_hbm.1) | copy-start | bytes 6291460
  100.7 1.0 copy-start.18
  101.7 0.8 copy-start.20
  102.5 3.0 %copy-start.14 = (bf16[3,3,256,256]{3,2,1,0:T(8,128)(2,1)S(1)}, bf16[3,3,256,256]{3,2,1,0:T(8,128)(2,1)}, u32[]{:S(2)}) copy-start(bf16[3,3,256,256]{3,2,1,0:T(8,128)(2,1)} %copy-done.13) | copy-start | bytes 3538948

commit v2 on v1

v2 whole, which is shorter than its diff:
```python
import functools

import jax
import jax.numpy as jnp
from jax import lax
from jax.experimental import pallas as pl
from jax.experimental.pallas import tpu as pltpu
from jax.sharding import PartitionSpec as P

F32 = jnp.float32
BF16 = jnp.bfloat16
META = 128
FIELDS = 6
VMEM_KIB = 60 * 1024 + 512


def dot_nt(left, right):
    return lax.dot_general(left, right, (((1,), (1,)), ((), ())), preferred_element_type=F32)


def dot_nn(left, right):
    return jnp.dot(left, right, preferred_element_type=F32)


def iota(shape, dim):
    return lax.broadcasted_iota(jnp.int32, shape, dim)


def kernel_call(body, outs, out_spaces, in_spaces, scratch=(), flops=0, moved=0, room=0, aliases=None, name=None):
    return pl.pallas_call(
        body,
        out_shape=outs,
        in_specs=[pl.BlockSpec(memory_space=space) for space in in_spaces],
        out_specs=[pl.BlockSpec(memory_space=space) for space in out_spaces],
        scratch_shapes=list(scratch),
        input_output_aliases=aliases or {},
        name=name,
        compiler_params=pltpu.CompilerParams(vmem_limit_bytes=(VMEM_KIB - room) * 1024),
        cost_estimate=pl.CostEstimate(flops=flops, bytes_accessed=moved, transcendentals=0),
    )


HBM = pltpu.HBM
VMEM = pltpu.VMEM


def copies(semaphores, *pairs):
    started = []
    for index, (source, target) in enumerate(pairs):
        copy = pltpu.make_async_copy(source, target, semaphores.at[index])
        copy.start()
        started.append(copy)
    return started


CORNER_LANE = 32
CORNER_WIDTH = 32


def corner_slots(lat, lon, capacity, shape, dim):
    lats, lons = lax.axis_size("lat"), lax.axis_size("lon")
    number = iota(shape, dim)
    result = jnp.full(shape, -1, jnp.int32)
    for index, (down, right) in enumerate(((-1, -1), (-1, 1), (1, -1), (1, 1))):
        row, column = lat + down, lax.rem(lon + right + lons, lons)
        inside = (row >= 0) & (row < lats)
        first = jnp.where(inside, (row * lons + column) * capacity, -4096)
        mine = (number >= index * 8) & (number < index * 8 + 8)
        result = jnp.where(mine, first + number - index * 8, result)
    return result


def corner_fold(shape, lane_dim):
    value, lane = iota(shape, 1 - lane_dim), iota(shape, lane_dim)
    chosen = (value % CORNER_WIDTH == lane - CORNER_LANE) & (lane >= CORNER_LANE)
    return (chosen & (lane < CORNER_LANE + CORNER_WIDTH)).astype(F32).astype(BF16)


def corner_mask(shape):
    return iota(shape, 1) // CORNER_WIDTH == iota(shape, 0) % 8


def corners_out(cells, lat, lon, capacity, first, count):
    channels = cells[0].shape[1]
    spread = jnp.concatenate([jnp.broadcast_to(cell, (8, channels)) for cell in cells], axis=0)
    kept = jnp.where(corner_mask(spread.shape), spread, 0.0).astype(BF16)
    folded = dot_nn(kept, corner_fold((channels, META), 1)).astype(BF16)
    target = corner_slots(lat, lon, capacity, (count, 32), 1)
    place = (iota((count, 32), 0) + first == target).astype(F32).astype(BF16)
    return dot_nn(place, folded)


def corners_in(lanes, lat, lon, capacity, channels):
    slots = lanes.shape[0]
    source = corner_slots(lat, lon, capacity, (32, slots), 0)
    place = (iota((32, slots), 1) == source).astype(F32).astype(BF16)
    folded = dot_nn(place, lanes).astype(BF16)
    spread = dot_nn(folded, corner_fold((META, channels), 0))
    kept = jnp.where(corner_mask(spread.shape), spread, 0.0)
    return [jnp.sum(kept[8 * index : 8 * index + 8], axis=0, keepdims=True) for index in range(4)]


def dispatch_kernel(
    capacity,
    tile_hbm,
    cell_hbm,
    frac_hbm,
    radiance_hbm,
    state_hbm,
    box_hbm,
    slot_hbm,
    west_hbm,
    east_hbm,
    top_hbm,
    bottom_hbm,
    tile_ref,
    cell_ref,
    frac_ref,
    radiance_ref,
    first_ref,
    last_ref,
    box_ref,
    slot_ref,
    west_ref,
    east_ref,
    semaphores,
    out_semaphores,
):
    rows, columns, _ = state_hbm.shape
    lat, lon = lax.axis_index("lat"), lax.axis_index("lon")
    waiting = copies(
        semaphores,
        (tile_hbm, tile_ref),
        (cell_hbm, cell_ref),
        (frac_hbm, frac_ref),
        (radiance_hbm, radiance_ref),
        (state_hbm.at[:, pl.ds(0, 16), :], first_ref),
        (state_hbm.at[:, pl.ds(columns - 16, 16), :], last_ref),
        (state_hbm.at[0], top_hbm),
        (state_hbm.at[rows - 1], bottom_hbm),
    )
    slots, width = box_ref.shape
    devices = slots // capacity
    count = tile_ref.shape[1]
    channels = width - META
    earlier = (iota((count, count), 0) < iota((count, count), 1)).astype(F32).astype(BF16)
    for copy in waiting[:3]:
        copy.wait()
    tile = tile_ref[...]
    match = (iota((devices, count), 0) == tile).astype(F32)
    before = dot_nn(match.astype(BF16), earlier)
    position = jnp.sum(before * match, axis=0, keepdims=True)
    slot = tile * capacity + position.astype(jnp.int32)
    slot_ref[...] = slot
    leaving = [pltpu.make_async_copy(slot_ref, slot_hbm, out_semaphores.at[0])]
    leaving[0].start()
    cell = cell_ref[...]
    low, side = frac_ref[0:1, :], frac_ref[1:2, :]
    fields = (
        (cell >> 7).astype(F32),
        (cell & 127).astype(F32),
        (1.0 - low) * (1.0 - side),
        (1.0 - low) * side,
        low * (1.0 - side),
        low * side,
    )
    number = iota((META, count), 0)
    meta = jnp.zeros((META, count), F32)
    for index, field in enumerate(fields):
        meta = jnp.where(number == index, field, meta)
    meta = meta.astype(BF16)
    waiting[3].wait()
    waiting[4].wait()
    waiting[5].wait()
    cells = []
    for block_ref, at, side_ref, side_hbm in (
        (first_ref, 0, west_ref, west_hbm),
        (last_ref, 15, east_ref, east_hbm),
    ):
        lines = [block_ref[row].astype(F32)[at : at + 1] for row in range(rows)]
        cells += [lines[0], lines[-1]]
        side_ref[...] = jnp.concatenate(lines, axis=0).astype(BF16)
        leaving.append(
            pltpu.make_async_copy(side_ref, side_hbm, out_semaphores.at[len(leaving)])
        )
        leaving[-1].start()
    cells = (cells[0], cells[2], cells[1], cells[3])
    step = slots // 4
    for index in range(4):
        part = slice(index * step, (index + 1) * step)
        place = (iota((step, count), 0) + index * step == slot).astype(F32).astype(BF16)
        corners = corners_out(cells, lat, lon, capacity, index * step, step)
        box_ref[part, channels:] = (dot_nt(place, meta) + corners).astype(BF16)
        box_ref[part, :channels] = dot_nn(place, radiance_ref[...]).astype(BF16)
        leaving.append(
            pltpu.make_async_copy(
                box_ref.at[part, :], box_hbm.at[part, :], out_semaphores.at[len(leaving)]
            )
        )
        leaving[-1].start()
    for copy in leaving + waiting[6:]:
        copy.wait()


CHUNK = 512


def fill_row(shifted, row, center, left, right):
    columns = center.shape[0]
    place = iota(center.shape, 0)
    where = pl.ds(row * columns, columns)
    shifted[1, where, :] = center.astype(BF16)
    shifted[0, where, :] = jnp.where(place == 0, left, pltpu.roll(center, 1, 0)).astype(BF16)
    shifted[2, where, :] = jnp.where(
        place == columns - 1, right, pltpu.roll(center, columns - 1, 0)
    ).astype(BF16)


def no_halo_rows(shifted, rows, columns):
    zero = jnp.zeros((3, columns, shifted.shape[2]), BF16)
    shifted[:, :columns, :] = zero
    shifted[:, (rows + 1) * columns :, :] = zero


def halo_terms(left, right, north, south, corners, weight_ref):
    rows, columns = left.shape[0], north.shape[0]

    def along_row(center, first, last, row_step):
        place = iota(center.shape, 0)
        west = jnp.where(place == 0, first, pltpu.roll(center, 1, 0))
        east = jnp.where(place == columns - 1, last, pltpu.roll(center, columns - 1, 0))
        return sum(
            dot_nn(window.astype(BF16), weight_ref[row_step, col_step])
            for col_step, window in enumerate((west, center, east))
        )

    def along_column(side, col_step):
        place = iota(side.shape, 0)
        up = jnp.where(place == 0, 0.0, pltpu.roll(side, 1, 0))
        down = jnp.where(place == rows - 1, 0.0, pltpu.roll(side, rows - 1, 0))
        return sum(
            dot_nn(window.astype(BF16), weight_ref[row_step, col_step])
            for row_step, window in enumerate((up, side, down))
        )

    top = along_row(north, corners[0], corners[1], 0)
    bottom = along_row(south, corners[2], corners[3], 2)
    west, east = along_column(left, 0), along_column(right, 2)
    return top, bottom, west, east


def with_ends(term, first, last):
    place = iota(term.shape, 0)
    ends = jnp.where(place == 0, first, jnp.where(place == term.shape[0] - 1, last, 0.0))
    return term + ends


def convolve_rows(shifted, weight_ref, start, count, columns):
    total = None
    for row_step in range(3):
        for col_step in range(3):
            first = start + row_step * columns
            term = dot_nn(
                shifted[col_step, first : first + count, :], weight_ref[row_step, col_step]
            )
            total = term if total is None else total + term
    return total


BORDERS = 4


def forecast_kernel(
    columns,
    state_hbm,
    slope_hbm,
    weight_hbm,
    out_hbm,
    mirrored_hbm,
    borders_hbm,
    state_ref,
    slope_ref,
    weight_ref,
    out_ref,
    mirrored_ref,
    borders_ref,
    shifted,
    semaphores,
    out_semaphores,
):
    cells, channels = state_ref.shape
    rows = cells // columns
    waiting = copies(
        semaphores, (state_hbm, state_ref), (weight_hbm, weight_ref), (slope_hbm, slope_ref)
    )
    no_halo_rows(shifted, rows, columns)
    for copy in waiting:
        copy.wait()
    zero = jnp.zeros((1, channels), F32)
    per = CHUNK // columns
    steps = cells // CHUNK
    leaving = []
    for index in range(steps + 1):
        if index < steps:
            for row in range(index * per, (index + 1) * per):
                center = state_ref[row * columns : (row + 1) * columns, :].astype(F32)
                fill_row(shifted, row + 1, center, zero, zero)
        if index > 0:
            start = (index - 1) * CHUNK
            part = slice(start, start + CHUNK)
            response = convolve_rows(shifted, weight_ref, start, CHUNK, columns)
            slope = slope_ref[part, :].astype(F32)
            total = state_ref[part, :].astype(F32) + slope * response
            out_ref[part, :] = total.astype(BF16)
            leaving.append(
                pltpu.make_async_copy(
                    out_ref.at[part, :], out_hbm.at[part, :], out_semaphores.at[index - 1]
                )
            )
            leaving[-1].start()
            for inner in range(per):
                row = (index - 1) * per + inner
                first, last = inner * columns, (inner + 1) * columns - 1
                for number, line in enumerate(
                    (slope[first : first + 1], slope[last : last + 1])
                    + (total[first : first + 1], total[last : last + 1])
                ):
                    at = number * rows + row
                    borders_ref[at : at + 1, :] = line
            if index == 1:
                borders_ref[BORDERS * rows : BORDERS * rows + columns, :] = total[:columns]
            if index == steps:
                borders_ref[BORDERS * rows + columns :, :] = total[CHUNK - columns :]
    for row_step in range(3):
        for col_step in range(3):
            mirrored_ref[row_step, col_step] = (
                weight_ref[2 - row_step, 2 - col_step].astype(F32).T.astype(BF16)
            )
    leaving += [
        pltpu.make_async_copy(mirrored_ref, mirrored_hbm, out_semaphores.at[steps]),
        pltpu.make_async_copy(borders_ref, borders_hbm, out_semaphores.at[steps + 1]),
    ]
    leaving[-2].start()
    leaving[-1].start()
    for copy in leaving:
        copy.wait()


def gradient_kernel(
    columns,
    adjoint_hbm,
    fields_hbm,
    slope_hbm,
    weight_hbm,
    out_hbm,
    adjoint,
    fields_ref,
    slope_ref,
    weight_ref,
    out_ref,
    shifted,
    semaphores,
    out_semaphores,
):
    waiting = copies(
        semaphores,
        (fields_hbm, fields_ref),
        (adjoint_hbm, adjoint),
        (slope_hbm, slope_ref),
        (weight_hbm, weight_ref),
    )
    cells, channels = slope_ref.shape
    rows = cells // columns
    no_halo_rows(shifted, rows, columns)
    waiting[0].wait()
    around = turned_weights(fields_ref[...], columns)
    for copy in waiting[1:]:
        copy.wait()
    zero = jnp.zeros((1, channels), F32)
    per = CHUNK // columns
    steps = cells // CHUNK
    leaving = []
    for index in range(steps + 1):
        if index < steps:
            part = slice(index * CHUNK, (index + 1) * CHUNK)
            weights = [blend(*around, index * per + row) for row in range(per)]
            spread = dot_nn(jnp.concatenate(weights, axis=0), adjoint[...])
            out_ref[part, :] = spread
            pulled = slope_ref[part, :].astype(F32) * spread
            for inner in range(per):
                center = pulled[inner * columns : (inner + 1) * columns, :]
                fill_row(shifted, index * per + inner + 1, center, zero, zero)
        if index > 0:
            start = (index - 1) * CHUNK
            part = slice(start, start + CHUNK)
            out_ref[part, :] += convolve_rows(shifted, weight_ref, start, CHUNK, columns)
            leaving.append(
                pltpu.make_async_copy(
                    out_ref.at[part, :], out_hbm.at[part, :], out_semaphores.at[index - 1]
                )
            )
            leaving[-1].start()
    for copy in leaving:
        copy.wait()


def finish_kernel(
    capacity,
    gradient_hbm,
    slot_hbm,
    box_hbm,
    weight_hbm,
    left_hbm,
    right_hbm,
    north_hbm,
    south_hbm,
    out_hbm,
    departures_hbm,
    slot_ref,
    box_ref,
    weight_ref,
    left_ref,
    right_ref,
    north_ref,
    south_ref,
    lines_ref,
    sides_ref,
    departures_ref,
    semaphores,
    out_semaphores,
):
    del gradient_hbm
    lat, lon = lax.axis_index("lat"), lax.axis_index("lon")
    rows, columns, cell_channels = out_hbm.shape
    inner = pl.ds(8, columns - 16)
    places = (
        (lines_ref.at[0], out_hbm.at[0, inner, :]),
        (lines_ref.at[1], out_hbm.at[rows - 1, inner, :]),
        (sides_ref.at[0], out_hbm.at[:, pl.ds(0, 8), :]),
        (sides_ref.at[1], out_hbm.at[:, pl.ds(columns - 8, 8), :]),
    )
    waiting = copies(
        semaphores,
        (slot_hbm, slot_ref),
        (box_hbm, box_ref),
        (weight_hbm, weight_ref),
        (left_hbm, left_ref),
        (right_hbm, right_ref),
        (north_hbm, north_ref),
        (south_hbm, south_ref),
        *((there, here) for here, there in places),
    )
    slots = box_ref.shape[0]
    count = slot_ref.shape[1]
    channels = box_ref.shape[1] - META
    waiting[0].wait()
    turned = jnp.broadcast_to(slot_ref[...].astype(F32), (128, count)).T
    lane = iota((count, 128), 1).astype(F32)
    parts = [
        (lane + float(first) == turned).astype(F32).astype(BF16) for first in range(0, slots, 128)
    ]
    place = jnp.concatenate(parts, axis=1)
    waiting[1].wait()
    step = count // 2
    leaving = []
    for index in range(2):
        part = slice(index * step, (index + 1) * step)
        departures_ref[part, :] = dot_nn(place[part, :], box_ref[:, :channels])
        leaving.append(
            pltpu.make_async_copy(
                departures_ref.at[part, :], departures_hbm.at[part, :], out_semaphores.at[4 + index]
            )
        )
        leaving[-1].start()
    for copy in waiting[2:]:
        copy.wait()
    top, bottom, west, east = halo_terms(
        left_ref[...].astype(F32),
        right_ref[...].astype(F32),
        north_ref[...].astype(F32),
        south_ref[...].astype(F32),
        corners_in(box_ref[:, channels:], lat, lon, capacity, cell_channels),
        weight_ref,
    )
    lines_ref[0] += top[8 : columns - 8]
    lines_ref[1] += bottom[8 : columns - 8]
    leaving += copies(out_semaphores, *places[:2])
    place = iota((8, cell_channels), 0)
    for number, side, at in ((0, west, 0), (1, east, 7)):
        ends = (top[:8], bottom[:8]) if number == 0 else (top[-8:], bottom[-8:])
        for row in range(rows):
            term = jnp.where(place == at, side[row : row + 1], 0.0)
            if row == 0:
                term = term + ends[0]
            if row == rows - 1:
                term = term + ends[1]
            sides_ref[number, row] += term
        leaving.append(pltpu.make_async_copy(*places[2 + number], out_semaphores.at[2 + number]))
        leaving[-1].start()
    for copy in leaving:
        copy.wait()


def sigmoid(value):
    return 0.5 + 0.5 * jnp.tanh(0.5 * value)


def blend(row_low, row_high, upper, lower, at):
    at = jnp.asarray(at, BF16)
    zero = jnp.zeros(upper.shape, BF16)
    return jnp.where(row_low == at, upper, jnp.where(row_high == at, lower, zero))


def turned_weights(fields, columns):
    slots = fields.shape[1]
    row, column, w00, w01, w10, w11 = (fields[index : index + 1, :] for index in range(FIELDS))
    place = iota((columns, slots), 0).astype(F32)
    here, beside = place == column, place == column + 1.0
    upper = (jnp.where(here, w00, 0.0) + jnp.where(beside, w01, 0.0)).astype(BF16)
    lower = (jnp.where(here, w10, 0.0) + jnp.where(beside, w11, 0.0)).astype(BF16)
    row_low = jnp.broadcast_to(row, (columns, slots)).astype(BF16)
    row_high = jnp.broadcast_to(row + 1.0, (columns, slots)).astype(BF16)
    return row_low, row_high, upper, lower


def observe_kernel(
    columns,
    capacity,
    box_hbm,
    grid_hbm,
    weight_in_hbm,
    weight_mid_hbm,
    weight_out_hbm,
    vectors_hbm,
    slope_hbm,
    borders_hbm,
    conv_hbm,
    left_hbm,
    right_hbm,
    north_hbm,
    south_hbm,
    departures_hbm,
    adjoint_hbm,
    fields_hbm,
    west_ref,
    east_ref,
    top_ref,
    bottom_ref,
    box_ref,
    grid_ref,
    weight_in_ref,
    weight_mid_ref,
    weight_out_ref,
    vectors_ref,
    ends_ref,
    borders_ref,
    conv_ref,
    left_ref,
    right_ref,
    north_ref,
    south_ref,
    sampled,
    departures_ref,
    adjoint,
    fields_ref,
    semaphores,
    out_semaphores,
):
    lat, lon = lax.axis_index("lat"), lax.axis_index("lon")
    slots, width = box_ref.shape
    cells, grid_channels = grid_ref.shape
    channels = width - META
    hidden = weight_in_ref.shape[1]
    rows = cells // columns
    waiting = copies(
        semaphores,
        (box_hbm, box_ref),
        (left_hbm, left_ref),
        (right_hbm, right_ref),
        (north_hbm, north_ref),
        (south_hbm, south_ref),
        (conv_hbm, conv_ref),
        (slope_hbm.at[pl.ds(0, columns), :], ends_ref.at[0]),
        (slope_hbm.at[pl.ds(cells - columns, columns), :], ends_ref.at[1]),
        (borders_hbm, borders_ref),
        (grid_hbm, grid_ref),
        (weight_in_hbm, weight_in_ref),
        (vectors_hbm, vectors_ref),
        (weight_mid_hbm, weight_mid_ref),
        (weight_out_hbm, weight_out_ref),
    )
    waiting[0].wait()
    pick = (iota((16, META), 0) == iota((16, META), 1)).astype(F32).astype(BF16)
    fields_ref[...] = dot_nt(pick, box_ref[:, channels:])
    fields_out = pltpu.make_async_copy(fields_ref, fields_hbm, out_semaphores.at[0])
    fields_out.start()
    pick = iota((META, FIELDS * columns), 0) == iota((META, FIELDS * columns), 1) // columns
    wide = dot_nn(box_ref[:, channels:], pick.astype(F32).astype(BF16))
    row, column, w00, w01, w10, w11 = (
        wide[:, index * columns : (index + 1) * columns] for index in range(FIELDS)
    )
    lane = iota((slots, columns), 1).astype(F32)
    here, beside = lane == column, lane == column + 1.0
    upper = (jnp.where(here, w00, 0.0) + jnp.where(beside, w01, 0.0)).astype(BF16)
    lower = (jnp.where(here, w10, 0.0) + jnp.where(beside, w11, 0.0)).astype(BF16)
    row_low = row.astype(BF16)
    row_high = (row + 1.0).astype(BF16)
    for copy in waiting[1:10]:
        copy.wait()
    top, bottom, west, east = halo_terms(
        left_ref[...].astype(F32),
        right_ref[...].astype(F32),
        north_ref[...].astype(F32),
        south_ref[...].astype(F32),
        corners_in(box_ref[:, channels:], lat, lon, capacity, grid_channels),
        conv_ref,
    )
    place = iota((16, grid_channels), 0)
    for number, side, others, at, first in (
        (0, west, (top[:1], bottom[:1]), 0, 0),
        (1, east, (top[-1:], bottom[-1:]), 15, columns - 16),
    ):
        slope = borders_ref[number * rows : (number + 1) * rows, :]
        value = borders_ref[(number + 2) * rows : (number + 3) * rows, :]
        value = value + slope * with_ends(side, *others)
        for row in range(rows):
            part = slice(row * columns + first, row * columns + first + 16)
            grid_ref[part, :] = jnp.where(
                place == at, value[row : row + 1], grid_ref[part, :].astype(F32)
            ).astype(BF16)
    for number, line, at in ((0, top, 0), (1, bottom, rows - 1)):
        first = BORDERS * rows + number * columns
        line = with_ends(line, west[at : at + 1], east[at : at + 1])
        grid_ref[at * columns : (at + 1) * columns, :] = (
            borders_ref[first : first + columns, :] + ends_ref[number].astype(F32) * line
        ).astype(BF16)
    per = 8
    for block in range(rows // per):
        parts = [
            blend(row_low, row_high, upper, lower, block * per + index) for index in range(per)
        ]
        first = block * per * columns
        term = dot_nn(jnp.concatenate(parts, axis=1), grid_ref[first : first + per * columns, :])
        if block == 0:
            sampled[...] = term
        else:
            sampled[...] += term
    for copy in waiting[10:]:
        copy.wait()
    bias_in = vectors_ref[:, :hidden]
    bias_mid = vectors_ref[:, hidden : 2 * hidden]
    bias_out = vectors_ref[:, 2 * hidden : 2 * hidden + channels]
    inv_error = vectors_ref[:, 2 * hidden + channels :]
    step = 256
    for start in range(0, slots, step):
        part = slice(start, start + step)
        pre = dot_nn(sampled[part, :].astype(BF16), weight_in_ref[...]) + bias_in
        gate = sigmoid(pre)
        act = pre * gate
        slope_first = gate + act * (1.0 - gate)
        pre = dot_nn(act.astype(BF16), weight_mid_ref[...]) + bias_mid
        gate = sigmoid(pre)
        act = pre * gate
        slope_second = gate + act * (1.0 - gate)
        evolved = dot_nn(act.astype(BF16), weight_out_ref[...]) + bias_out
        departures = (evolved - box_ref[part, :channels].astype(F32)) * inv_error
        departures_ref[part, :channels] = departures.astype(BF16)
        back = (departures * inv_error).astype(BF16)
        back = (dot_nt(back, weight_out_ref[...]) * slope_second).astype(BF16)
        back = (dot_nt(back, weight_mid_ref[...]) * slope_first).astype(BF16)
        adjoint[part, :] = dot_nt(back, weight_in_ref[...]).astype(BF16)
    results = copies(out_semaphores.at[pl.ds(2, 1)], (adjoint, adjoint_hbm))
    fields = fields_ref[...]
    around = turned_weights(fields, columns)
    cells_out = []
    for at, index, edge_ref in ((0, 0, top_ref), (rows - 1, 1, bottom_ref)):
        spread = dot_nn(blend(*around, at), adjoint[...])
        pulled = ends_ref[index].astype(F32) * spread
        edge_ref[...] = pulled.astype(BF16)
        cells_out += [pulled[:1], pulled[columns - 1 :]]
    departures_ref[:, channels:] = corners_out(cells_out, lat, lon, capacity, 0, slots).astype(BF16)
    results += copies(out_semaphores.at[pl.ds(1, 1)], (departures_ref, departures_hbm))
    row, column, w00, w01, w10, w11 = (fields[index : index + 1, :] for index in range(FIELDS))
    place = iota((rows, slots), 0).astype(F32)
    here, below = place == row, place == row + 1.0
    zero = jnp.zeros((rows, slots), F32)
    for at, index, edge_ref, high, low in (
        (0.0, 0, west_ref, w00, w10),
        (columns - 2.0, 1, east_ref, w01, w11),
    ):
        chosen = column == at
        weights = jnp.where(
            here & chosen, high, jnp.where(below & chosen, low, zero)
        ).astype(BF16)
        slope = borders_ref[index * rows : (index + 1) * rows, :]
        edge_ref[...] = (slope * dot_nn(weights, adjoint[...])).astype(BF16)
    fields_out.wait()
    for copy in results:
        copy.wait()


def beside(west, east):
    count = lax.axis_size("lon")
    onward = [(i, (i + 1) % count) for i in range(count)]
    left = lax.ppermute(east, "lon", onward)
    right = lax.ppermute(west, "lon", [(target, source) for source, target in onward])
    return left, right


def over(top, bottom):
    down = [(i, i + 1) for i in range(lax.axis_size("lat") - 1)]
    north = lax.ppermute(bottom, "lat", down)
    south = lax.ppermute(top, "lat", [(target, source) for source, target in down])
    return north, south


def body(
    model_state,
    tangent_slope,
    conv_weight,
    weight_in,
    bias_in,
    weight_mid,
    bias_mid,
    weight_out,
    bias_out,
    obs_tile,
    obs_cell,
    obs_frac,
    radiance,
    inv_error,
):
    rows, columns, channels = model_state.shape
    cells = rows * columns
    devices = lax.axis_size("lat") * lax.axis_size("lon")
    count, bands = radiance.shape
    capacity = 2 * count // devices
    slots = devices * capacity
    hidden = weight_in.shape[1]
    sds = jax.ShapeDtypeStruct
    dma = pltpu.SemaphoreType.DMA

    def exchange(box):
        return lax.all_to_all(
            box.reshape(devices, capacity, -1), ("lat", "lon"), split_axis=0, concat_axis=0, tiled=True
        ).reshape(slots, -1)

    box, slot, west, east, top, bottom = kernel_call(
        functools.partial(dispatch_kernel, capacity),
        (
            sds((slots, bands + META), BF16),
            sds((1, count), jnp.int32),
            sds((rows, channels), BF16),
            sds((rows, channels), BF16),
            sds((columns, channels), BF16),
            sds((columns, channels), BF16),
        ),
        (HBM,) * 6,
        (HBM,) * 5,
        (
            pltpu.VMEM((1, count), jnp.int32),
            pltpu.VMEM((1, count), jnp.int32),
            pltpu.VMEM((2, count), F32),
            pltpu.VMEM((count, bands), BF16),
            pltpu.VMEM((rows, 16, channels), BF16),
            pltpu.VMEM((rows, 16, channels), BF16),
            pltpu.VMEM((slots, bands + META), BF16),
            pltpu.VMEM((1, count), jnp.int32),
            pltpu.VMEM((rows, channels), BF16),
            pltpu.VMEM((rows, channels), BF16),
            dma((8,)),
            dma((7,)),
        ),
        flops=2 * slots * count * (bands + META),
        moved=2 * slots * (bands + META),
        name="dispatch",
    )(obs_tile.reshape(1, count), obs_cell.reshape(1, count), obs_frac.T, radiance, model_state)
    arrived = exchange(box)

    conv_flops = 2 * 9 * cells * channels * channels
    steps = cells // CHUNK
    halo_scratch = (
        pltpu.VMEM((rows, channels), BF16),
        pltpu.VMEM((rows, channels), BF16),
        pltpu.VMEM((columns, channels), BF16),
        pltpu.VMEM((columns, channels), BF16),
    )
    shifted = pltpu.VMEM((3, (rows + 2) * columns, channels), BF16)
    borders_shape = (BORDERS * rows + 2 * columns, channels)
    flat_slope = tangent_slope.reshape(cells, channels)
    halo = beside(west, east) + over(top, bottom)
    forecast, mirrored, borders = kernel_call(
        functools.partial(forecast_kernel, columns),
        (sds((cells, channels), BF16), sds(conv_weight.shape, BF16), sds(borders_shape, F32)),
        (HBM,) * 3,
        (HBM,) * 3,
        (
            pltpu.VMEM((cells, channels), BF16),
            pltpu.VMEM((cells, channels), BF16),
            pltpu.VMEM(conv_weight.shape, BF16),
            pltpu.VMEM((cells, channels), BF16),
            pltpu.VMEM(conv_weight.shape, BF16),
            pltpu.VMEM(borders_shape, F32),
            shifted,
            dma((3,)),
            dma((steps + 2,)),
        ),
        flops=conv_flops,
        moved=6 * cells * channels,
        room=512,
        name="forecast",
    )(model_state.reshape(cells, channels), flat_slope, conv_weight)

    vectors = jnp.concatenate([bias_in, bias_mid, bias_out, inv_error]).reshape(1, -1)
    network_flops = 2 * slots * (channels * hidden + hidden * hidden + hidden * bands)
    departures_box, adjoint, fields, west, east, top, bottom = kernel_call(
        functools.partial(observe_kernel, columns, capacity),
        (
            sds((slots, bands + META), BF16),
            sds((slots, channels), BF16),
            sds((16, slots), F32),
            sds((rows, channels), BF16),
            sds((rows, channels), BF16),
            sds((columns, channels), BF16),
            sds((columns, channels), BF16),
        ),
        (HBM,) * 3 + (VMEM,) * 4,
        (HBM,) * 13,
        (
            pltpu.VMEM((slots, bands + META), BF16),
            pltpu.VMEM((cells, channels), BF16),
            pltpu.VMEM(weight_in.shape, BF16),
            pltpu.VMEM(weight_mid.shape, BF16),
            pltpu.VMEM(weight_out.shape, BF16),
            pltpu.VMEM(vectors.shape, F32),
            pltpu.VMEM((2, columns, channels), BF16),
            pltpu.VMEM(borders_shape, F32),
            pltpu.VMEM(conv_weight.shape, BF16),
            *halo_scratch,
            pltpu.VMEM((slots, channels), F32),
            pltpu.VMEM((slots, bands + META), BF16),
            pltpu.VMEM((slots, channels), BF16),
            pltpu.VMEM((16, slots), F32),
            dma((14,)),
            dma((3,)),
        ),
        flops=2 * network_flops + 2 * slots * cells * channels,
        moved=2 * cells * channels,
        room=1024 + 256,
        name="observe",
    )(
        arrived,
        forecast,
        weight_in,
        weight_mid,
        weight_out,
        vectors,
        flat_slope,
        borders,
        conv_weight,
        *halo,
    )

    returned = exchange(departures_box)
    halo = beside(west, east) + over(top, bottom)
    gradient, = kernel_call(
        functools.partial(gradient_kernel, columns),
        (sds((cells, channels), F32),),
        (HBM,),
        (HBM,) * 4,
        (
            pltpu.VMEM((slots, channels), BF16),
            pltpu.VMEM((16, slots), F32),
            pltpu.VMEM((cells, channels), BF16),
            pltpu.VMEM(conv_weight.shape, BF16),
            pltpu.VMEM((cells, channels), F32),
            shifted,
            dma((4,)),
            dma((steps,)),
        ),
        flops=conv_flops + 2 * slots * cells * channels,
        moved=4 * cells * channels,
        room=400,
        name="gradient",
    )(adjoint, fields, flat_slope, mirrored)
    gradient, departures = kernel_call(
        functools.partial(finish_kernel, capacity),
        (sds((rows, columns, channels), F32), sds((count, bands), F32)),
        (HBM, HBM),
        (HBM,) * 8,
        (
            pltpu.VMEM((1, count), jnp.int32),
            pltpu.VMEM((slots, bands + META), BF16),
            pltpu.VMEM(conv_weight.shape, BF16),
            *halo_scratch,
            pltpu.VMEM((2, columns - 16, channels), F32),
            pltpu.VMEM((2, rows, 8, channels), F32),
            pltpu.VMEM((count, bands), F32),
            dma((11,)),
            dma((6,)),
        ),
        flops=2 * slots * count * bands,
        moved=4 * count * bands,
        aliases={0: 0},
        room=1024 + 192,
        name="finish",
    )(gradient.reshape(rows, columns, channels), slot, returned, mirrored, *halo)
    return departures, gradient


def solution(mesh):
    in_specs = (
        P("lat", "lon", None),
        P("lat", "lon", None),
        P(),
        P(),
        P(),
        P(),
        P(),
        P(),
        P(),
        P(("lat", "lon"), None),
        P(("lat", "lon")),
        P(("lat", "lon"), None),
        P(("lat", "lon"), None),
        P(),
    )
    out_specs = (P(("lat", "lon"), None), P("lat", "lon", None))
    return jax.shard_map(body, mesh=mesh, in_specs=in_specs, out_specs=out_specs, check_vma=False)
```

time: 116 us -> 89.1 us (0.77)
  the two profiles are of different devices: /device:TPU:19 before, /device:TPU:1 now
where the time goes in v2:
time: 89.1 us; the launch traced here: 88.7 us
  Pallas kernels  44.5 us (50%)
  starting transfers between devices  40.4 us (45%)
  local copies, waits for them, and re-layouts  2.64 us (3%)
  between operations  1.2 us (1%)
    all_to_all x2, starting transfers between devices, exchange(): lax.all_to_all(box.reshape(devices, capacity, -1), ('lat', 'lon'), split_...  17.6 us
    pallas_call x1, Pallas kernels, body(): kernel_call(functools.partial(observe_kernel, columns, capacity), (sds((s...  15.6 us
    pallas_call x1, Pallas kernels, body(): kernel_call(functools.partial(gradient_kernel, columns), (sds((cells, cha...  10.7 us
    pallas_call x1, Pallas kernels, body(): kernel_call(functools.partial(forecast_kernel, columns), (sds((cells, cha...  9.48 us
    ppermute x2, starting transfers between devices, beside(): lax.ppermute(west, 'lon', [(target, source) for source, target in onward])  8.3 us
    ppermute x2, starting transfers between devices, over(): north = lax.ppermute(bottom, 'lat', down)  7.25 us
    pallas_call x1, Pallas kernels, body(): kernel_call(functools.partial(dispatch_kernel, capacity), (sds((slots, ba...  5.21 us
    ppermute x2, starting transfers between devices, over(): lax.ppermute(top, 'lat', [(target, source) for source, target in down])  4.02 us
  transfers between devices with their start and end apart: 10, of which 0 were waited for; matrix products, arithmetic and copies ran while one was open for 1% of the time, Pallas kernels for 23%

profile of v2, /device:TPU:1, one launch (start us, length us, event | category | flops | bytes accessed | tf_op | source)
XLA Modules:
  0.0 88.7 jit_solution(8420207863209596620)
XLA Ops:
  0.6 5.2 %dispatch.1 = (bf16[1024,512]{1,0:T(8,128)(2,1)}, s32[1,512]{1,0:T(1,128)}, bf16[32,256]{1,0:T(8,128)(2,1)}, bf16[32,256]{1,0:T(8,128)(2,1)}, bf16[128,256]{1,0:T(8,128)(2,1)}, /*index=5*/bf16[128,256]{1,0:T(8,128)(2,1)}) custom-call(s32[1,512]{1,0:T(1,128)} %bitcast.17, s32[1,512]{1,0:T(1,128)} %bitcast.18, f32[2,512]{1,0:T(2,128)} %bitcast.16, ...), custom_call_target="tpu_custom_call" | custom-call | flops 536870912 | bytes 1048576 | tf_op jit(solution)/shard_map/dispatch/pallas_call | solution.py:748
  5.9 0.0 copy-start.21
  5.9 0.0 copy-start.20
  5.9 0.0 copy-start.14
  5.9 0.0 copy-start.12
  5.9 11.5 %all-to-all-start = ((bf16[128,8,512]{2,1,0:T(8,128)(2,1)}), bf16[128,8,512]{2,1,0:T(8,128)(2,1)S(1)}, u32[]{:S(2)}, u32[]{:S(2)}) async-start(bf16[128,8,512]{2,1,0:T(8,128)(2,1)} %bitcast.15), calls=%async_computation | async-start | bytes 2097152 | tf_op jit(solution)/shard_map/all_to_all | solution.py:744
  17.4 0.0 copy-done.21
  17.4 1.6 %collective-permute-start = (bf16[32,256]{1,0:T(8,128)(2,1)S(1)}, bf16[32,256]{1,0:T(8,128)(2,1)S(1)}, u32[]{:S(2)}, u32[]{:S(2)}) collective-permute-start(bf16[32,256]{1,0:T(8,128)(2,1)S(1)} %copy-done.21), channel_id=1, source_target_pairs={{0,1},{1,2},{2,3},{3,4},{4,5},{5,6},{6,7},{7,8},{8,9},{9,10},{10,1... | collective-permute-start | bytes 49160 | tf_op jit(solution)/shard_map/ppermute | solution.py:705
  19.0 0.0 copy-done.20
  19.0 4.2 %collective-permute-start.1 = (bf16[32,256]{1,0:T(8,128)(2,1)S(1)}, bf16[32,256]{1,0:T(8,128)(2,1)S(1)}, u32[]{:S(2)}, u32[]{:S(2)}) collective-permute-start(bf16[32,256]{1,0:T(8,128)(2,1)S(1)} %copy-done.20), channel_id=1, source_target_pairs={{1,0},{2,1},{3,2},{4,3},{5,4},{6,5},{7,6},{8,7},{9,8},{10,9},{11,1... | collective-permute-start | bytes 49160 | tf_op jit(solution)/shard_map/ppermute | solution.py:706
  23.1 0.0 copy-done.14
  23.1 3.6 %collective-permute-start.2 = (bf16[128,256]{1,0:T(8,128)(2,1)S(1)}, bf16[128,256]{1,0:T(8,128)(2,1)S(1)}, u32[]{:S(2)}, u32[]{:S(2)}) collective-permute-start(bf16[128,256]{1,0:T(8,128)(2,1)S(1)} %copy-done.14), channel_id=1, source_target_pairs={{0,16},{16,32},{32,48},{48,64},{64,80},{80,96},{96,112},{1,17},{17... | collective-permute-start | bytes 196616 | tf_op jit(solution)/shard_map/ppermute | solution.py:712
  26.8 0.0 copy-done.12
  26.8 2.1 %collective-permute-start.3 = (bf16[128,256]{1,0:T(8,128)(2,1)S(1)}, bf16[128,256]{1,0:T(8,128)(2,1)S(1)}, u32[]{:S(2)}, u32[]{:S(2)}) collective-permute-start(bf16[128,256]{1,0:T(8,128)(2,1)S(1)} %copy-done.12), channel_id=1, source_target_pairs={{16,0},{32,16},{48,32},{64,48},{80,64},{96,80},{112,96},{17,1},{33... | collective-permute-start | bytes 196616 | tf_op jit(solution)/shard_map/ppermute | solution.py:713
  28.9 0.0 copy-start.6
  28.9 0.0 copy-start.7
  28.9 0.0 copy-start.8
  28.9 0.0 copy-start.9
  28.9 9.5 %forecast.1 = (bf16[4096,256]{1,0:T(8,128)(2,1)}, bf16[3,3,256,256]{3,2,1,0:T(8,128)(2,1)}, f32[384,256]{1,0:T(8,128)}) custom-call(bf16[4096,256]{1,0:T(8,128)(2,1)} %bitcast.12, bf16[4096,256]{1,0:T(8,128)(2,1)} %bitcast.19, bf16[3,3,256,256]{3,2,1,0:T(8,128)(2,1)} %conv_hbm.1), custom_call_target="tpu_custom_call" | custom-call | flops 4831838208 | bytes 6291456 | tf_op jit(solution)/shard_map/forecast/pallas_call | solution.py:792
  38.4 0.0 copy-done.6
  38.4 0.0 copy-done.7
  38.5 0.0 copy-done.8
  38.5 0.0 copy-done.9
  38.5 0.6 reshape.40.vectors_hbm
  39.1 0.0 collective-permute-done.left_hbm
  39.1 0.0 collective-permute-done.1.right_hbm
  39.1 0.0 copy-start.17
  39.1 0.0 collective-permute-done.2.north_hbm
  39.1 0.0 copy-start.13
  39.1 0.0 collective-permute-done.3.south_hbm
  39.2 0.0 copy-start.15
  39.2 0.0 all-to-all-done
  39.2 0.0 copy-start.1
  39.2 0.5 copy-done.16
  39.7 0.0 copy-done.17
  39.7 0.0 copy-done.13
  39.8 0.0 copy-done.15
  39.8 0.4 copy-done.1
  40.2 15.6 %observe.1 = (bf16[1024,512]{1,0:T(8,128)(2,1)}, bf16[1024,256]{1,0:T(8,128)(2,1)}, f32[16,1024]{1,0:T(8,128)}, bf16[32,256]{1,0:T(8,128)(2,1)}, bf16[32,256]{1,...) custom-call(bf16[1024,512]{1,0:T(8,128)(2,1)} %bitcast.13, ...), custom_call_target="tpu_custom_call" | custom-call | flops 4563402752 | bytes 2097152 | tf_op jit(solution)/shard_map/observe/pallas_call | solution.py:816
  55.7 0.0 copy-start.19
  55.7 0.0 copy-start.18
  55.8 0.0 copy-start.11
  55.8 0.0 copy-start.10
  55.8 6.1 %all-to-all-start.1 = ((bf16[128,8,512]{2,1,0:T(8,128)(2,1)}), bf16[128,8,512]{2,1,0:T(8,128)(2,1)S(1)}, u32[]{:S(2)}, u32[]{:S(2)}) async-start(bf16[128,8,512]{2,1,0:T(8,128)(2,1)} %bitcast.14), calls=%async_computation.1 | async-start | bytes 2097152 | tf_op jit(solution)/shard_map/all_to_all | solution.py:744
  61.9 0.0 copy-done.19
  61.9 1.6 %collective-permute-start.4 = (bf16[32,256]{1,0:T(8,128)(2,1)S(1)}, bf16[32,256]{1,0:T(8,128)(2,1)S(1)}, u32[]{:S(2)}, u32[]{:S(2)}) collective-permute-start(bf16[32,256]{1,0:T(8,128)(2,1)S(1)} %copy-done.19), channel_id=1, source_target_pairs={{0,1},{1,2},{2,3},{3,4},{4,5},{5,6},{6,7},{7,8},{8,9},{9,10},{10,1... | collective-permute-start | bytes 49160 | tf_op jit(solution)/shard_map/ppermute | solution.py:705
  63.5 0.0 copy-done.18
  63.5 4.2 %collective-permute-start.5 = (bf16[32,256]{1,0:T(8,128)(2,1)S(1)}, bf16[32,256]{1,0:T(8,128)(2,1)S(1)}, u32[]{:S(2)}, u32[]{:S(2)}) collective-permute-start(bf16[32,256]{1,0:T(8,128)(2,1)S(1)} %copy-done.18), channel_id=1, source_target_pairs={{1,0},{2,1},{3,2},{4,3},{5,4},{6,5},{7,6},{8,7},{9,8},{10,9},{11,1... | collective-permute-start | bytes 49160 | tf_op jit(solution)/shard_map/ppermute | solution.py:706
  67.7 3.6 %collective-permute-start.6 = (bf16[128,256]{1,0:T(8,128)(2,1)S(1)}, bf16[128,256]{1,0:T(8,128)(2,1)S(1)}, u32[]{:S(2)}, u32[]{:S(2)}) collective-permute-start(bf16[128,256]{1,0:T(8,128)(2,1)S(1)} %copy-done.11), channel_id=1, source_target_pairs={{0,16},{16,32},{32,48},{48,64},{64,80},{80,96},{96,112},{1,17},{17... | collective-permute-start | bytes 196616 | tf_op jit(solution)/shard_map/ppermute | solution.py:712
  71.3 1.9 %collective-permute-start.7 = (bf16[128,256]{1,0:T(8,128)(2,1)S(1)}, bf16[128,256]{1,0:T(8,128)(2,1)S(1)}, u32[]{:S(2)}, u32[]{:S(2)}) collective-permute-start(bf16[128,256]{1,0:T(8,128)(2,1)S(1)} %copy-done.10), channel_id=1, source_target_pairs={{16,0},{32,16},{48,32},{64,48},{80,64},{96,80},{112,96},{17,1},{33... | collective-permute-start | bytes 196616 | tf_op jit(solution)/shard_map/ppermute | solution.py:713
  73.2 10.7 %gradient.1 = f32[4096,256]{1,0:T(8,128)} custom-call(bf16[1024,256]{1,0:T(8,128)(2,1)} %get-tuple-element.27.adjoint_hbm, f32[16,1024]{1,0:T(8,128)} %get-tuple-element.28.fields_hbm, bf16[4096,256]{1,0:T(8,128)(2,1)} %bitcast.21, bf16[3,3,256,256]{3,2,1,0:T(8,128)(2,1)} %get-tuple-element.29.weight_hbm), custom_call_target="tpu_custom_call" | custom-call | flops 6979321856 | bytes 4194304 | tf_op jit(solution)/shard_map/gradient/pallas_call | solution.py:866
  84.0 0.0 collective-permute-done.4.left_hbm
  84.0 0.0 copy-start.4
  84.0 0.0 collective-permute-done.5.right_hbm
  84.0 0.0 collective-permute-done.6.north_hbm
  84.0 0.0 collective-permute-done.7.south_hbm
  84.0 0.0 copy-start.3
  84.1 0.0 all-to-all-done.1
  84.1 0.5 copy-done.4
  84.6 0.0 copy-done.5
  84.6 0.0 copy-done.2
  84.6 0.0 copy-done.3
  84.7 0.4 copy-done
  85.0 3.5 %finish.1 = (f32[32,128,256]{2,1,0:T(8,128)}, f32[512,384]{1,0:T(8,128)}) custom-call(f32[32,128,256]{2,1,0:T(8,128)} %bitcast.10, s32[1,512]{1,0:T(1,128)} %get-tuple-element.30.slot_hbm, bf16[1024,512]{1,0:T(8,128)(2,1)} %bitcast.11, bf16[3,3,256,256]{3,2,1,0:T(8,128)(2,1)} %get-tuple-element.29.weight_hbm, ...), custom_call_target="tpu_custom_call", output_to_operand_aliasing={{0}: (0, {})} | custom-call | flops 402653184 | bytes 786432 | tf_op jit(solution)/shard_map/finish/pallas_call | solution.py:886
  (7 shorter events, 0.0 us)
Async XLA Ops:
  5.9 11.6 %copy-start.21 = (bf16[32,256]{1,0:T(8,128)(2,1)S(1)}, bf16[32,256]{1,0:T(8,128)(2,1)}, u32[]{:S(2)}) copy-start(bf16[32,256]{1,0:T(8,128)(2,1)} %get-tuple-element.23) | copy-start | bytes 49156
  5.9 13.1 %copy-start.20 = (bf16[32,256]{1,0:T(8,128)(2,1)S(1)}, bf16[32,256]{1,0:T(8,128)(2,1)}, u32[]{:S(2)}) copy-start(bf16[32,256]{1,0:T(8,128)(2,1)} %get-tuple-element.24) | copy-start | bytes 49156
  5.9 17.3 %copy-start.14 = (bf16[128,256]{1,0:T(8,128)(2,1)S(1)}, bf16[128,256]{1,0:T(8,128)(2,1)}, u32[]{:S(2)}) copy-start(bf16[128,256]{1,0:T(8,128)(2,1)} %get-tuple-element.25) | copy-start | bytes 196612
  5.9 20.9 %copy-start.12 = (bf16[128,256]{1,0:T(8,128)(2,1)S(1)}, bf16[128,256]{1,0:T(8,128)(2,1)}, u32[]{:S(2)}) copy-start(bf16[128,256]{1,0:T(8,128)(2,1)} %get-tuple-element.26) | copy-start | bytes 196612
  5.9 33.3 %all-to-all-start = ((bf16[128,8,512]{2,1,0:T(8,128)(2,1)}), bf16[128,8,512]{2,1,0:T(8,128)(2,1)S(1)}, u32[]{:S(2)}, u32[]{:S(2)}) async-start(bf16[128,8,512]{2,1,0:T(8,128)(2,1)} %bitcast.15), calls=%async_computation | async-start | bytes 2097152 | tf_op jit(solution)/shard_map/all_to_all | solution.py:744
  17.4 21.7 %collective-permute-start = (bf16[32,256]{1,0:T(8,128)(2,1)S(1)}, bf16[32,256]{1,0:T(8,128)(2,1)S(1)}, u32[]{:S(2)}, u32[]{:S(2)}) collective-permute-start(bf16[32,256]{1,0:T(8,128)(2,1)S(1)} %copy-done.21), channel_id=1, source_target_pairs={{0,1},{1,2},{2,3},{3,4},{4,5},{5,6},{6,7},{7,8},{8,9},{9,10},{10,1... | collective-permute-start | bytes 49160 | tf_op jit(solution)/shard_map/ppermute | solution.py:705
  19.0 20.1 %collective-permute-start.1 = (bf16[32,256]{1,0:T(8,128)(2,1)S(1)}, bf16[32,256]{1,0:T(8,128)(2,1)S(1)}, u32[]{:S(2)}, u32[]{:S(2)}) collective-permute-start(bf16[32,256]{1,0:T(8,128)(2,1)S(1)} %copy-done.20), channel_id=1, source_target_pairs={{1,0},{2,1},{3,2},{4,3},{5,4},{6,5},{7,6},{8,7},{9,8},{10,9},{11,1... | collective-permute-start | bytes 49160 | tf_op jit(solution)/shard_map/ppermute | solution.py:706
  23.1 16.0 %collective-permute-start.2 = (bf16[128,256]{1,0:T(8,128)(2,1)S(1)}, bf16[128,256]{1,0:T(8,128)(2,1)S(1)}, u32[]{:S(2)}, u32[]{:S(2)}) collective-permute-start(bf16[128,256]{1,0:T(8,128)(2,1)S(1)} %copy-done.14), channel_id=1, source_target_pairs={{0,16},{16,32},{32,48},{48,64},{64,80},{80,96},{96,112},{1,17},{17... | collective-permute-start | bytes 196616 | tf_op jit(solution)/shard_map/ppermute | solution.py:712
  26.8 12.4 %collective-permute-start.3 = (bf16[128,256]{1,0:T(8,128)(2,1)S(1)}, bf16[128,256]{1,0:T(8,128)(2,1)S(1)}, u32[]{:S(2)}, u32[]{:S(2)}) collective-permute-start(bf16[128,256]{1,0:T(8,128)(2,1)S(1)} %copy-done.12), channel_id=1, source_target_pairs={{16,0},{32,16},{48,32},{64,48},{80,64},{96,80},{112,96},{17,1},{33... | collective-permute-start | bytes 196616 | tf_op jit(solution)/shard_map/ppermute | solution.py:713
  28.9 9.5 %copy-start.6 = (f32[384]{0:T(512)S(1)}, f32[384]{0:T(512)}, u32[]{:S(2)}) copy-start(f32[384]{0:T(512)} %param.27) | copy-start | bytes 4612
  28.9 9.5 %copy-start.7 = (f32[384]{0:T(512)S(1)}, f32[384]{0:T(512)}, u32[]{:S(2)}) copy-start(f32[384]{0:T(512)} %param.22) | copy-start | bytes 4612
  28.9 9.5 %copy-start.8 = (f32[512]{0:T(512)S(1)}, f32[512]{0:T(512)}, u32[]{:S(2)}) copy-start(f32[512]{0:T(512)} %param.20) | copy-start | bytes 6148
  28.9 9.5 %copy-start.9 = (f32[512]{0:T(512)S(1)}, f32[512]{0:T(512)}, u32[]{:S(2)}) copy-start(f32[512]{0:T(512)} %param.18) | copy-start | bytes 6148
  39.1 0.6 copy-start.16
  39.1 0.6 copy-start.17
  39.1 0.6 copy-start.13
  39.2 0.6 copy-start.15
  39.2 1.0 %copy-start.1 = (bf16[128,8,512]{2,1,0:T(8,128)(2,1)}, bf16[128,8,512]{2,1,0:T(8,128)(2,1)S(1)}, u32[]{:S(2)}) copy-start(bf16[128,8,512]{2,1,0:T(8,128)(2,1)S(1)} %all-to-all-done) | copy-start | bytes 3145732
  55.7 6.2 %copy-start.19 = (bf16[32,256]{1,0:T(8,128)(2,1)S(1)}, bf16[32,256]{1,0:T(8,128)(2,1)}, u32[]{:S(2)}) copy-start(bf16[32,256]{1,0:T(8,128)(2,1)} %get-tuple-element.32) | copy-start | bytes 49156
  55.7 7.8 %copy-start.18 = (bf16[32,256]{1,0:T(8,128)(2,1)S(1)}, bf16[32,256]{1,0:T(8,128)(2,1)}, u32[]{:S(2)}) copy-start(bf16[32,256]{1,0:T(8,128)(2,1)} %get-tuple-element.33) | copy-start | bytes 49156
  55.8 11.9 %copy-start.11 = (bf16[128,256]{1,0:T(8,128)(2,1)S(1)}, bf16[128,256]{1,0:T(8,128)(2,1)}, u32[]{:S(2)}) copy-start(bf16[128,256]{1,0:T(8,128)(2,1)} %get-tuple-element.34) | copy-start | bytes 196612
  55.8 15.5 %copy-start.10 = (bf16[128,256]{1,0:T(8,128)(2,1)S(1)}, bf16[128,256]{1,0:T(8,128)(2,1)}, u32[]{:S(2)}) copy-start(bf16[128,256]{1,0:T(8,128)(2,1)} %get-tuple-element.35) | copy-start | bytes 196612
  55.8 28.3 %all-to-all-start.1 = ((bf16[128,8,512]{2,1,0:T(8,128)(2,1)}), bf16[128,8,512]{2,1,0:T(8,128)(2,1)S(1)}, u32[]{:S(2)}, u32[]{:S(2)}) async-start(bf16[128,8,512]{2,1,0:T(8,128)(2,1)} %bitcast.14), calls=%async_computation.1 | async-start | bytes 2097152 | tf_op jit(solution)/shard_map/all_to_all | solution.py:744
  61.9 22.0 %collective-permute-start.4 = (bf16[32,256]{1,0:T(8,128)(2,1)S(1)}, bf16[32,256]{1,0:T(8,128)(2,1)S(1)}, u32[]{:S(2)}, u32[]{:S(2)}) collective-permute-start(bf16[32,256]{1,0:T(8,128)(2,1)S(1)} %copy-done.19), channel_id=1, source_target_pairs={{0,1},{1,2},{2,3},{3,4},{4,5},{5,6},{6,7},{7,8},{8,9},{9,10},{10,1... | collective-permute-start | bytes 49160 | tf_op jit(solution)/shard_map/ppermute | solution.py:705
  63.5 20.5 %collective-permute-start.5 = (bf16[32,256]{1,0:T(8,128)(2,1)S(1)}, bf16[32,256]{1,0:T(8,128)(2,1)S(1)}, u32[]{:S(2)}, u32[]{:S(2)}) collective-permute-start(bf16[32,256]{1,0:T(8,128)(2,1)S(1)} %copy-done.18), channel_id=1, source_target_pairs={{1,0},{2,1},{3,2},{4,3},{5,4},{6,5},{7,6},{8,7},{9,8},{10,9},{11,1... | collective-permute-start | bytes 49160 | tf_op jit(solution)/shard_map/ppermute | solution.py:706
  67.7 16.4 %collective-permute-start.6 = (bf16[128,256]{1,0:T(8,128)(2,1)S(1)}, bf16[128,256]{1,0:T(8,128)(2,1)S(1)}, u32[]{:S(2)}, u32[]{:S(2)}) collective-permute-start(bf16[128,256]{1,0:T(8,128)(2,1)S(1)} %copy-done.11), channel_id=1, source_target_pairs={{0,16},{16,32},{32,48},{48,64},{64,80},{80,96},{96,112},{1,17},{17... | collective-permute-start | bytes 196616 | tf_op jit(solution)/shard_map/ppermute | solution.py:712
  71.3 12.7 %collective-permute-start.7 = (bf16[128,256]{1,0:T(8,128)(2,1)S(1)}, bf16[128,256]{1,0:T(8,128)(2,1)S(1)}, u32[]{:S(2)}, u32[]{:S(2)}) collective-permute-start(bf16[128,256]{1,0:T(8,128)(2,1)S(1)} %copy-done.10), channel_id=1, source_target_pairs={{16,0},{32,16},{48,32},{64,48},{80,64},{96,80},{112,96},{17,1},{33... | collective-permute-start | bytes 196616 | tf_op jit(solution)/shard_map/ppermute | solution.py:713
  84.0 0.6 copy-start.4
  84.0 0.6 copy-start.5
  84.0 0.6 copy-start.2
  84.0 0.6 copy-start.3
  84.1 1.0 %copy-start = (bf16[128,8,512]{2,1,0:T(8,128)(2,1)}, bf16[128,8,512]{2,1,0:T(8,128)(2,1)S(1)}, u32[]{:S(2)}) copy-start(bf16[128,8,512]{2,1,0:T(8,128)(2,1)S(1)} %all-to-all-done.1) | copy-start | bytes 3145732

commit v3 on v2

--- a/solution.py
+++ b/solution.py
@@ -12,6 +12,7 @@
 META = 128
 FIELDS = 6
 VMEM_KIB = 60 * 1024 + 512
+ROOM = 1024 + 256
 
 
 def dot_nt(left, right):
@@ -57,17 +58,16 @@
 CORNER_WIDTH = 32
 
 
-def corner_slots(lat, lon, capacity, shape, dim):
+def diagonal_blocks(lat, lon, capacity):
     lats, lons = lax.axis_size("lat"), lax.axis_size("lon")
-    number = iota(shape, dim)
-    result = jnp.full(shape, -1, jnp.int32)
-    for index, (down, right) in enumerate(((-1, -1), (-1, 1), (1, -1), (1, 1))):
+    blocks = []
+    for down, right in ((-1, -1), (-1, 1), (1, -1), (1, 1)):
         row, column = lat + down, lax.rem(lon + right + lons, lons)
         inside = (row >= 0) & (row < lats)
-        first = jnp.where(inside, (row * lons + column) * capacity, -4096)
-        mine = (number >= index * 8) & (number < index * 8 + 8)
-        result = jnp.where(mine, first + number - index * 8, result)
-    return result
+        first = jnp.where(inside, row * lons + column, 0) * capacity
+        aligned = pl.multiple_of((first // 16) * 16, 16)
+        blocks.append((inside, aligned, lax.rem(first, 16)))
+    return blocks
 
 
 def corner_fold(shape, lane_dim):
@@ -80,22 +80,30 @@
     return iota(shape, 1) // CORNER_WIDTH == iota(shape, 0) % 8
 
 
-def corners_out(cells, lat, lon, capacity, first, count):
-    channels = cells[0].shape[1]
-    spread = jnp.concatenate([jnp.broadcast_to(cell, (8, channels)) for cell in cells], axis=0)
+def corners_out(cells, lat, lon, capacity, box_ref, channels):
+    width = cells[0].shape[1]
+    spread = jnp.concatenate([jnp.broadcast_to(cell, (8, width)) for cell in cells], axis=0)
     kept = jnp.where(corner_mask(spread.shape), spread, 0.0).astype(BF16)
-    folded = dot_nn(kept, corner_fold((channels, META), 1)).astype(BF16)
-    target = corner_slots(lat, lon, capacity, (count, 32), 1)
-    place = (iota((count, 32), 0) + first == target).astype(F32).astype(BF16)
-    return dot_nn(place, folded)
-
-
-def corners_in(lanes, lat, lon, capacity, channels):
-    slots = lanes.shape[0]
-    source = corner_slots(lat, lon, capacity, (32, slots), 0)
-    place = (iota((32, slots), 1) == source).astype(F32).astype(BF16)
-    folded = dot_nn(place, lanes).astype(BF16)
-    spread = dot_nn(folded, corner_fold((META, channels), 0))
+    folded = dot_nn(kept, corner_fold((width, META), 1))
+    half = (iota((16, META), 0) // 8) * 8
+    for index, (inside, first, own) in enumerate(diagonal_blocks(lat, lon, capacity)):
+        lines = folded[8 * index : 8 * index + 8]
+        lines = jnp.where(half == own, jnp.concatenate([lines, lines], axis=0), 0.0)
+
+        @pl.when(inside)
+        def _():
+            which = pl.ds(first, 16)
+            box_ref[which, channels:] = (box_ref[which, channels:].astype(F32) + lines).astype(BF16)
+
+
+def corners_in(box_ref, lat, lon, capacity, channels, width):
+    lines = []
+    for inside, first, own in diagonal_blocks(lat, lon, capacity):
+        block = box_ref[pl.ds(first, 16), channels:].astype(F32)
+        mine = jnp.where(own == 0, block[:8], block[8:])
+        lines.append(jnp.where(inside, mine, 0.0))
+    folded = jnp.concatenate(lines, axis=0).astype(BF16)
+    spread = dot_nn(folded, corner_fold((META, width), 0))
     kept = jnp.where(corner_mask(spread.shape), spread, 0.0)
     return [jnp.sum(kept[8 * index : 8 * index + 8], axis=0, keepdims=True) for index in range(4)]
 
@@ -123,6 +131,7 @@
     slot_ref,
     west_ref,
     east_ref,
+    lines_ref,
     semaphores,
     out_semaphores,
 ):
@@ -136,8 +145,8 @@
         (radiance_hbm, radiance_ref),
         (state_hbm.at[:, pl.ds(0, 16), :], first_ref),
         (state_hbm.at[:, pl.ds(columns - 16, 16), :], last_ref),
-        (state_hbm.at[0], top_hbm),
-        (state_hbm.at[rows - 1], bottom_hbm),
+        (state_hbm.at[0], lines_ref.at[0]),
+        (state_hbm.at[rows - 1], lines_ref.at[1]),
     )
     slots, width = box_ref.shape
     devices = slots // capacity
@@ -170,8 +179,13 @@
         meta = jnp.where(number == index, field, meta)
     meta = meta.astype(BF16)
     waiting[3].wait()
-    waiting[4].wait()
-    waiting[5].wait()
+    for copy in waiting[4:]:
+        copy.wait()
+    for index, line_hbm in enumerate((top_hbm, bottom_hbm)):
+        leaving.append(
+            pltpu.make_async_copy(lines_ref.at[index], line_hbm, out_semaphores.at[len(leaving)])
+        )
+        leaving[-1].start()
     cells = []
     for block_ref, at, side_ref, side_hbm in (
         (first_ref, 0, west_ref, west_hbm),
@@ -189,20 +203,18 @@
     for index in range(4):
         part = slice(index * step, (index + 1) * step)
         place = (iota((step, count), 0) + index * step == slot).astype(F32).astype(BF16)
-        corners = corners_out(cells, lat, lon, capacity, index * step, step)
-        box_ref[part, channels:] = (dot_nt(place, meta) + corners).astype(BF16)
+        box_ref[part, channels:] = dot_nt(place, meta).astype(BF16)
         box_ref[part, :channels] = dot_nn(place, radiance_ref[...]).astype(BF16)
-        leaving.append(
-            pltpu.make_async_copy(
-                box_ref.at[part, :], box_hbm.at[part, :], out_semaphores.at[len(leaving)]
-            )
-        )
-        leaving[-1].start()
-    for copy in leaving + waiting[6:]:
+    corners_out(cells, lat, lon, capacity, box_ref, channels)
+    leaving.append(pltpu.make_async_copy(box_ref, box_hbm, out_semaphores.at[len(leaving)]))
+    leaving[-1].start()
+    for copy in leaving:
         copy.wait()
 
 
 CHUNK = 512
+FORECAST_GROUPS = (0, 2, 6, 8)
+GRADIENT_GROUPS = (0, 4, 8)
 
 
 def fill_row(shifted, row, center, left, right):
@@ -222,30 +234,42 @@
     shifted[:, (rows + 1) * columns :, :] = zero
 
 
-def halo_terms(left, right, north, south, corners, weight_ref):
+def halo_terms(left, right, north, south, corners, weight_ref, mirror):
     rows, columns = left.shape[0], north.shape[0]
-
-    def along_row(center, first, last, row_step):
+    product, weight_of = taps(weight_ref, mirror)
+
+    def row_windows(center, first, last):
         place = iota(center.shape, 0)
         west = jnp.where(place == 0, first, pltpu.roll(center, 1, 0))
         east = jnp.where(place == columns - 1, last, pltpu.roll(center, columns - 1, 0))
-        return sum(
-            dot_nn(window.astype(BF16), weight_ref[row_step, col_step])
-            for col_step, window in enumerate((west, center, east))
-        )
-
-    def along_column(side, col_step):
+        return west, center, east
+
+    def column_windows(side):
         place = iota(side.shape, 0)
         up = jnp.where(place == 0, 0.0, pltpu.roll(side, 1, 0))
         down = jnp.where(place == rows - 1, 0.0, pltpu.roll(side, rows - 1, 0))
-        return sum(
-            dot_nn(window.astype(BF16), weight_ref[row_step, col_step])
-            for row_step, window in enumerate((up, side, down))
-        )
-
-    top = along_row(north, corners[0], corners[1], 0)
-    bottom = along_row(south, corners[2], corners[3], 2)
-    west, east = along_column(left, 0), along_column(right, 2)
+        return up, side, down
+
+    lines = {0: row_windows(north, *corners[:2]), 2: row_windows(south, *corners[2:])}
+    sides = {0: column_windows(left), 2: column_windows(right)}
+    line_terms, side_terms = {0: 0.0, 2: 0.0}, {0: 0.0, 2: 0.0}
+    for row_step in range(3):
+        for col_step in range(3):
+            windows = []
+            if row_step != 1:
+                windows.append(lines[row_step][col_step])
+            if col_step != 1:
+                windows.append(sides[col_step][row_step])
+            if not windows:
+                continue
+            term = product(
+                jnp.concatenate(windows, axis=0).astype(BF16), weight_of(row_step, col_step)
+            )
+            if row_step != 1:
+                line_terms[row_step] += term[:columns]
+            if col_step != 1:
+                side_terms[col_step] += term[-rows:]
+    top, bottom, west, east = line_terms[0], line_terms[2], side_terms[0], side_terms[2]
     return top, bottom, west, east
 
 
@@ -255,16 +279,26 @@
     return term + ends
 
 
-def convolve_rows(shifted, weight_ref, start, count, columns):
+def taps(weight_ref, mirror):
+    if mirror:
+        return dot_nt, lambda row_step, col_step: weight_ref[2 - row_step, 2 - col_step]
+    return dot_nn, lambda row_step, col_step: weight_ref[row_step, col_step]
+
+
+def convolve_rows(shifted, weight_ref, start, count, columns, mirror):
+    product, weight_of = taps(weight_ref, mirror)
     total = None
     for row_step in range(3):
         for col_step in range(3):
             first = start + row_step * columns
-            term = dot_nn(
-                shifted[col_step, first : first + count, :], weight_ref[row_step, col_step]
-            )
+            term = product(shifted[col_step, first : first + count, :], weight_of(row_step, col_step))
             total = term if total is None else total + term
     return total
+
+
+def span_copy(source, target, semaphore, first, last):
+    which = pl.ds(first * CHUNK, (last - first) * CHUNK)
+    return pltpu.make_async_copy(source.at[which, :], target.at[which, :], semaphore)
 
 
 BORDERS = 4
@@ -276,73 +310,82 @@
     slope_hbm,
     weight_hbm,
     out_hbm,
-    mirrored_hbm,
     borders_hbm,
     state_ref,
     slope_ref,
     weight_ref,
     out_ref,
-    mirrored_ref,
     borders_ref,
     shifted,
-    semaphores,
+    weight_semaphore,
+    state_semaphores,
+    slope_semaphores,
     out_semaphores,
 ):
     cells, channels = state_ref.shape
     rows = cells // columns
-    waiting = copies(
-        semaphores, (state_hbm, state_ref), (weight_hbm, weight_ref), (slope_hbm, slope_ref)
-    )
-    no_halo_rows(shifted, rows, columns)
-    for copy in waiting:
-        copy.wait()
-    zero = jnp.zeros((1, channels), F32)
     per = CHUNK // columns
     steps = cells // CHUNK
-    leaving = []
-    for index in range(steps + 1):
-        if index < steps:
-            for row in range(index * per, (index + 1) * per):
-                center = state_ref[row * columns : (row + 1) * columns, :].astype(F32)
-                fill_row(shifted, row + 1, center, zero, zero)
-        if index > 0:
-            start = (index - 1) * CHUNK
-            part = slice(start, start + CHUNK)
-            response = convolve_rows(shifted, weight_ref, start, CHUNK, columns)
+    zero = jnp.zeros((1, channels), F32)
+    groups = list(zip(FORECAST_GROUPS[:-1], FORECAST_GROUPS[1:]))
+
+    def copies_in(number):
+        first, last = groups[number]
+        ahead = (first + 1 if number else 0), min(last + 1, steps)
+        found = [
+            span_copy(slope_hbm, slope_ref, slope_semaphores.at[number], first, last)
+        ]
+        if ahead[0] < ahead[1]:
+            found.append(span_copy(state_hbm, state_ref, state_semaphores.at[number], *ahead))
+        if number == 0:
+            found.append(pltpu.make_async_copy(weight_hbm, weight_ref, weight_semaphore.at[0]))
+        return found[::-1]
+
+    def fill(index):
+        for row in range(index * per, (index + 1) * per):
+            center = state_ref[row * columns : (row + 1) * columns, :].astype(F32)
+            fill_row(shifted, row + 1, center, zero, zero)
+
+    coming = copies_in(0)
+    for copy in coming:
+        copy.start()
+    no_halo_rows(shifted, rows, columns)
+    out = []
+    for number, (low, high) in enumerate(groups):
+        for copy in coming:
+            copy.wait()
+        if number + 1 < len(groups):
+            coming = copies_in(number + 1)
+            for copy in coming:
+                copy.start()
+        if number == 0:
+            fill(0)
+        for index in range(low, high):
+            if index + 1 < steps:
+                fill(index + 1)
+            part = slice(index * CHUNK, (index + 1) * CHUNK)
+            response = convolve_rows(shifted, weight_ref, part.start, CHUNK, columns, False)
             slope = slope_ref[part, :].astype(F32)
             total = state_ref[part, :].astype(F32) + slope * response
             out_ref[part, :] = total.astype(BF16)
-            leaving.append(
-                pltpu.make_async_copy(
-                    out_ref.at[part, :], out_hbm.at[part, :], out_semaphores.at[index - 1]
-                )
-            )
-            leaving[-1].start()
             for inner in range(per):
-                row = (index - 1) * per + inner
+                row = index * per + inner
                 first, last = inner * columns, (inner + 1) * columns - 1
-                for number, line in enumerate(
+                for kind, line in enumerate(
                     (slope[first : first + 1], slope[last : last + 1])
                     + (total[first : first + 1], total[last : last + 1])
                 ):
-                    at = number * rows + row
+                    at = kind * rows + row
                     borders_ref[at : at + 1, :] = line
-            if index == 1:
+            if index == 0:
                 borders_ref[BORDERS * rows : BORDERS * rows + columns, :] = total[:columns]
-            if index == steps:
+            if index == steps - 1:
                 borders_ref[BORDERS * rows + columns :, :] = total[CHUNK - columns :]
-    for row_step in range(3):
-        for col_step in range(3):
-            mirrored_ref[row_step, col_step] = (
-                weight_ref[2 - row_step, 2 - col_step].astype(F32).T.astype(BF16)
-            )
-    leaving += [
-        pltpu.make_async_copy(mirrored_ref, mirrored_hbm, out_semaphores.at[steps]),
-        pltpu.make_async_copy(borders_ref, borders_hbm, out_semaphores.at[steps + 1]),
-    ]
-    leaving[-2].start()
-    leaving[-1].start()
-    for copy in leaving:
+        out.append(span_copy(out_ref, out_hbm, out_semaphores.at[number], low, high))
+        out[-1].start()
+    out.append(pltpu.make_async_copy(borders_ref, borders_hbm, out_semaphores.at[steps]))
+    out[-1].start()
+    for copy in out:
         copy.wait()
 
 
@@ -360,47 +403,65 @@
     out_ref,
     shifted,
     semaphores,
+    slope_semaphores,
     out_semaphores,
 ):
-    waiting = copies(
-        semaphores,
-        (fields_hbm, fields_ref),
-        (adjoint_hbm, adjoint),
-        (slope_hbm, slope_ref),
-        (weight_hbm, weight_ref),
-    )
     cells, channels = slope_ref.shape
     rows = cells // columns
+    per = CHUNK // columns
+    steps = cells // CHUNK
+    waiting = copies(semaphores, (fields_hbm, fields_ref), (adjoint_hbm, adjoint))
+    zero = jnp.zeros((1, channels), F32)
+    groups = list(zip(GRADIENT_GROUPS[:-1], GRADIENT_GROUPS[1:]))
+
+    def copies_in(number):
+        first, last = groups[number]
+        ahead = (first + 1 if number else 0), min(last + 1, steps)
+        if ahead[0] == ahead[1]:
+            return []
+        return [span_copy(slope_hbm, slope_ref, slope_semaphores.at[number], *ahead)]
+
+    coming = copies_in(0) + [pltpu.make_async_copy(weight_hbm, weight_ref, semaphores.at[2])]
+    for copy in coming:
+        copy.start()
     no_halo_rows(shifted, rows, columns)
     waiting[0].wait()
     around = turned_weights(fields_ref[...], columns)
-    for copy in waiting[1:]:
-        copy.wait()
-    zero = jnp.zeros((1, channels), F32)
-    per = CHUNK // columns
-    steps = cells // CHUNK
-    leaving = []
-    for index in range(steps + 1):
-        if index < steps:
+    waiting[1].wait()
+
+    def spread(index):
+        weights = [blend(*around, index * per + row) for row in range(per)]
+        out_ref[index * CHUNK : (index + 1) * CHUNK, :] = dot_nn(
+            jnp.concatenate(weights, axis=0), adjoint[...]
+        )
+
+    def fill(index):
+        part = slice(index * CHUNK, (index + 1) * CHUNK)
+        pulled = slope_ref[part, :].astype(F32) * out_ref[part, :]
+        for inner in range(per):
+            center = pulled[inner * columns : (inner + 1) * columns, :]
+            fill_row(shifted, index * per + inner + 1, center, zero, zero)
+
+    for index in range(steps):
+        spread(index)
+    out = []
+    for number, (low, high) in enumerate(groups):
+        for copy in coming:
+            copy.wait()
+        if number + 1 < len(groups):
+            coming = copies_in(number + 1)
+            for copy in coming:
+                copy.start()
+        if number == 0:
+            fill(0)
+        for index in range(low, high):
+            if index + 1 < steps:
+                fill(index + 1)
             part = slice(index * CHUNK, (index + 1) * CHUNK)
-            weights = [blend(*around, index * per + row) for row in range(per)]
-            spread = dot_nn(jnp.concatenate(weights, axis=0), adjoint[...])
-            out_ref[part, :] = spread
-            pulled = slope_ref[part, :].astype(F32) * spread
-            for inner in range(per):
-                center = pulled[inner * columns : (inner + 1) * columns, :]
-                fill_row(shifted, index * per + inner + 1, center, zero, zero)
-        if index > 0:
-            start = (index - 1) * CHUNK
-            part = slice(start, start + CHUNK)
-            out_ref[part, :] += convolve_rows(shifted, weight_ref, start, CHUNK, columns)
-            leaving.append(
-                pltpu.make_async_copy(
-                    out_ref.at[part, :], out_hbm.at[part, :], out_semaphores.at[index - 1]
-                )
-            )
-            leaving[-1].start()
-    for copy in leaving:
+            out_ref[part, :] += convolve_rows(shifted, weight_ref, part.start, CHUNK, columns, True)
+        out.append(span_copy(out_ref, out_hbm, out_semaphores.at[number], low, high))
+        out[-1].start()
+    for copy in out:
         copy.wait()
 
 
@@ -479,8 +540,9 @@
         right_ref[...].astype(F32),
         north_ref[...].astype(F32),
         south_ref[...].astype(F32),
-        corners_in(box_ref[:, channels:], lat, lon, capacity, cell_channels),
+        corners_in(box_ref, lat, lon, capacity, channels, cell_channels),
         weight_ref,
+        True,
     )
     lines_ref[0] += top[8 : columns - 8]
     lines_ref[1] += bottom[8 : columns - 8]
@@ -531,7 +593,10 @@
     weight_in_hbm,
     weight_mid_hbm,
     weight_out_hbm,
-    vectors_hbm,
+    bias_in_hbm,
+    bias_mid_hbm,
+    bias_out_hbm,
+    inv_error_hbm,
     slope_hbm,
     borders_hbm,
     conv_hbm,
@@ -551,7 +616,10 @@
     weight_in_ref,
     weight_mid_ref,
     weight_out_ref,
-    vectors_ref,
+    bias_in_ref,
+    bias_mid_ref,
+    bias_out_ref,
+    inv_error_ref,
     ends_ref,
     borders_ref,
     conv_ref,
@@ -572,22 +640,27 @@
     channels = width - META
     hidden = weight_in_ref.shape[1]
     rows = cells // columns
+    lanes, spare = pl.ds(0, channels), pl.ds(channels, META)
     waiting = copies(
         semaphores,
-        (box_hbm, box_ref),
+        (box_hbm.at[:, spare], box_ref.at[:, spare]),
         (left_hbm, left_ref),
         (right_hbm, right_ref),
         (north_hbm, north_ref),
         (south_hbm, south_ref),
         (conv_hbm, conv_ref),
+        (grid_hbm, grid_ref),
         (slope_hbm.at[pl.ds(0, columns), :], ends_ref.at[0]),
         (slope_hbm.at[pl.ds(cells - columns, columns), :], ends_ref.at[1]),
         (borders_hbm, borders_ref),
-        (grid_hbm, grid_ref),
         (weight_in_hbm, weight_in_ref),
-        (vectors_hbm, vectors_ref),
+        (bias_in_hbm, bias_in_ref),
+        (bias_mid_hbm, bias_mid_ref),
+        (bias_out_hbm, bias_out_ref),
+        (inv_error_hbm, inv_error_ref),
         (weight_mid_hbm, weight_mid_ref),
         (weight_out_hbm, weight_out_ref),
+        (box_hbm.at[:, lanes], box_ref.at[:, lanes]),
     )
     waiting[0].wait()
     pick = (iota((16, META), 0) == iota((16, META), 1)).astype(F32).astype(BF16)
@@ -605,16 +678,19 @@
     lower = (jnp.where(here, w10, 0.0) + jnp.where(beside, w11, 0.0)).astype(BF16)
     row_low = row.astype(BF16)
     row_high = (row + 1.0).astype(BF16)
-    for copy in waiting[1:10]:
+    for copy in waiting[1:6]:
         copy.wait()
     top, bottom, west, east = halo_terms(
         left_ref[...].astype(F32),
         right_ref[...].astype(F32),
         north_ref[...].astype(F32),
         south_ref[...].astype(F32),
-        corners_in(box_ref[:, channels:], lat, lon, capacity, grid_channels),
+        corners_in(box_ref, lat, lon, capacity, channels, grid_channels),
         conv_ref,
-    )
+        False,
+    )
+    for copy in waiting[6:10]:
+        copy.wait()
     place = iota((16, grid_channels), 0)
     for number, side, others, at, first in (
         (0, west, (top[:1], bottom[:1]), 0, 0),
@@ -634,24 +710,18 @@
         grid_ref[at * columns : (at + 1) * columns, :] = (
             borders_ref[first : first + columns, :] + ends_ref[number].astype(F32) * line
         ).astype(BF16)
-    per = 8
-    for block in range(rows // per):
-        parts = [
-            blend(row_low, row_high, upper, lower, block * per + index) for index in range(per)
-        ]
-        first = block * per * columns
-        term = dot_nn(jnp.concatenate(parts, axis=1), grid_ref[first : first + per * columns, :])
-        if block == 0:
-            sampled[...] = term
-        else:
-            sampled[...] += term
+    strip = 256
+    for start in range(0, slots, strip):
+        part = slice(start, start + strip)
+        parts = [blend(row_low[part], row_high[part], upper[part], lower[part], at) for at in range(rows)]
+        sampled[part, :] = dot_nn(jnp.concatenate(parts, axis=1), grid_ref[...])
     for copy in waiting[10:]:
         copy.wait()
-    bias_in = vectors_ref[:, :hidden]
-    bias_mid = vectors_ref[:, hidden : 2 * hidden]
-    bias_out = vectors_ref[:, 2 * hidden : 2 * hidden + channels]
-    inv_error = vectors_ref[:, 2 * hidden + channels :]
-    step = 256
+    bias_in, bias_mid, bias_out, inv_error = (
+        ref[...].reshape(1, -1) for ref in (bias_in_ref, bias_mid_ref, bias_out_ref, inv_error_ref)
+    )
+    step = 512
+    results = []
     for start in range(0, slots, step):
         part = slice(start, start + step)
         pre = dot_nn(sampled[part, :].astype(BF16), weight_in_ref[...]) + bias_in
@@ -669,31 +739,41 @@
         back = (dot_nt(back, weight_out_ref[...]) * slope_second).astype(BF16)
         back = (dot_nt(back, weight_mid_ref[...]) * slope_first).astype(BF16)
         adjoint[part, :] = dot_nt(back, weight_in_ref[...]).astype(BF16)
-    results = copies(out_semaphores.at[pl.ds(2, 1)], (adjoint, adjoint_hbm))
+        which = pl.ds(start, step)
+        results += copies(
+            out_semaphores.at[pl.ds(1 + len(results), 2)],
+            (departures_ref.at[which, lanes], departures_hbm.at[which, lanes]),
+            (adjoint.at[which, :], adjoint_hbm.at[which, :]),
+        )
     fields = fields_ref[...]
     around = turned_weights(fields, columns)
-    cells_out = []
-    for at, index, edge_ref in ((0, 0, top_ref), (rows - 1, 1, bottom_ref)):
-        spread = dot_nn(blend(*around, at), adjoint[...])
-        pulled = ends_ref[index].astype(F32) * spread
-        edge_ref[...] = pulled.astype(BF16)
-        cells_out += [pulled[:1], pulled[columns - 1 :]]
-    departures_ref[:, channels:] = corners_out(cells_out, lat, lon, capacity, 0, slots).astype(BF16)
-    results += copies(out_semaphores.at[pl.ds(1, 1)], (departures_ref, departures_hbm))
     row, column, w00, w01, w10, w11 = (fields[index : index + 1, :] for index in range(FIELDS))
     place = iota((rows, slots), 0).astype(F32)
     here, below = place == row, place == row + 1.0
     zero = jnp.zeros((rows, slots), F32)
-    for at, index, edge_ref, high, low in (
-        (0.0, 0, west_ref, w00, w10),
-        (columns - 2.0, 1, east_ref, w01, w11),
-    ):
+    weights = [blend(*around, 0), blend(*around, rows - 1)]
+    for at, high, low in ((0.0, w00, w10), (columns - 2.0, w01, w11)):
         chosen = column == at
-        weights = jnp.where(
-            here & chosen, high, jnp.where(below & chosen, low, zero)
-        ).astype(BF16)
+        weights.append(
+            jnp.where(here & chosen, high, jnp.where(below & chosen, low, zero)).astype(BF16)
+        )
+    spread = dot_nn(jnp.concatenate(weights, axis=0), adjoint[...])
+    cells_out = []
+    for index, edge_ref in enumerate((top_ref, bottom_ref)):
+        first = index * columns
+        pulled = ends_ref[index].astype(F32) * spread[first : first + columns]
+        edge_ref[...] = pulled.astype(BF16)
+        cells_out += [pulled[:1], pulled[columns - 1 :]]
+    for index, edge_ref in enumerate((west_ref, east_ref)):
+        first = 2 * columns + index * rows
         slope = borders_ref[index * rows : (index + 1) * rows, :]
-        edge_ref[...] = (slope * dot_nn(weights, adjoint[...])).astype(BF16)
+        edge_ref[...] = (slope * spread[first : first + rows]).astype(BF16)
+    departures_ref[:, channels:] = jnp.zeros((slots, META), BF16)
+    corners_out(cells_out, lat, lon, capacity, departures_ref, channels)
+    results += copies(
+        out_semaphores.at[pl.ds(1 + len(results), 1)],
+        (departures_ref.at[:, spare], departures_hbm.at[:, spare]),
+    )
     fields_out.wait()
     for copy in results:
         copy.wait()
@@ -768,8 +848,9 @@
             pltpu.VMEM((1, count), jnp.int32),
             pltpu.VMEM((rows, channels), BF16),
             pltpu.VMEM((rows, channels), BF16),
+            pltpu.VMEM((2, columns, channels), BF16),
             dma((8,)),
-            dma((7,)),
+            dma((6,)),
         ),
         flops=2 * slots * count * (bands + META),
         moved=2 * slots * (bands + META),
@@ -789,21 +870,22 @@
     borders_shape = (BORDERS * rows + 2 * columns, channels)
     flat_slope = tangent_slope.reshape(cells, channels)
     halo = beside(west, east) + over(top, bottom)
-    forecast, mirrored, borders = kernel_call(
+    forecast, borders = kernel_call(
         functools.partial(forecast_kernel, columns),
-        (sds((cells, channels), BF16), sds(conv_weight.shape, BF16), sds(borders_shape, F32)),
-        (HBM,) * 3,
+        (sds((cells, channels), BF16), sds(borders_shape, F32)),
+        (HBM,) * 2,
         (HBM,) * 3,
         (
             pltpu.VMEM((cells, channels), BF16),
             pltpu.VMEM((cells, channels), BF16),
             pltpu.VMEM(conv_weight.shape, BF16),
             pltpu.VMEM((cells, channels), BF16),
-            pltpu.VMEM(conv_weight.shape, BF16),
             pltpu.VMEM(borders_shape, F32),
             shifted,
-            dma((3,)),
-            dma((steps + 2,)),
+            dma((1,)),
+            dma((steps,)),
+            dma((steps,)),
+            dma((steps + 1,)),
         ),
         flops=conv_flops,
         moved=6 * cells * channels,
@@ -811,7 +893,6 @@
         name="forecast",
     )(model_state.reshape(cells, channels), flat_slope, conv_weight)
 
-    vectors = jnp.concatenate([bias_in, bias_mid, bias_out, inv_error]).reshape(1, -1)
     network_flops = 2 * slots * (channels * hidden + hidden * hidden + hidden * bands)
     departures_box, adjoint, fields, west, east, top, bottom = kernel_call(
         functools.partial(observe_kernel, columns, capacity),
@@ -825,14 +906,14 @@
             sds((columns, channels), BF16),
         ),
         (HBM,) * 3 + (VMEM,) * 4,
-        (HBM,) * 13,
+        (HBM,) * 16,
         (
             pltpu.VMEM((slots, bands + META), BF16),
             pltpu.VMEM((cells, channels), BF16),
             pltpu.VMEM(weight_in.shape, BF16),
             pltpu.VMEM(weight_mid.shape, BF16),
             pltpu.VMEM(weight_out.shape, BF16),
-            pltpu.VMEM(vectors.shape, F32),
+            *(pltpu.VMEM(vector.shape, F32) for vector in (bias_in, bias_mid, bias_out, inv_error)),
             pltpu.VMEM((2, columns, channels), BF16),
             pltpu.VMEM(borders_shape, F32),
             pltpu.VMEM(conv_weight.shape, BF16),
@@ -841,12 +922,12 @@
             pltpu.VMEM((slots, bands + META), BF16),
             pltpu.VMEM((slots, channels), BF16),
             pltpu.VMEM((16, slots), F32),
-            dma((14,)),
-            dma((3,)),
+            dma((18,)),
+            dma((6,)),
         ),
         flops=2 * network_flops + 2 * slots * cells * channels,
         moved=2 * cells * channels,
-        room=1024 + 256,
+        room=ROOM,
         name="observe",
     )(
         arrived,
@@ -854,7 +935,10 @@
         weight_in,
         weight_mid,
         weight_out,
-        vectors,
+        bias_in,
+        bias_mid,
+        bias_out,
+        inv_error,
         flat_slope,
         borders,
         conv_weight,
@@ -875,14 +959,15 @@
             pltpu.VMEM(conv_weight.shape, BF16),
             pltpu.VMEM((cells, channels), F32),
             shifted,
-            dma((4,)),
+            dma((3,)),
+            dma((steps,)),
             dma((steps,)),
         ),
         flops=conv_flops + 2 * slots * cells * channels,
         moved=4 * cells * channels,
         room=400,
         name="gradient",
-    )(adjoint, fields, flat_slope, mirrored)
+    )(adjoint, fields, flat_slope, conv_weight)
     gradient, departures = kernel_call(
         functools.partial(finish_kernel, capacity),
         (sds((rows, columns, channels), F32), sds((count, bands), F32)),
@@ -904,7 +989,7 @@
         aliases={0: 0},
         room=1024 + 192,
         name="finish",
-    )(gradient.reshape(rows, columns, channels), slot, returned, mirrored, *halo)
+    )(gradient.reshape(rows, columns, channels), slot, returned, conv_weight, *halo)
     return departures, gradient
 
 

time: 89.1 us -> 79.9 us (0.90)
  Pallas kernels: 44.5 us -> 36 us
    pallas_call x1, Pallas kernels: 15.6 us -> 9.96 us  [body(): kernel_call(functools.partial(observe_kernel, columns, capacity), (sds((s...]
    pallas_call x1, Pallas kernels: 5.21 us -> 3.29 us  [body(): kernel_call(functools.partial(dispatch_kernel, capacity), (sds((slots, ba...]
    pallas_call x1, Pallas kernels: 9.48 us -> 8.44 us  [body(): kernel_call(functools.partial(forecast_kernel, columns), (sds((cells, cha...]
    unnamed x44 -> x36, local copies, waits for them, and re-layouts: 2.02 us -> 1.98 us
  transfers between devices with their start and end apart: 10 -> 10, of which waited for: 0 -> 0; matrix products, arithmetic and copies ran while one was open for 1% -> 0% of each run, Pallas kernels for 23% -> 24%
where the time goes in v3:
time: 79.9 us; the launch traced here: 79.5 us
  starting transfers between devices  40.4 us (51%)
  Pallas kernels  36 us (45%)
  local copies, waits for them, and re-layouts  1.98 us (2%)
  between operations  1.15 us (1%)
    all_to_all x2, starting transfers between devices, exchange(): lax.all_to_all(box.reshape(devices, capacity, -1), ('lat', 'lon'), split_...  17.6 us
    pallas_call x1, Pallas kernels, body(): kernel_call(functools.partial(gradient_kernel, columns), (sds((cells, cha...  10.4 us
    pallas_call x1, Pallas kernels, body(): kernel_call(functools.partial(observe_kernel, columns, capacity), (sds((s...  9.96 us
    pallas_call x1, Pallas kernels, body(): kernel_call(functools.partial(forecast_kernel, columns), (sds((cells, cha...  8.44 us
    ppermute x2, starting transfers between devices, beside(): lax.ppermute(west, 'lon', [(target, source) for source, target in onward])  8.3 us
    ppermute x2, starting transfers between devices, over(): north = lax.ppermute(bottom, 'lat', down)  7.25 us
    ppermute x2, starting transfers between devices, over(): lax.ppermute(top, 'lat', [(target, source) for source, target in down])  4.02 us
    pallas_call x1, Pallas kernels, body(): kernel_call(functools.partial(finish_kernel, capacity), (sds((rows, colum...  3.87 us
  transfers between devices with their start and end apart: 10, of which 0 were waited for; matrix products, arithmetic and copies ran while one was open for 0% of the time, Pallas kernels for 24%

profile of v3, /device:TPU:1, one launch (start us, length us, event | category | flops | bytes accessed | tf_op | source)
XLA Modules:
  0.0 79.5 jit_solution(3188563970836306067)
XLA Ops:
  0.6 3.3 %dispatch.1 = (bf16[1024,512]{1,0:T(8,128)(2,1)}, s32[1,512]{1,0:T(1,128)}, bf16[32,256]{1,0:T(8,128)(2,1)}, bf16[32,256]{1,0:T(8,128)(2,1)}, bf16[128,256]{1,0:T(8,128)(2,1)}, /*index=5*/bf16[128,256]{1,0:T(8,128)(2,1)}) custom-call(s32[1,512]{1,0:T(1,128)} %bitcast.17, s32[1,512]{1,0:T(1,128)} %bitcast.18, f32[2,512]{1,0:T(2,128)} %bitcast.16, ...), custom_call_target="tpu_custom_call" | custom-call | flops 536870912 | bytes 1048576 | tf_op jit(solution)/shard_map/dispatch/pallas_call | solution.py:828
  3.9 0.0 copy-start.17
  3.9 0.0 copy-start.16
  3.9 0.0 copy-start.11
  4.0 0.0 copy-start.9
  4.0 11.5 %all-to-all-start = ((bf16[128,8,512]{2,1,0:T(8,128)(2,1)}), bf16[128,8,512]{2,1,0:T(8,128)(2,1)S(1)}, u32[]{:S(2)}, u32[]{:S(2)}) async-start(bf16[128,8,512]{2,1,0:T(8,128)(2,1)} %bitcast.15), calls=%async_computation | async-start | bytes 2097152 | tf_op jit(solution)/shard_map/all_to_all | solution.py:824
  15.5 0.0 copy-done.17
  15.5 1.6 %collective-permute-start = (bf16[32,256]{1,0:T(8,128)(2,1)S(1)}, bf16[32,256]{1,0:T(8,128)(2,1)S(1)}, u32[]{:S(2)}, u32[]{:S(2)}) collective-permute-start(bf16[32,256]{1,0:T(8,128)(2,1)S(1)} %copy-done.17), channel_id=1, source_target_pairs={{0,1},{1,2},{2,3},{3,4},{4,5},{5,6},{6,7},{7,8},{8,9},{9,10},{10,1... | collective-permute-start | bytes 49160 | tf_op jit(solution)/shard_map/ppermute | solution.py:785
  17.1 0.0 copy-done.16
  17.1 4.2 %collective-permute-start.1 = (bf16[32,256]{1,0:T(8,128)(2,1)S(1)}, bf16[32,256]{1,0:T(8,128)(2,1)S(1)}, u32[]{:S(2)}, u32[]{:S(2)}) collective-permute-start(bf16[32,256]{1,0:T(8,128)(2,1)S(1)} %copy-done.16), channel_id=1, source_target_pairs={{1,0},{2,1},{3,2},{4,3},{5,4},{6,5},{7,6},{8,7},{9,8},{10,9},{11,1... | collective-permute-start | bytes 49160 | tf_op jit(solution)/shard_map/ppermute | solution.py:786
  21.2 0.0 copy-done.11
  21.2 3.6 %collective-permute-start.2 = (bf16[128,256]{1,0:T(8,128)(2,1)S(1)}, bf16[128,256]{1,0:T(8,128)(2,1)S(1)}, u32[]{:S(2)}, u32[]{:S(2)}) collective-permute-start(bf16[128,256]{1,0:T(8,128)(2,1)S(1)} %copy-done.11), channel_id=1, source_target_pairs={{0,16},{16,32},{32,48},{48,64},{64,80},{80,96},{96,112},{1,17},{17... | collective-permute-start | bytes 196616 | tf_op jit(solution)/shard_map/ppermute | solution.py:792
  24.9 0.0 copy-done.9
  24.9 2.1 %collective-permute-start.3 = (bf16[128,256]{1,0:T(8,128)(2,1)S(1)}, bf16[128,256]{1,0:T(8,128)(2,1)S(1)}, u32[]{:S(2)}, u32[]{:S(2)}) collective-permute-start(bf16[128,256]{1,0:T(8,128)(2,1)S(1)} %copy-done.9), channel_id=1, source_target_pairs={{16,0},{32,16},{48,32},{64,48},{80,64},{96,80},{112,96},{17,1},{33... | collective-permute-start | bytes 196616 | tf_op jit(solution)/shard_map/ppermute | solution.py:793
  27.0 8.4 %forecast.1 = (bf16[4096,256]{1,0:T(8,128)(2,1)}, f32[384,256]{1,0:T(8,128)}) custom-call(bf16[4096,256]{1,0:T(8,128)(2,1)} %bitcast.12, bf16[4096,256]{1,0:T(8,128)(2,1)} %bitcast.19, bf16[3,3,256,256]{3,2,1,0:T(8,128)(2,1)} %weight_hbm.5), custom_call_target="tpu_custom_call" | custom-call | flops 4831838208 | bytes 6291456 | tf_op jit(solution)/shard_map/forecast/pallas_call | solution.py:873
  35.4 0.0 collective-permute-done.left_hbm
  35.4 0.0 copy-start.12
  35.4 0.0 collective-permute-done.1.right_hbm
  35.4 0.0 copy-start.13
  35.5 0.0 collective-permute-done.2.north_hbm
  35.5 0.0 copy-start.8
  35.5 0.0 collective-permute-done.3.south_hbm
  35.5 0.0 copy-start.10
  35.5 0.0 all-to-all-done
  35.5 0.0 copy-start.1
  35.5 0.5 copy-done.12
  36.0 0.0 copy-done.13
  36.1 0.0 copy-done.8
  36.1 0.0 copy-done.10
  36.1 0.4 copy-done.1
  36.5 10.0 %observe.1 = (bf16[1024,512]{1,0:T(8,128)(2,1)}, bf16[1024,256]{1,0:T(8,128)(2,1)}, f32[16,1024]{1,0:T(8,128)}, bf16[32,256]{1,0:T(8,128)(2,1)}, bf16[32,256]{1,...) custom-call(bf16[1024,512]{1,0:T(8,128)(2,1)} %bitcast.13, ...), custom_call_target="tpu_custom_call" | custom-call | flops 4563402752 | bytes 2097152 | tf_op jit(solution)/shard_map/observe/pallas_call | solution.py:897
  46.5 0.0 copy-start.15
  46.5 0.0 copy-start.14
  46.5 0.0 copy-start.7
  46.5 0.0 copy-start.6
  46.5 6.1 %all-to-all-start.1 = ((bf16[128,8,512]{2,1,0:T(8,128)(2,1)}), bf16[128,8,512]{2,1,0:T(8,128)(2,1)S(1)}, u32[]{:S(2)}, u32[]{:S(2)}) async-start(bf16[128,8,512]{2,1,0:T(8,128)(2,1)} %bitcast.14), calls=%async_computation.1 | async-start | bytes 2097152 | tf_op jit(solution)/shard_map/all_to_all | solution.py:824
  52.6 0.0 copy-done.15
  52.6 1.6 %collective-permute-start.4 = (bf16[32,256]{1,0:T(8,128)(2,1)S(1)}, bf16[32,256]{1,0:T(8,128)(2,1)S(1)}, u32[]{:S(2)}, u32[]{:S(2)}) collective-permute-start(bf16[32,256]{1,0:T(8,128)(2,1)S(1)} %copy-done.15), channel_id=1, source_target_pairs={{0,1},{1,2},{2,3},{3,4},{4,5},{5,6},{6,7},{7,8},{8,9},{9,10},{10,1... | collective-permute-start | bytes 49160 | tf_op jit(solution)/shard_map/ppermute | solution.py:785
  54.2 0.0 copy-done.14
  54.2 4.2 %collective-permute-start.5 = (bf16[32,256]{1,0:T(8,128)(2,1)S(1)}, bf16[32,256]{1,0:T(8,128)(2,1)S(1)}, u32[]{:S(2)}, u32[]{:S(2)}) collective-permute-start(bf16[32,256]{1,0:T(8,128)(2,1)S(1)} %copy-done.14), channel_id=1, source_target_pairs={{1,0},{2,1},{3,2},{4,3},{5,4},{6,5},{7,6},{8,7},{9,8},{10,9},{11,1... | collective-permute-start | bytes 49160 | tf_op jit(solution)/shard_map/ppermute | solution.py:786
  58.4 0.0 copy-done.7
  58.4 3.6 %collective-permute-start.6 = (bf16[128,256]{1,0:T(8,128)(2,1)S(1)}, bf16[128,256]{1,0:T(8,128)(2,1)S(1)}, u32[]{:S(2)}, u32[]{:S(2)}) collective-permute-start(bf16[128,256]{1,0:T(8,128)(2,1)S(1)} %copy-done.7), channel_id=1, source_target_pairs={{0,16},{16,32},{32,48},{48,64},{64,80},{80,96},{96,112},{1,17},{17... | collective-permute-start | bytes 196616 | tf_op jit(solution)/shard_map/ppermute | solution.py:792
  62.0 0.0 copy-done.6
  62.0 1.9 %collective-permute-start.7 = (bf16[128,256]{1,0:T(8,128)(2,1)S(1)}, bf16[128,256]{1,0:T(8,128)(2,1)S(1)}, u32[]{:S(2)}, u32[]{:S(2)}) collective-permute-start(bf16[128,256]{1,0:T(8,128)(2,1)S(1)} %copy-done.6), channel_id=1, source_target_pairs={{16,0},{32,16},{48,32},{64,48},{80,64},{96,80},{112,96},{17,1},{33... | collective-permute-start | bytes 196616 | tf_op jit(solution)/shard_map/ppermute | solution.py:793
  63.9 10.4 %gradient.1 = f32[4096,256]{1,0:T(8,128)} custom-call(bf16[1024,256]{1,0:T(8,128)(2,1)} %get-tuple-element.26.adjoint_hbm, f32[16,1024]{1,0:T(8,128)} %get-tuple-element.27.fields_hbm, bf16[4096,256]{1,0:T(8,128)(2,1)} %bitcast.21, bf16[3,3,256,256]{3,2,1,0:T(8,128)(2,1)} %weight_hbm.5), custom_call_target="tpu_custom_call" | custom-call | flops 6979321856 | bytes 4194304 | tf_op jit(solution)/shard_map/gradient/pallas_call | solution.py:950
  74.4 0.0 collective-permute-done.4.left_hbm
  74.4 0.0 copy-start.4
  74.4 0.0 collective-permute-done.5.right_hbm
  74.4 0.0 copy-start.5
  74.4 0.0 collective-permute-done.6.north_hbm
  74.4 0.0 copy-start.2
  74.4 0.0 collective-permute-done.7.south_hbm
  74.4 0.0 copy-start.3
  74.4 0.0 all-to-all-done.1
  74.5 0.0 copy-start
  74.5 0.5 copy-done.4
  75.0 0.0 copy-done.5
  75.0 0.0 copy-done.2
  75.0 0.0 copy-done.3
  75.1 0.4 copy-done
  75.4 3.9 %finish.1 = (f32[32,128,256]{2,1,0:T(8,128)}, f32[512,384]{1,0:T(8,128)}) custom-call(f32[32,128,256]{2,1,0:T(8,128)} %bitcast.10, s32[1,512]{1,0:T(1,128)} %get-tuple-element.28.slot_hbm, bf16[1024,512]{1,0:T(8,128)(2,1)} %bitcast.11, bf16[3,3,256,256]{3,2,1,0:T(8,128)(2,1)} %weight_hbm.5, ...), custom_call_target="tpu_custom_call", output_to_operand_aliasing={{0}: (0, {})} | custom-call | flops 402653184 | bytes 786432 | tf_op jit(solution)/shard_map/finish/pallas_call | solution.py:971
Async XLA Ops:
  3.9 11.6 %copy-start.17 = (bf16[32,256]{1,0:T(8,128)(2,1)S(1)}, bf16[32,256]{1,0:T(8,128)(2,1)}, u32[]{:S(2)}) copy-start(bf16[32,256]{1,0:T(8,128)(2,1)} %get-tuple-element.22) | copy-start | bytes 49156
  3.9 13.1 %copy-start.16 = (bf16[32,256]{1,0:T(8,128)(2,1)S(1)}, bf16[32,256]{1,0:T(8,128)(2,1)}, u32[]{:S(2)}) copy-start(bf16[32,256]{1,0:T(8,128)(2,1)} %get-tuple-element.23) | copy-start | bytes 49156
  3.9 17.3 %copy-start.11 = (bf16[128,256]{1,0:T(8,128)(2,1)S(1)}, bf16[128,256]{1,0:T(8,128)(2,1)}, u32[]{:S(2)}) copy-start(bf16[128,256]{1,0:T(8,128)(2,1)} %get-tuple-element.24) | copy-start | bytes 196612
  4.0 20.9 %copy-start.9 = (bf16[128,256]{1,0:T(8,128)(2,1)S(1)}, bf16[128,256]{1,0:T(8,128)(2,1)}, u32[]{:S(2)}) copy-start(bf16[128,256]{1,0:T(8,128)(2,1)} %get-tuple-element.25) | copy-start | bytes 196612
  4.0 31.5 %all-to-all-start = ((bf16[128,8,512]{2,1,0:T(8,128)(2,1)}), bf16[128,8,512]{2,1,0:T(8,128)(2,1)S(1)}, u32[]{:S(2)}, u32[]{:S(2)}) async-start(bf16[128,8,512]{2,1,0:T(8,128)(2,1)} %bitcast.15), calls=%async_computation | async-start | bytes 2097152 | tf_op jit(solution)/shard_map/all_to_all | solution.py:824
  15.5 19.9 %collective-permute-start = (bf16[32,256]{1,0:T(8,128)(2,1)S(1)}, bf16[32,256]{1,0:T(8,128)(2,1)S(1)}, u32[]{:S(2)}, u32[]{:S(2)}) collective-permute-start(bf16[32,256]{1,0:T(8,128)(2,1)S(1)} %copy-done.17), channel_id=1, source_target_pairs={{0,1},{1,2},{2,3},{3,4},{4,5},{5,6},{6,7},{7,8},{8,9},{9,10},{10,1... | collective-permute-start | bytes 49160 | tf_op jit(solution)/shard_map/ppermute | solution.py:785
  17.1 18.4 %collective-permute-start.1 = (bf16[32,256]{1,0:T(8,128)(2,1)S(1)}, bf16[32,256]{1,0:T(8,128)(2,1)S(1)}, u32[]{:S(2)}, u32[]{:S(2)}) collective-permute-start(bf16[32,256]{1,0:T(8,128)(2,1)S(1)} %copy-done.16), channel_id=1, source_target_pairs={{1,0},{2,1},{3,2},{4,3},{5,4},{6,5},{7,6},{8,7},{9,8},{10,9},{11,1... | collective-permute-start | bytes 49160 | tf_op jit(solution)/shard_map/ppermute | solution.py:786
  21.2 14.2 %collective-permute-start.2 = (bf16[128,256]{1,0:T(8,128)(2,1)S(1)}, bf16[128,256]{1,0:T(8,128)(2,1)S(1)}, u32[]{:S(2)}, u32[]{:S(2)}) collective-permute-start(bf16[128,256]{1,0:T(8,128)(2,1)S(1)} %copy-done.11), channel_id=1, source_target_pairs={{0,16},{16,32},{32,48},{48,64},{64,80},{80,96},{96,112},{1,17},{17... | collective-permute-start | bytes 196616 | tf_op jit(solution)/shard_map/ppermute | solution.py:792
  24.9 10.6 %collective-permute-start.3 = (bf16[128,256]{1,0:T(8,128)(2,1)S(1)}, bf16[128,256]{1,0:T(8,128)(2,1)S(1)}, u32[]{:S(2)}, u32[]{:S(2)}) collective-permute-start(bf16[128,256]{1,0:T(8,128)(2,1)S(1)} %copy-done.9), channel_id=1, source_target_pairs={{16,0},{32,16},{48,32},{64,48},{80,64},{96,80},{112,96},{17,1},{33... | collective-permute-start | bytes 196616 | tf_op jit(solution)/shard_map/ppermute | solution.py:793
  35.4 0.6 copy-start.12
  35.4 0.6 copy-start.13
  35.5 0.6 copy-start.8
  35.5 0.6 copy-start.10
  35.5 1.0 %copy-start.1 = (bf16[128,8,512]{2,1,0:T(8,128)(2,1)}, bf16[128,8,512]{2,1,0:T(8,128)(2,1)S(1)}, u32[]{:S(2)}) copy-start(bf16[128,8,512]{2,1,0:T(8,128)(2,1)S(1)} %all-to-all-done) | copy-start | bytes 3145732
  46.5 6.2 %copy-start.15 = (bf16[32,256]{1,0:T(8,128)(2,1)S(1)}, bf16[32,256]{1,0:T(8,128)(2,1)}, u32[]{:S(2)}) copy-start(bf16[32,256]{1,0:T(8,128)(2,1)} %get-tuple-element.30) | copy-start | bytes 49156
  46.5 7.8 %copy-start.14 = (bf16[32,256]{1,0:T(8,128)(2,1)S(1)}, bf16[32,256]{1,0:T(8,128)(2,1)}, u32[]{:S(2)}) copy-start(bf16[32,256]{1,0:T(8,128)(2,1)} %get-tuple-element.31) | copy-start | bytes 49156
  46.5 11.9 %copy-start.7 = (bf16[128,256]{1,0:T(8,128)(2,1)S(1)}, bf16[128,256]{1,0:T(8,128)(2,1)}, u32[]{:S(2)}) copy-start(bf16[128,256]{1,0:T(8,128)(2,1)} %get-tuple-element.32) | copy-start | bytes 196612
  46.5 15.5 %copy-start.6 = (bf16[128,256]{1,0:T(8,128)(2,1)S(1)}, bf16[128,256]{1,0:T(8,128)(2,1)}, u32[]{:S(2)}) copy-start(bf16[128,256]{1,0:T(8,128)(2,1)} %get-tuple-element.33) | copy-start | bytes 196612
  46.5 28.0 %all-to-all-start.1 = ((bf16[128,8,512]{2,1,0:T(8,128)(2,1)}), bf16[128,8,512]{2,1,0:T(8,128)(2,1)S(1)}, u32[]{:S(2)}, u32[]{:S(2)}) async-start(bf16[128,8,512]{2,1,0:T(8,128)(2,1)} %bitcast.14), calls=%async_computation.1 | async-start | bytes 2097152 | tf_op jit(solution)/shard_map/all_to_all | solution.py:824
  52.6 21.7 %collective-permute-start.4 = (bf16[32,256]{1,0:T(8,128)(2,1)S(1)}, bf16[32,256]{1,0:T(8,128)(2,1)S(1)}, u32[]{:S(2)}, u32[]{:S(2)}) collective-permute-start(bf16[32,256]{1,0:T(8,128)(2,1)S(1)} %copy-done.15), channel_id=1, source_target_pairs={{0,1},{1,2},{2,3},{3,4},{4,5},{5,6},{6,7},{7,8},{8,9},{9,10},{10,1... | collective-permute-start | bytes 49160 | tf_op jit(solution)/shard_map/ppermute | solution.py:785
  54.2 20.2 %collective-permute-start.5 = (bf16[32,256]{1,0:T(8,128)(2,1)S(1)}, bf16[32,256]{1,0:T(8,128)(2,1)S(1)}, u32[]{:S(2)}, u32[]{:S(2)}) collective-permute-start(bf16[32,256]{1,0:T(8,128)(2,1)S(1)} %copy-done.14), channel_id=1, source_target_pairs={{1,0},{2,1},{3,2},{4,3},{5,4},{6,5},{7,6},{8,7},{9,8},{10,9},{11,1... | collective-permute-start | bytes 49160 | tf_op jit(solution)/shard_map/ppermute | solution.py:786
  58.4 16.0 %collective-permute-start.6 = (bf16[128,256]{1,0:T(8,128)(2,1)S(1)}, bf16[128,256]{1,0:T(8,128)(2,1)S(1)}, u32[]{:S(2)}, u32[]{:S(2)}) collective-permute-start(bf16[128,256]{1,0:T(8,128)(2,1)S(1)} %copy-done.7), channel_id=1, source_target_pairs={{0,16},{16,32},{32,48},{48,64},{64,80},{80,96},{96,112},{1,17},{17... | collective-permute-start | bytes 196616 | tf_op jit(solution)/shard_map/ppermute | solution.py:792
  62.0 12.4 %collective-permute-start.7 = (bf16[128,256]{1,0:T(8,128)(2,1)S(1)}, bf16[128,256]{1,0:T(8,128)(2,1)S(1)}, u32[]{:S(2)}, u32[]{:S(2)}) collective-permute-start(bf16[128,256]{1,0:T(8,128)(2,1)S(1)} %copy-done.6), channel_id=1, source_target_pairs={{16,0},{32,16},{48,32},{64,48},{80,64},{96,80},{112,96},{17,1},{33... | collective-permute-start | bytes 196616 | tf_op jit(solution)/shard_map/ppermute | solution.py:793
  74.4 0.6 copy-start.4
  74.4 0.6 copy-start.5
  74.4 0.6 copy-start.2
  74.4 0.6 copy-start.3
  74.5 1.0 %copy-start = (bf16[128,8,512]{2,1,0:T(8,128)(2,1)}, bf16[128,8,512]{2,1,0:T(8,128)(2,1)S(1)}, u32[]{:S(2)}) copy-start(bf16[128,8,512]{2,1,0:T(8,128)(2,1)S(1)} %all-to-all-done.1) | copy-start | bytes 3145732

commit v4 on v3

--- a/solution.py
+++ b/solution.py
@@ -178,7 +178,6 @@
     for index, field in enumerate(fields):
         meta = jnp.where(number == index, field, meta)
     meta = meta.astype(BF16)
-    waiting[3].wait()
     for copy in waiting[4:]:
         copy.wait()
     for index, line_hbm in enumerate((top_hbm, bottom_hbm)):
@@ -199,15 +198,23 @@
         )
         leaving[-1].start()
     cells = (cells[0], cells[2], cells[1], cells[3])
-    step = slots // 4
-    for index in range(4):
+    places = []
+    step = slots // 2
+    for index in range(2):
         part = slice(index * step, (index + 1) * step)
-        place = (iota((step, count), 0) + index * step == slot).astype(F32).astype(BF16)
-        box_ref[part, channels:] = dot_nt(place, meta).astype(BF16)
-        box_ref[part, :channels] = dot_nn(place, radiance_ref[...]).astype(BF16)
+        places.append((iota((step, count), 0) + index * step == slot).astype(F32).astype(BF16))
+        box_ref[part, channels:] = dot_nt(places[index], meta).astype(BF16)
     corners_out(cells, lat, lon, capacity, box_ref, channels)
-    leaving.append(pltpu.make_async_copy(box_ref, box_hbm, out_semaphores.at[len(leaving)]))
-    leaving[-1].start()
+    waiting[3].wait()
+    for index in range(2):
+        part = slice(index * step, (index + 1) * step)
+        box_ref[part, :channels] = dot_nn(places[index], radiance_ref[...]).astype(BF16)
+        leaving.append(
+            pltpu.make_async_copy(
+                box_ref.at[part, :], box_hbm.at[part, :], out_semaphores.at[len(leaving)]
+            )
+        )
+        leaving[-1].start()
     for copy in leaving:
         copy.wait()
 
@@ -236,6 +243,9 @@
 
 def halo_terms(left, right, north, south, corners, weight_ref, mirror):
     rows, columns = left.shape[0], north.shape[0]
+    lat = lax.axis_index("lat")
+    north = jnp.where(lat > 0, north, 0.0)
+    south = jnp.where(lat < lax.axis_size("lat") - 1, south, 0.0)
     product, weight_of = taps(weight_ref, mirror)
 
     def row_windows(center, first, last):
@@ -391,43 +401,24 @@
 
 def gradient_kernel(
     columns,
-    adjoint_hbm,
-    fields_hbm,
-    slope_hbm,
-    weight_hbm,
-    out_hbm,
     adjoint,
     fields_ref,
     slope_ref,
     weight_ref,
+    out_hbm,
     out_ref,
     shifted,
-    semaphores,
-    slope_semaphores,
     out_semaphores,
 ):
     cells, channels = slope_ref.shape
     rows = cells // columns
     per = CHUNK // columns
     steps = cells // CHUNK
-    waiting = copies(semaphores, (fields_hbm, fields_ref), (adjoint_hbm, adjoint))
     zero = jnp.zeros((1, channels), F32)
     groups = list(zip(GRADIENT_GROUPS[:-1], GRADIENT_GROUPS[1:]))
 
-    def copies_in(number):
-        first, last = groups[number]
-        ahead = (first + 1 if number else 0), min(last + 1, steps)
-        if ahead[0] == ahead[1]:
-            return []
-        return [span_copy(slope_hbm, slope_ref, slope_semaphores.at[number], *ahead)]
-
-    coming = copies_in(0) + [pltpu.make_async_copy(weight_hbm, weight_ref, semaphores.at[2])]
-    for copy in coming:
-        copy.start()
     no_halo_rows(shifted, rows, columns)
-    waiting[0].wait()
     around = turned_weights(fields_ref[...], columns)
-    waiting[1].wait()
 
     def spread(index):
         weights = [blend(*around, index * per + row) for row in range(per)]
@@ -446,12 +437,6 @@
         spread(index)
     out = []
     for number, (low, high) in enumerate(groups):
-        for copy in coming:
-            copy.wait()
-        if number + 1 < len(groups):
-            coming = copies_in(number + 1)
-            for copy in coming:
-                copy.start()
         if number == 0:
             fill(0)
         for index in range(low, high):
@@ -469,7 +454,7 @@
     capacity,
     gradient_hbm,
     slot_hbm,
-    box_hbm,
+    box_ref,
     weight_hbm,
     left_hbm,
     right_hbm,
@@ -478,7 +463,6 @@
     out_hbm,
     departures_hbm,
     slot_ref,
-    box_ref,
     weight_ref,
     left_ref,
     right_ref,
@@ -503,7 +487,6 @@
     waiting = copies(
         semaphores,
         (slot_hbm, slot_ref),
-        (box_hbm, box_ref),
         (weight_hbm, weight_ref),
         (left_hbm, left_ref),
         (right_hbm, right_ref),
@@ -521,7 +504,6 @@
         (lane + float(first) == turned).astype(F32).astype(BF16) for first in range(0, slots, 128)
     ]
     place = jnp.concatenate(parts, axis=1)
-    waiting[1].wait()
     step = count // 2
     leaving = []
     for index in range(2):
@@ -533,7 +515,7 @@
             )
         )
         leaving[-1].start()
-    for copy in waiting[2:]:
+    for copy in waiting[1:]:
         copy.wait()
     top, bottom, west, east = halo_terms(
         left_ref[...].astype(F32),
@@ -788,7 +770,8 @@
 
 
 def over(top, bottom):
-    down = [(i, i + 1) for i in range(lax.axis_size("lat") - 1)]
+    count = lax.axis_size("lat")
+    down = [(i, (i + 1) % count) for i in range(count)]
     north = lax.ppermute(bottom, "lat", down)
     south = lax.ppermute(top, "lat", [(target, source) for source, target in down])
     return north, south
@@ -850,7 +833,7 @@
             pltpu.VMEM((rows, channels), BF16),
             pltpu.VMEM((2, columns, channels), BF16),
             dma((8,)),
-            dma((6,)),
+            dma((7,)),
         ),
         flops=2 * slots * count * (bands + META),
         moved=2 * slots * (bands + META),
@@ -951,31 +934,24 @@
         functools.partial(gradient_kernel, columns),
         (sds((cells, channels), F32),),
         (HBM,),
-        (HBM,) * 4,
+        (VMEM,) * 4,
         (
-            pltpu.VMEM((slots, channels), BF16),
-            pltpu.VMEM((16, slots), F32),
-            pltpu.VMEM((cells, channels), BF16),
-            pltpu.VMEM(conv_weight.shape, BF16),
             pltpu.VMEM((cells, channels), F32),
             shifted,
-            dma((3,)),
-            dma((steps,)),
             dma((steps,)),
         ),
         flops=conv_flops + 2 * slots * cells * channels,
         moved=4 * cells * channels,
-        room=400,
+        room=30720,
         name="gradient",
     )(adjoint, fields, flat_slope, conv_weight)
     gradient, departures = kernel_call(
         functools.partial(finish_kernel, capacity),
         (sds((rows, columns, channels), F32), sds((count, bands), F32)),
         (HBM, HBM),
-        (HBM,) * 8,
+        (HBM, HBM, VMEM) + (HBM,) * 5,
         (
             pltpu.VMEM((1, count), jnp.int32),
-            pltpu.VMEM((slots, bands + META), BF16),
             pltpu.VMEM(conv_weight.shape, BF16),
             *halo_scratch,
             pltpu.VMEM((2, columns - 16, channels), F32),
@@ -987,7 +963,7 @@
         flops=2 * slots * count * bands,
         moved=4 * count * bands,
         aliases={0: 0},
-        room=1024 + 192,
+        room=30720,
         name="finish",
     )(gradient.reshape(rows, columns, channels), slot, returned, conv_weight, *halo)
     return departures, gradient

time: 79.9 us -> 73.5 us (0.920)
  starting transfers between devices: 40.4 us -> 31.8 us
  waiting for transfers between devices: 0.03 us -> 3.85 us
  Pallas kernels: 36 us -> 33.7 us
    ppermute x2, starting transfers between devices: 4.02 us -> 0.01 us  [over(): lax.ppermute(top, 'lat', [(target, source) for source, target in down])]
    all_to_all x2, waiting for transfers between devices: 0.01 us -> 3.83 us  [exchange(): lax.all_to_all(box.reshape(devices, capacity, -1), ('lat', 'lon'), split_...]
    ppermute x2, starting transfers between devices: 7.25 us -> 3.45 us  [over(): north = lax.ppermute(bottom, 'lat', down)]
    pallas_call x1, Pallas kernels: 10.4 us -> 8.67 us  [body(): kernel_call(functools.partial(gradient_kernel, columns), (sds((cells, cha...]
    all_to_all x2, starting transfers between devices: 17.6 us -> 16.6 us  [exchange(): lax.all_to_all(box.reshape(devices, capacity, -1), ('lat', 'lon'), split_...]
  transfers between devices with their start and end apart: 10 -> 10, of which waited for: 0 -> 2; matrix products, arithmetic and copies ran while one was open for 0% -> 0% of each run, Pallas kernels for 24% -> 23%
where the time goes in v4:
time: 73.5 us; the launch traced here: 73.1 us
  Pallas kernels  33.7 us (46%)
  starting transfers between devices  31.8 us (43%)
  waiting for transfers between devices  3.85 us (5%)
  local copies, waits for them, and re-layouts  2.61 us (4%)
  between operations  1.11 us (2%)
    all_to_all x2, starting transfers between devices, exchange(): lax.all_to_all(box.reshape(devices, capacity, -1), ('lat', 'lon'), split_...  16.6 us
    pallas_call x1, Pallas kernels, body(): kernel_call(functools.partial(observe_kernel, columns, capacity), (sds((s...  9.99 us
    pallas_call x1, Pallas kernels, body(): kernel_call(functools.partial(gradient_kernel, columns), (sds((cells, cha...  8.67 us
    ppermute x2, starting transfers between devices, beside(): lax.ppermute(west, 'lon', [(target, source) for source, target in onward])  8.48 us
    pallas_call x1, Pallas kernels, body(): kernel_call(functools.partial(forecast_kernel, columns), (sds((cells, cha...  8.44 us
    all_to_all x2, waiting for transfers between devices, exchange(): lax.all_to_all(box.reshape(devices, capacity, -1), ('lat', 'lon'), split_...  3.83 us
    ppermute x2, starting transfers between devices, over(): north = lax.ppermute(bottom, 'lat', down)  3.45 us
    pallas_call x1, Pallas kernels, body(): kernel_call(functools.partial(finish_kernel, capacity), (sds((rows, colum...  3.32 us
  transfers between devices with their start and end apart: 10, of which 2 were waited for; matrix products, arithmetic and copies ran while one was open for 0% of the time, Pallas kernels for 23%

profile of v4, /device:TPU:1, one launch (start us, length us, event | category | flops | bytes accessed | tf_op | source)
XLA Modules:
  0.0 73.1 jit_solution(16788792481482958219)
XLA Ops:
  0.6 3.3 %dispatch.1 = (bf16[1024,512]{1,0:T(8,128)(2,1)}, s32[1,512]{1,0:T(1,128)}, bf16[32,256]{1,0:T(8,128)(2,1)}, bf16[32,256]{1,0:T(8,128)(2,1)}, bf16[128,256]{1,0:T(8,128)(2,1)}, /*index=5*/bf16[128,256]{1,0:T(8,128)(2,1)}) custom-call(s32[1,512]{1,0:T(1,128)} %bitcast.20, s32[1,512]{1,0:T(1,128)} %bitcast.21, f32[2,512]{1,0:T(2,128)} %bitcast.19, ...), custom_call_target="tpu_custom_call" | custom-call | flops 536870912 | bytes 1048576 | tf_op jit(solution)/shard_map/dispatch/pallas_call | solution.py:811
  3.9 0.0 copy-start.17
  3.9 0.0 copy-start.16
  4.0 0.0 copy-start.11
  4.0 0.0 copy-start.9
  4.0 11.5 %all-to-all-start = ((bf16[128,8,512]{2,1,0:T(8,128)(2,1)}), bf16[128,8,512]{2,1,0:T(8,128)(2,1)S(1)}, u32[]{:S(2)}, u32[]{:S(2)}) async-start(bf16[128,8,512]{2,1,0:T(8,128)(2,1)} %bitcast.18), calls=%async_computation | async-start | bytes 2097152 | tf_op jit(solution)/shard_map/all_to_all | solution.py:807
  15.5 0.0 copy-done.17
  15.5 1.6 %collective-permute-start = (bf16[32,256]{1,0:T(8,128)(2,1)S(1)}, bf16[32,256]{1,0:T(8,128)(2,1)S(1)}, u32[]{:S(2)}, u32[]{:S(2)}) collective-permute-start(bf16[32,256]{1,0:T(8,128)(2,1)S(1)} %copy-done.17), channel_id=1, source_target_pairs={{0,1},{1,2},{2,3},{3,4},{4,5},{5,6},{6,7},{7,8},{8,9},{9,10},{10,1... | collective-permute-start | bytes 49160 | tf_op jit(solution)/shard_map/ppermute | solution.py:767
  17.1 0.0 copy-done.16
  17.1 4.3 %collective-permute-start.1 = (bf16[32,256]{1,0:T(8,128)(2,1)S(1)}, bf16[32,256]{1,0:T(8,128)(2,1)S(1)}, u32[]{:S(2)}, u32[]{:S(2)}) collective-permute-start(bf16[32,256]{1,0:T(8,128)(2,1)S(1)} %copy-done.16), channel_id=1, source_target_pairs={{1,0},{2,1},{3,2},{4,3},{5,4},{6,5},{7,6},{8,7},{9,8},{10,9},{11,1... | collective-permute-start | bytes 49160 | tf_op jit(solution)/shard_map/ppermute | solution.py:768
  21.4 0.0 copy-done.11
  21.4 1.7 %collective-permute-start.2 = (bf16[128,256]{1,0:T(8,128)(2,1)S(1)}, bf16[128,256]{1,0:T(8,128)(2,1)S(1)}, u32[]{:S(2)}, u32[]{:S(2)}) collective-permute-start(bf16[128,256]{1,0:T(8,128)(2,1)S(1)} %copy-done.11), channel_id=1, source_target_pairs={{0,16},{16,32},{32,48},{48,64},{64,80},{80,96},{96,112},{112,0},{1... | collective-permute-start | bytes 196616 | tf_op jit(solution)/shard_map/ppermute | solution.py:775
  23.1 0.0 copy-done.9
  23.1 0.0 collective-permute-start.3
  23.1 8.4 %forecast.1 = (bf16[4096,256]{1,0:T(8,128)(2,1)}, f32[384,256]{1,0:T(8,128)}) custom-call(bf16[4096,256]{1,0:T(8,128)(2,1)} %bitcast.15, bf16[4096,256]{1,0:T(8,128)(2,1)} %bitcast.11, bf16[3,3,256,256]{3,2,1,0:T(8,128)(2,1)} %weight_hbm.3), custom_call_target="tpu_custom_call" | custom-call | flops 4831838208 | bytes 6291456 | tf_op jit(solution)/shard_map/forecast/pallas_call | solution.py:856
  31.6 0.0 collective-permute-done.left_hbm
  31.6 0.0 copy-start.12
  31.6 0.0 collective-permute-done.1.right_hbm
  31.6 0.0 copy-start.13
  31.6 0.0 collective-permute-done.2.north_hbm
  31.6 0.0 copy-start.8
  31.6 0.0 collective-permute-done.3.south_hbm
  31.7 0.0 copy-start.10
  31.7 2.7 %all-to-all-done = bf16[128,8,512]{2,1,0:T(8,128)(2,1)S(1)} async-done(((bf16[128,8,512]{2,1,0:T(8,128)(2,1)}), bf16[128,8,512]{2,1,0:T(8,128)(2,1)S(1)}, u32[]{:S(2)}, u32[]{:S(2)}) %all-to-all-start) | async-done | bytes 1048608 | tf_op jit(solution)/shard_map/all_to_all | solution.py:807
  34.4 0.0 copy-start.5
  34.4 0.0 copy-done.12
  34.4 0.0 copy-done.13
  34.4 0.0 copy-done.8
  34.4 0.0 copy-done.10
  34.4 1.0 %copy-done.5 = bf16[128,8,512]{2,1,0:T(8,128)(2,1)} copy-done((bf16[128,8,512]{2,1,0:T(8,128)(2,1)}, bf16[128,8,512]{2,1,0:T(8,128)(2,1)S(1)}, u32[]{:S(2)}) %copy-start.5) | copy-done | bytes 1048600
  35.4 10.0 %observe.1 = (bf16[1024,512]{1,0:T(8,128)(2,1)}, bf16[1024,256]{1,0:T(8,128)(2,1)}, f32[16,1024]{1,0:T(8,128)}, bf16[32,256]{1,0:T(8,128)(2,1)}, bf16[32,256]{1,...) custom-call(bf16[1024,512]{1,0:T(8,128)(2,1)} %bitcast.16, ...), custom_call_target="tpu_custom_call" | custom-call | flops 4563402752 | bytes 2097152 | tf_op jit(solution)/shard_map/observe/pallas_call | solution.py:880
  45.4 0.0 copy-start.15
  45.4 0.0 copy-start.14
  45.4 0.0 copy-start.7
  45.4 0.0 copy-start.6
  45.4 0.0 copy-start
  45.4 0.0 copy-start.3
  45.4 0.0 copy-start.4
  45.4 5.1 %all-to-all-start.1 = ((bf16[128,8,512]{2,1,0:T(8,128)(2,1)}), bf16[128,8,512]{2,1,0:T(8,128)(2,1)S(1)}, u32[]{:S(2)}, u32[]{:S(2)}) async-start(bf16[128,8,512]{2,1,0:T(8,128)(2,1)} %bitcast.17), calls=%async_computation.1 | async-start | bytes 2097152 | tf_op jit(solution)/shard_map/all_to_all | solution.py:807
  50.6 0.0 copy-done.15
  50.6 1.7 %collective-permute-start.4 = (bf16[32,256]{1,0:T(8,128)(2,1)S(1)}, bf16[32,256]{1,0:T(8,128)(2,1)S(1)}, u32[]{:S(2)}, u32[]{:S(2)}) collective-permute-start(bf16[32,256]{1,0:T(8,128)(2,1)S(1)} %copy-done.15), channel_id=1, source_target_pairs={{0,1},{1,2},{2,3},{3,4},{4,5},{5,6},{6,7},{7,8},{8,9},{9,10},{10,1... | collective-permute-start | bytes 49160 | tf_op jit(solution)/shard_map/ppermute | solution.py:767
  52.3 0.0 copy-done.14
  52.3 4.2 %collective-permute-start.5 = (bf16[32,256]{1,0:T(8,128)(2,1)S(1)}, bf16[32,256]{1,0:T(8,128)(2,1)S(1)}, u32[]{:S(2)}, u32[]{:S(2)}) collective-permute-start(bf16[32,256]{1,0:T(8,128)(2,1)S(1)} %copy-done.14), channel_id=1, source_target_pairs={{1,0},{2,1},{3,2},{4,3},{5,4},{6,5},{7,6},{8,7},{9,8},{10,9},{11,1... | collective-permute-start | bytes 49160 | tf_op jit(solution)/shard_map/ppermute | solution.py:768
  56.4 0.0 copy-done.7
  56.4 1.7 %collective-permute-start.6 = (bf16[128,256]{1,0:T(8,128)(2,1)S(1)}, bf16[128,256]{1,0:T(8,128)(2,1)S(1)}, u32[]{:S(2)}, u32[]{:S(2)}) collective-permute-start(bf16[128,256]{1,0:T(8,128)(2,1)S(1)} %copy-done.7), channel_id=1, source_target_pairs={{0,16},{16,32},{32,48},{48,64},{64,80},{80,96},{96,112},{112,0},{1... | collective-permute-start | bytes 196616 | tf_op jit(solution)/shard_map/ppermute | solution.py:775
  58.2 0.0 copy-done.6
  58.2 0.0 collective-permute-start.7
  58.2 0.0 copy-done
  58.2 0.0 copy-done.3
  58.2 0.0 copy-done.4
  58.2 0.0 copy-start.2
  58.2 1.6 %copy-done.2 = bf16[32,128,256]{2,1,0:T(8,128)(2,1)S(1)} copy-done((bf16[32,128,256]{2,1,0:T(8,128)(2,1)S(1)}, bf16[32,128,256]{2,1,0:T(8,128)(2,1)}, u32[]{:S(2)}) %copy-start.2) | copy-done | bytes 2097176
  59.8 0.0 copy-start.1
  59.8 8.7 %gradient.1 = f32[4096,256]{1,0:T(8,128)} custom-call(bf16[1024,256]{1,0:T(8,128)(2,1)S(1)} %copy-done.3, f32[16,1024]{1,0:T(8,128)S(1)} %copy-done.4, bf16[4096,256]{1,0:T(8,128)(2,1)S(1)} %bitcast.13, bf16[3,3,256,256]{3,2,1,0:T(8,128)(2,1)S(1)} %copy-done), custom_call_target="tpu_custom_call" | custom-call | flops 6979321856 | bytes 4194304 | tf_op jit(solution)/shard_map/gradient/pallas_call | solution.py:933
  68.5 0.0 collective-permute-done.4.left_hbm
  68.5 0.0 collective-permute-done.5.right_hbm
  68.5 0.0 collective-permute-done.6.north_hbm
  68.5 0.0 collective-permute-done.7.south_hbm
  68.5 1.1 %all-to-all-done.1 = bf16[128,8,512]{2,1,0:T(8,128)(2,1)S(1)} async-done(((bf16[128,8,512]{2,1,0:T(8,128)(2,1)}), bf16[128,8,512]{2,1,0:T(8,128)(2,1)S(1)}, u32[]{:S(2)}, u32[]{:S(2)}) %all-to-all-start.1) | async-done | bytes 1048608 | tf_op jit(solution)/shard_map/all_to_all | solution.py:807
  69.6 0.0 copy-done.1
  69.6 3.3 %finish.1 = (f32[32,128,256]{2,1,0:T(8,128)}, f32[512,384]{1,0:T(8,128)}) custom-call(f32[32,128,256]{2,1,0:T(8,128)} %bitcast.14, s32[1,512]{1,0:T(1,128)S(1)} %copy-done.1, bf16[1024,512]{1,0:T(8,128)(2,1)S(1)} %bitcast.10, bf16[3,3,256,256]{3,2,1,0:T(8,128)(2,1)S(1)} %copy-done, ...), custom_call_target="tpu_custom_call", output_to_operand_aliasing={{0}: (0, {})} | custom-call | flops 402653184 | bytes 786432 | tf_op jit(solution)/shard_map/finish/pallas_call | solution.py:948
Async XLA Ops:
  3.9 11.6 %copy-start.17 = (bf16[32,256]{1,0:T(8,128)(2,1)S(1)}, bf16[32,256]{1,0:T(8,128)(2,1)}, u32[]{:S(2)}) copy-start(bf16[32,256]{1,0:T(8,128)(2,1)} %get-tuple-element.22) | copy-start | bytes 49156
  3.9 13.1 %copy-start.16 = (bf16[32,256]{1,0:T(8,128)(2,1)S(1)}, bf16[32,256]{1,0:T(8,128)(2,1)}, u32[]{:S(2)}) copy-start(bf16[32,256]{1,0:T(8,128)(2,1)} %get-tuple-element.23) | copy-start | bytes 49156
  4.0 17.5 %copy-start.11 = (bf16[128,256]{1,0:T(8,128)(2,1)S(1)}, bf16[128,256]{1,0:T(8,128)(2,1)}, u32[]{:S(2)}) copy-start(bf16[128,256]{1,0:T(8,128)(2,1)} %get-tuple-element.24) | copy-start | bytes 196612
  4.0 19.2 %copy-start.9 = (bf16[128,256]{1,0:T(8,128)(2,1)S(1)}, bf16[128,256]{1,0:T(8,128)(2,1)}, u32[]{:S(2)}) copy-start(bf16[128,256]{1,0:T(8,128)(2,1)} %get-tuple-element.25) | copy-start | bytes 196612
  4.0 30.4 %all-to-all-start = ((bf16[128,8,512]{2,1,0:T(8,128)(2,1)}), bf16[128,8,512]{2,1,0:T(8,128)(2,1)S(1)}, u32[]{:S(2)}, u32[]{:S(2)}) async-start(bf16[128,8,512]{2,1,0:T(8,128)(2,1)} %bitcast.18), calls=%async_computation | async-start | bytes 2097152 | tf_op jit(solution)/shard_map/all_to_all | solution.py:807
  15.5 16.1 %collective-permute-start = (bf16[32,256]{1,0:T(8,128)(2,1)S(1)}, bf16[32,256]{1,0:T(8,128)(2,1)S(1)}, u32[]{:S(2)}, u32[]{:S(2)}) collective-permute-start(bf16[32,256]{1,0:T(8,128)(2,1)S(1)} %copy-done.17), channel_id=1, source_target_pairs={{0,1},{1,2},{2,3},{3,4},{4,5},{5,6},{6,7},{7,8},{8,9},{9,10},{10,1... | collective-permute-start | bytes 49160 | tf_op jit(solution)/shard_map/ppermute | solution.py:767
  17.1 14.5 %collective-permute-start.1 = (bf16[32,256]{1,0:T(8,128)(2,1)S(1)}, bf16[32,256]{1,0:T(8,128)(2,1)S(1)}, u32[]{:S(2)}, u32[]{:S(2)}) collective-permute-start(bf16[32,256]{1,0:T(8,128)(2,1)S(1)} %copy-done.16), channel_id=1, source_target_pairs={{1,0},{2,1},{3,2},{4,3},{5,4},{6,5},{7,6},{8,7},{9,8},{10,9},{11,1... | collective-permute-start | bytes 49160 | tf_op jit(solution)/shard_map/ppermute | solution.py:768
  21.4 10.2 %collective-permute-start.2 = (bf16[128,256]{1,0:T(8,128)(2,1)S(1)}, bf16[128,256]{1,0:T(8,128)(2,1)S(1)}, u32[]{:S(2)}, u32[]{:S(2)}) collective-permute-start(bf16[128,256]{1,0:T(8,128)(2,1)S(1)} %copy-done.11), channel_id=1, source_target_pairs={{0,16},{16,32},{32,48},{48,64},{64,80},{80,96},{96,112},{112,0},{1... | collective-permute-start | bytes 196616 | tf_op jit(solution)/shard_map/ppermute | solution.py:775
  23.1 8.5 %collective-permute-start.3 = (bf16[128,256]{1,0:T(8,128)(2,1)S(1)}, bf16[128,256]{1,0:T(8,128)(2,1)S(1)}, u32[]{:S(2)}, u32[]{:S(2)}) collective-permute-start(bf16[128,256]{1,0:T(8,128)(2,1)S(1)} %copy-done.9), channel_id=1, source_target_pairs={{16,0},{32,16},{48,32},{64,48},{80,64},{96,80},{112,96},{0,112},{1... | collective-permute-start | bytes 196616 | tf_op jit(solution)/shard_map/ppermute | solution.py:776
  31.6 2.8 %copy-start.12 = (bf16[32,256]{1,0:T(8,128)(2,1)}, bf16[32,256]{1,0:T(8,128)(2,1)S(1)}, u32[]{:S(2)}) copy-start(bf16[32,256]{1,0:T(8,128)(2,1)S(1)} %collective-permute-done.left_hbm) | copy-start | bytes 49156
  31.6 2.8 %copy-start.13 = (bf16[32,256]{1,0:T(8,128)(2,1)}, bf16[32,256]{1,0:T(8,128)(2,1)S(1)}, u32[]{:S(2)}) copy-start(bf16[32,256]{1,0:T(8,128)(2,1)S(1)} %collective-permute-done.1.right_hbm) | copy-start | bytes 49156
  31.6 2.8 %copy-start.8 = (bf16[128,256]{1,0:T(8,128)(2,1)}, bf16[128,256]{1,0:T(8,128)(2,1)S(1)}, u32[]{:S(2)}) copy-start(bf16[128,256]{1,0:T(8,128)(2,1)S(1)} %collective-permute-done.2.north_hbm) | copy-start | bytes 196612
  31.7 2.8 %copy-start.10 = (bf16[128,256]{1,0:T(8,128)(2,1)}, bf16[128,256]{1,0:T(8,128)(2,1)S(1)}, u32[]{:S(2)}) copy-start(bf16[128,256]{1,0:T(8,128)(2,1)S(1)} %collective-permute-done.3.south_hbm) | copy-start | bytes 196612
  34.4 1.0 %copy-start.5 = (bf16[128,8,512]{2,1,0:T(8,128)(2,1)}, bf16[128,8,512]{2,1,0:T(8,128)(2,1)S(1)}, u32[]{:S(2)}) copy-start(bf16[128,8,512]{2,1,0:T(8,128)(2,1)S(1)} %all-to-all-done) | copy-start | bytes 3145732
  45.4 5.2 %copy-start.15 = (bf16[32,256]{1,0:T(8,128)(2,1)S(1)}, bf16[32,256]{1,0:T(8,128)(2,1)}, u32[]{:S(2)}) copy-start(bf16[32,256]{1,0:T(8,128)(2,1)} %get-tuple-element.30) | copy-start | bytes 49156
  45.4 6.9 %copy-start.14 = (bf16[32,256]{1,0:T(8,128)(2,1)S(1)}, bf16[32,256]{1,0:T(8,128)(2,1)}, u32[]{:S(2)}) copy-start(bf16[32,256]{1,0:T(8,128)(2,1)} %get-tuple-element.31) | copy-start | bytes 49156
  45.4 11.1 %copy-start.7 = (bf16[128,256]{1,0:T(8,128)(2,1)S(1)}, bf16[128,256]{1,0:T(8,128)(2,1)}, u32[]{:S(2)}) copy-start(bf16[128,256]{1,0:T(8,128)(2,1)} %get-tuple-element.32) | copy-start | bytes 196612
  45.4 12.8 %copy-start.6 = (bf16[128,256]{1,0:T(8,128)(2,1)S(1)}, bf16[128,256]{1,0:T(8,128)(2,1)}, u32[]{:S(2)}) copy-start(bf16[128,256]{1,0:T(8,128)(2,1)} %get-tuple-element.33) | copy-start | bytes 196612
  45.4 12.8 %copy-start = (bf16[3,3,256,256]{3,2,1,0:T(8,128)(2,1)S(1)}, bf16[3,3,256,256]{3,2,1,0:T(8,128)(2,1)}, u32[]{:S(2)}) copy-start(bf16[3,3,256,256]{3,2,1,0:T(8,128)(2,1)} %weight_hbm.3) | copy-start | bytes 3538948
  45.4 12.8 %copy-start.3 = (bf16[1024,256]{1,0:T(8,128)(2,1)S(1)}, bf16[1024,256]{1,0:T(8,128)(2,1)}, u32[]{:S(2)}) copy-start(bf16[1024,256]{1,0:T(8,128)(2,1)} %get-tuple-element.26.adjoint) | copy-start | bytes 1572868
  45.4 12.8 %copy-start.4 = (f32[16,1024]{1,0:T(8,128)S(1)}, f32[16,1024]{1,0:T(8,128)}, u32[]{:S(2)}) copy-start(f32[16,1024]{1,0:T(8,128)} %get-tuple-element.27.fields_ref) | copy-start | bytes 196612
  45.4 24.2 %all-to-all-start.1 = ((bf16[128,8,512]{2,1,0:T(8,128)(2,1)}), bf16[128,8,512]{2,1,0:T(8,128)(2,1)S(1)}, u32[]{:S(2)}, u32[]{:S(2)}) async-start(bf16[128,8,512]{2,1,0:T(8,128)(2,1)} %bitcast.17), calls=%async_computation.1 | async-start | bytes 2097152 | tf_op jit(solution)/shard_map/all_to_all | solution.py:807
  50.6 17.9 %collective-permute-start.4 = (bf16[32,256]{1,0:T(8,128)(2,1)S(1)}, bf16[32,256]{1,0:T(8,128)(2,1)S(1)}, u32[]{:S(2)}, u32[]{:S(2)}) collective-permute-start(bf16[32,256]{1,0:T(8,128)(2,1)S(1)} %copy-done.15), channel_id=1, source_target_pairs={{0,1},{1,2},{2,3},{3,4},{4,5},{5,6},{6,7},{7,8},{8,9},{9,10},{10,1... | collective-permute-start | bytes 49160 | tf_op jit(solution)/shard_map/ppermute | solution.py:767
  52.3 16.2 %collective-permute-start.5 = (bf16[32,256]{1,0:T(8,128)(2,1)S(1)}, bf16[32,256]{1,0:T(8,128)(2,1)S(1)}, u32[]{:S(2)}, u32[]{:S(2)}) collective-permute-start(bf16[32,256]{1,0:T(8,128)(2,1)S(1)} %copy-done.14), channel_id=1, source_target_pairs={{1,0},{2,1},{3,2},{4,3},{5,4},{6,5},{7,6},{8,7},{9,8},{10,9},{11,1... | collective-permute-start | bytes 49160 | tf_op jit(solution)/shard_map/ppermute | solution.py:768
  56.4 12.1 %collective-permute-start.6 = (bf16[128,256]{1,0:T(8,128)(2,1)S(1)}, bf16[128,256]{1,0:T(8,128)(2,1)S(1)}, u32[]{:S(2)}, u32[]{:S(2)}) collective-permute-start(bf16[128,256]{1,0:T(8,128)(2,1)S(1)} %copy-done.7), channel_id=1, source_target_pairs={{0,16},{16,32},{32,48},{48,64},{64,80},{80,96},{96,112},{112,0},{1... | collective-permute-start | bytes 196616 | tf_op jit(solution)/shard_map/ppermute | solution.py:775
  58.2 10.3 %collective-permute-start.7 = (bf16[128,256]{1,0:T(8,128)(2,1)S(1)}, bf16[128,256]{1,0:T(8,128)(2,1)S(1)}, u32[]{:S(2)}, u32[]{:S(2)}) collective-permute-start(bf16[128,256]{1,0:T(8,128)(2,1)S(1)} %copy-done.6), channel_id=1, source_target_pairs={{16,0},{32,16},{48,32},{64,48},{80,64},{96,80},{112,96},{0,112},{1... | collective-permute-start | bytes 196616 | tf_op jit(solution)/shard_map/ppermute | solution.py:776
  58.2 1.6 %copy-start.2 = (bf16[32,128,256]{2,1,0:T(8,128)(2,1)S(1)}, bf16[32,128,256]{2,1,0:T(8,128)(2,1)}, u32[]{:S(2)}) copy-start(bf16[32,128,256]{2,1,0:T(8,128)(2,1)} %param.15) | copy-start | bytes 6291460
  59.8 9.8 %copy-start.1 = (s32[1,512]{1,0:T(1,128)S(1)}, s32[1,512]{1,0:T(1,128)}, u32[]{:S(2)}) copy-start(s32[1,512]{1,0:T(1,128)} %get-tuple-element.28.slot_hbm) | copy-start | bytes 6148

commit v5 on v4

--- a/solution.py
+++ b/solution.py
@@ -222,6 +222,7 @@
 CHUNK = 512
 FORECAST_GROUPS = (0, 2, 6, 8)
 GRADIENT_GROUPS = (0, 4, 8)
+SPREAD_AHEAD = 6
 
 
 def fill_row(shifted, row, center, left, right):
@@ -403,11 +404,13 @@
     columns,
     adjoint,
     fields_ref,
-    slope_ref,
+    slope_hbm,
     weight_ref,
     out_hbm,
+    slope_ref,
     out_ref,
     shifted,
+    slope_semaphore,
     out_semaphores,
 ):
     cells, channels = slope_ref.shape
@@ -417,6 +420,7 @@
     zero = jnp.zeros((1, channels), F32)
     groups = list(zip(GRADIENT_GROUPS[:-1], GRADIENT_GROUPS[1:]))
 
+    slope_in = copies(slope_semaphore, (slope_hbm, slope_ref))[0]
     no_halo_rows(shifted, rows, columns)
     around = turned_weights(fields_ref[...], columns)
 
@@ -433,14 +437,17 @@
             center = pulled[inner * columns : (inner + 1) * columns, :]
             fill_row(shifted, index * per + inner + 1, center, zero, zero)
 
-    for index in range(steps):
+    for index in range(SPREAD_AHEAD):
         spread(index)
+    slope_in.wait()
     out = []
     for number, (low, high) in enumerate(groups):
         if number == 0:
             fill(0)
         for index in range(low, high):
             if index + 1 < steps:
+                if index + 1 >= SPREAD_AHEAD:
+                    spread(index + 1)
                 fill(index + 1)
             part = slice(index * CHUNK, (index + 1) * CHUNK)
             out_ref[part, :] += convolve_rows(shifted, weight_ref, part.start, CHUNK, columns, True)
@@ -515,7 +522,7 @@
             )
         )
         leaving[-1].start()
-    for copy in waiting[1:]:
+    for copy in waiting[1:6]:
         copy.wait()
     top, bottom, west, east = halo_terms(
         left_ref[...].astype(F32),
@@ -526,6 +533,8 @@
         weight_ref,
         True,
     )
+    for copy in waiting[6:]:
+        copy.wait()
     lines_ref[0] += top[8 : columns - 8]
     lines_ref[1] += bottom[8 : columns - 8]
     leaving += copies(out_semaphores, *places[:2])
@@ -589,10 +598,10 @@
     departures_hbm,
     adjoint_hbm,
     fields_hbm,
-    west_ref,
-    east_ref,
-    top_ref,
-    bottom_ref,
+    west_hbm,
+    east_hbm,
+    top_hbm,
+    bottom_hbm,
     box_ref,
     grid_ref,
     weight_in_ref,
@@ -613,6 +622,8 @@
     departures_ref,
     adjoint,
     fields_ref,
+    sides_ref,
+    lines_ref,
     semaphores,
     out_semaphores,
 ):
@@ -671,6 +682,7 @@
         conv_ref,
         False,
     )
+    departures_ref[:, channels:] = jnp.zeros((slots, META), BF16)
     for copy in waiting[6:10]:
         copy.wait()
     place = iota((16, grid_channels), 0)
@@ -741,16 +753,22 @@
         )
     spread = dot_nn(jnp.concatenate(weights, axis=0), adjoint[...])
     cells_out = []
-    for index, edge_ref in enumerate((top_ref, bottom_ref)):
+    for index in range(2):
         first = index * columns
         pulled = ends_ref[index].astype(F32) * spread[first : first + columns]
-        edge_ref[...] = pulled.astype(BF16)
+        lines_ref[index] = pulled.astype(BF16)
         cells_out += [pulled[:1], pulled[columns - 1 :]]
-    for index, edge_ref in enumerate((west_ref, east_ref)):
+    for index in range(2):
         first = 2 * columns + index * rows
         slope = borders_ref[index * rows : (index + 1) * rows, :]
-        edge_ref[...] = (slope * spread[first : first + rows]).astype(BF16)
-    departures_ref[:, channels:] = jnp.zeros((slots, META), BF16)
+        sides_ref[index] = (slope * spread[first : first + rows]).astype(BF16)
+    results += copies(
+        out_semaphores.at[pl.ds(1 + len(results), 4)],
+        (sides_ref.at[0], west_hbm),
+        (sides_ref.at[1], east_hbm),
+        (lines_ref.at[0], top_hbm),
+        (lines_ref.at[1], bottom_hbm),
+    )
     corners_out(cells_out, lat, lon, capacity, departures_ref, channels)
     results += copies(
         out_semaphores.at[pl.ds(1 + len(results), 1)],
@@ -888,7 +906,7 @@
             sds((columns, channels), BF16),
             sds((columns, channels), BF16),
         ),
-        (HBM,) * 3 + (VMEM,) * 4,
+        (HBM,) * 7,
         (HBM,) * 16,
         (
             pltpu.VMEM((slots, bands + META), BF16),
@@ -905,8 +923,10 @@
             pltpu.VMEM((slots, bands + META), BF16),
             pltpu.VMEM((slots, channels), BF16),
             pltpu.VMEM((16, slots), F32),
+            pltpu.VMEM((2, rows, channels), BF16),
+            pltpu.VMEM((2, columns, channels), BF16),
             dma((18,)),
-            dma((6,)),
+            dma((10,)),
         ),
         flops=2 * network_flops + 2 * slots * cells * channels,
         moved=2 * cells * channels,
@@ -934,15 +954,17 @@
         functools.partial(gradient_kernel, columns),
         (sds((cells, channels), F32),),
         (HBM,),
-        (VMEM,) * 4,
+        (VMEM, VMEM, HBM, VMEM),
         (
+            pltpu.VMEM((cells, channels), BF16),
             pltpu.VMEM((cells, channels), F32),
             shifted,
+            dma((1,)),
             dma((steps,)),
         ),
         flops=conv_flops + 2 * slots * cells * channels,
         moved=4 * cells * channels,
-        room=30720,
+        room=9216,
         name="gradient",
     )(adjoint, fields, flat_slope, conv_weight)
     gradient, departures = kernel_call(

time: 73.5 us -> 72.7 us (0.989)
  local copies, waits for them, and re-layouts: 2.61 us -> 1.03 us
  waiting for transfers between devices: 3.85 us -> 5.2 us
    unnamed x36 -> x34, local copies, waits for them, and re-layouts: 2.61 us -> 1.03 us
    all_to_all x2, waiting for transfers between devices: 3.83 us -> 5.18 us  [exchange(): lax.all_to_all(box.reshape(devices, capacity, -1), ('lat', 'lon'), split_...]
  transfers between devices with their start and end apart: 10 -> 10, of which waited for: 2 -> 2; matrix products, arithmetic and copies ran while one was open for 0% -> 0% of each run, Pallas kernels for 23% -> 24%
where the time goes in v5:
time: 72.7 us; the launch traced here: 72.4 us
  Pallas kernels  33.2 us (46%)
  starting transfers between devices  31.8 us (44%)
  waiting for transfers between devices  5.2 us (7%)
  between operations  1.11 us (2%)
  local copies, waits for them, and re-layouts  1.03 us (1%)
    all_to_all x2, starting transfers between devices, exchange(): lax.all_to_all(box.reshape(devices, capacity, -1), ('lat', 'lon'), split_...  16.6 us
    pallas_call x1, Pallas kernels, body(): kernel_call(functools.partial(observe_kernel, columns, capacity), (sds((s...  9.38 us
    pallas_call x1, Pallas kernels, body(): kernel_call(functools.partial(gradient_kernel, columns), (sds((cells, cha...  8.91 us
    ppermute x2, starting transfers between devices, beside(): lax.ppermute(west, 'lon', [(target, source) for source, target in onward])  8.48 us
    pallas_call x1, Pallas kernels, body(): kernel_call(functools.partial(forecast_kernel, columns), (sds((cells, cha...  8.44 us
    all_to_all x2, waiting for transfers between devices, exchange(): lax.all_to_all(box.reshape(devices, capacity, -1), ('lat', 'lon'), split_...  5.18 us
    ppermute x2, starting transfers between devices, over(): north = lax.ppermute(bottom, 'lat', down)  3.45 us
    pallas_call x1, Pallas kernels, body(): kernel_call(functools.partial(dispatch_kernel, capacity), (sds((slots, ba...  3.3 us
  transfers between devices with their start and end apart: 10, of which 2 were waited for; matrix products, arithmetic and copies ran while one was open for 0% of the time, Pallas kernels for 24%

profile of v5, /device:TPU:1, one launch (start us, length us, event | category | flops | bytes accessed | tf_op | source)
XLA Modules:
  0.0 72.4 jit_solution(7946047572594997883)
XLA Ops:
  0.6 3.3 %dispatch.1 = (bf16[1024,512]{1,0:T(8,128)(2,1)}, s32[1,512]{1,0:T(1,128)}, bf16[32,256]{1,0:T(8,128)(2,1)}, bf16[32,256]{1,0:T(8,128)(2,1)}, bf16[128,256]{1,0:T(8,128)(2,1)}, /*index=5*/bf16[128,256]{1,0:T(8,128)(2,1)}) custom-call(s32[1,512]{1,0:T(1,128)} %bitcast.17, s32[1,512]{1,0:T(1,128)} %bitcast.18, f32[2,512]{1,0:T(2,128)} %bitcast.16, ...), custom_call_target="tpu_custom_call" | custom-call | flops 536870912 | bytes 1048576 | tf_op jit(solution)/shard_map/dispatch/pallas_call | solution.py:829
  3.9 0.0 copy-start.16
  3.9 0.0 copy-start.15
  4.0 0.0 copy-start.10
  4.0 0.0 copy-start.8
  4.0 11.5 %all-to-all-start = ((bf16[128,8,512]{2,1,0:T(8,128)(2,1)}), bf16[128,8,512]{2,1,0:T(8,128)(2,1)S(1)}, u32[]{:S(2)}, u32[]{:S(2)}) async-start(bf16[128,8,512]{2,1,0:T(8,128)(2,1)} %bitcast.15), calls=%async_computation | async-start | bytes 2097152 | tf_op jit(solution)/shard_map/all_to_all | solution.py:825
  15.5 0.0 copy-done.16
  15.5 1.6 %collective-permute-start = (bf16[32,256]{1,0:T(8,128)(2,1)S(1)}, bf16[32,256]{1,0:T(8,128)(2,1)S(1)}, u32[]{:S(2)}, u32[]{:S(2)}) collective-permute-start(bf16[32,256]{1,0:T(8,128)(2,1)S(1)} %copy-done.16), channel_id=1, source_target_pairs={{0,1},{1,2},{2,3},{3,4},{4,5},{5,6},{6,7},{7,8},{8,9},{9,10},{10,1... | collective-permute-start | bytes 49160 | tf_op jit(solution)/shard_map/ppermute | solution.py:785
  17.1 0.0 copy-done.15
  17.1 4.3 %collective-permute-start.1 = (bf16[32,256]{1,0:T(8,128)(2,1)S(1)}, bf16[32,256]{1,0:T(8,128)(2,1)S(1)}, u32[]{:S(2)}, u32[]{:S(2)}) collective-permute-start(bf16[32,256]{1,0:T(8,128)(2,1)S(1)} %copy-done.15), channel_id=1, source_target_pairs={{1,0},{2,1},{3,2},{4,3},{5,4},{6,5},{7,6},{8,7},{9,8},{10,9},{11,1... | collective-permute-start | bytes 49160 | tf_op jit(solution)/shard_map/ppermute | solution.py:786
  21.4 0.0 copy-done.10
  21.4 1.7 %collective-permute-start.2 = (bf16[128,256]{1,0:T(8,128)(2,1)S(1)}, bf16[128,256]{1,0:T(8,128)(2,1)S(1)}, u32[]{:S(2)}, u32[]{:S(2)}) collective-permute-start(bf16[128,256]{1,0:T(8,128)(2,1)S(1)} %copy-done.10), channel_id=1, source_target_pairs={{0,16},{16,32},{32,48},{48,64},{64,80},{80,96},{96,112},{112,0},{1... | collective-permute-start | bytes 196616 | tf_op jit(solution)/shard_map/ppermute | solution.py:793
  23.1 0.0 copy-done.8
  23.1 0.0 collective-permute-start.3
  23.1 8.4 %forecast.1 = (bf16[4096,256]{1,0:T(8,128)(2,1)}, f32[384,256]{1,0:T(8,128)}) custom-call(bf16[4096,256]{1,0:T(8,128)(2,1)} %bitcast.12, bf16[4096,256]{1,0:T(8,128)(2,1)} %bitcast.19, bf16[3,3,256,256]{3,2,1,0:T(8,128)(2,1)} %weight_hbm.3), custom_call_target="tpu_custom_call" | custom-call | flops 4831838208 | bytes 6291456 | tf_op jit(solution)/shard_map/forecast/pallas_call | solution.py:874
  31.6 0.0 collective-permute-done.left_hbm
  31.6 0.0 copy-start.11
  31.6 0.0 collective-permute-done.1.right_hbm
  31.6 0.0 copy-start.12
  31.6 0.0 collective-permute-done.2.north_hbm
  31.6 0.0 copy-start.7
  31.7 0.0 collective-permute-done.3.south_hbm
  31.7 0.0 copy-start.9
  31.7 2.7 %all-to-all-done = bf16[128,8,512]{2,1,0:T(8,128)(2,1)S(1)} async-done(((bf16[128,8,512]{2,1,0:T(8,128)(2,1)}), bf16[128,8,512]{2,1,0:T(8,128)(2,1)S(1)}, u32[]{:S(2)}, u32[]{:S(2)}) %all-to-all-start) | async-done | bytes 1048608 | tf_op jit(solution)/shard_map/all_to_all | solution.py:825
  34.4 0.0 copy-start.4
  34.4 0.0 copy-done.11
  34.4 0.0 copy-done.12
  34.4 0.0 copy-done.7
  34.4 0.0 copy-done.9
  34.4 1.0 %copy-done.4 = bf16[128,8,512]{2,1,0:T(8,128)(2,1)} copy-done((bf16[128,8,512]{2,1,0:T(8,128)(2,1)}, bf16[128,8,512]{2,1,0:T(8,128)(2,1)S(1)}, u32[]{:S(2)}) %copy-start.4) | copy-done | bytes 1048600
  35.4 9.4 %observe.1 = (bf16[1024,512]{1,0:T(8,128)(2,1)}, bf16[1024,256]{1,0:T(8,128)(2,1)}, f32[16,1024]{1,0:T(8,128)}, bf16[32,256]{1,0:T(8,128)(2,1)}, bf16[32,256]{1,...) custom-call(bf16[1024,512]{1,0:T(8,128)(2,1)} %bitcast.13, ...), custom_call_target="tpu_custom_call" | custom-call | flops 4563402752 | bytes 2097152 | tf_op jit(solution)/shard_map/observe/pallas_call | solution.py:898
  44.8 0.0 copy-start.14
  44.8 0.0 copy-start.13
  44.8 0.0 copy-start.6
  44.8 0.0 copy-start.5
  44.8 0.0 copy-start
  44.8 0.0 copy-start.2
  44.8 0.0 copy-start.3
  44.9 5.1 %all-to-all-start.1 = ((bf16[128,8,512]{2,1,0:T(8,128)(2,1)}), bf16[128,8,512]{2,1,0:T(8,128)(2,1)S(1)}, u32[]{:S(2)}, u32[]{:S(2)}) async-start(bf16[128,8,512]{2,1,0:T(8,128)(2,1)} %bitcast.14), calls=%async_computation.1 | async-start | bytes 2097152 | tf_op jit(solution)/shard_map/all_to_all | solution.py:825
  49.9 0.0 copy-done.14
  49.9 1.7 %collective-permute-start.4 = (bf16[32,256]{1,0:T(8,128)(2,1)S(1)}, bf16[32,256]{1,0:T(8,128)(2,1)S(1)}, u32[]{:S(2)}, u32[]{:S(2)}) collective-permute-start(bf16[32,256]{1,0:T(8,128)(2,1)S(1)} %copy-done.14), channel_id=1, source_target_pairs={{0,1},{1,2},{2,3},{3,4},{4,5},{5,6},{6,7},{7,8},{8,9},{9,10},{10,1... | collective-permute-start | bytes 49160 | tf_op jit(solution)/shard_map/ppermute | solution.py:785
  51.7 0.0 copy-done.13
  51.7 4.2 %collective-permute-start.5 = (bf16[32,256]{1,0:T(8,128)(2,1)S(1)}, bf16[32,256]{1,0:T(8,128)(2,1)S(1)}, u32[]{:S(2)}, u32[]{:S(2)}) collective-permute-start(bf16[32,256]{1,0:T(8,128)(2,1)S(1)} %copy-done.13), channel_id=1, source_target_pairs={{1,0},{2,1},{3,2},{4,3},{5,4},{6,5},{7,6},{8,7},{9,8},{10,9},{11,1... | collective-permute-start | bytes 49160 | tf_op jit(solution)/shard_map/ppermute | solution.py:786
  55.8 0.0 copy-done.6
  55.8 1.7 %collective-permute-start.6 = (bf16[128,256]{1,0:T(8,128)(2,1)S(1)}, bf16[128,256]{1,0:T(8,128)(2,1)S(1)}, u32[]{:S(2)}, u32[]{:S(2)}) collective-permute-start(bf16[128,256]{1,0:T(8,128)(2,1)S(1)} %copy-done.6), channel_id=1, source_target_pairs={{0,16},{16,32},{32,48},{48,64},{64,80},{80,96},{96,112},{112,0},{1... | collective-permute-start | bytes 196616 | tf_op jit(solution)/shard_map/ppermute | solution.py:793
  57.5 0.0 copy-done.5
  57.5 0.0 collective-permute-start.7
  57.5 0.0 copy-done
  57.5 0.0 copy-done.2
  57.6 0.0 copy-done.3
  57.6 0.0 copy-start.1
  57.6 8.9 %gradient.1 = f32[4096,256]{1,0:T(8,128)} custom-call(bf16[1024,256]{1,0:T(8,128)(2,1)S(1)} %copy-done.2, f32[16,1024]{1,0:T(8,128)S(1)} %copy-done.3, bf16[4096,256]{1,0:T(8,128)(2,1)} %bitcast.21, bf16[3,3,256,256]{3,2,1,0:T(8,128)(2,1)S(1)} %copy-done), custom_call_target="tpu_custom_call" | custom-call | flops 6979321856 | bytes 4194304 | tf_op jit(solution)/shard_map/gradient/pallas_call | solution.py:953
  66.5 0.0 collective-permute-done.4.left_hbm
  66.5 0.0 collective-permute-done.5.right_hbm
  66.5 0.0 collective-permute-done.6.north_hbm
  66.5 0.0 collective-permute-done.7.south_hbm
  66.5 2.4 %all-to-all-done.1 = bf16[128,8,512]{2,1,0:T(8,128)(2,1)S(1)} async-done(((bf16[128,8,512]{2,1,0:T(8,128)(2,1)}), bf16[128,8,512]{2,1,0:T(8,128)(2,1)S(1)}, u32[]{:S(2)}, u32[]{:S(2)}) %all-to-all-start.1) | async-done | bytes 1048608 | tf_op jit(solution)/shard_map/all_to_all | solution.py:825
  69.0 0.0 copy-done.1
  69.0 3.2 %finish.1 = (f32[32,128,256]{2,1,0:T(8,128)}, f32[512,384]{1,0:T(8,128)}) custom-call(f32[32,128,256]{2,1,0:T(8,128)} %bitcast.11, s32[1,512]{1,0:T(1,128)S(1)} %copy-done.1, bf16[1024,512]{1,0:T(8,128)(2,1)S(1)} %bitcast.10, bf16[3,3,256,256]{3,2,1,0:T(8,128)(2,1)S(1)} %copy-done, ...), custom_call_target="tpu_custom_call", output_to_operand_aliasing={{0}: (0, {})} | custom-call | flops 402653184 | bytes 786432 | tf_op jit(solution)/shard_map/finish/pallas_call | solution.py:970
Async XLA Ops:
  3.9 11.6 %copy-start.16 = (bf16[32,256]{1,0:T(8,128)(2,1)S(1)}, bf16[32,256]{1,0:T(8,128)(2,1)}, u32[]{:S(2)}) copy-start(bf16[32,256]{1,0:T(8,128)(2,1)} %get-tuple-element.22) | copy-start | bytes 49156
  3.9 13.1 %copy-start.15 = (bf16[32,256]{1,0:T(8,128)(2,1)S(1)}, bf16[32,256]{1,0:T(8,128)(2,1)}, u32[]{:S(2)}) copy-start(bf16[32,256]{1,0:T(8,128)(2,1)} %get-tuple-element.23) | copy-start | bytes 49156
  4.0 17.5 %copy-start.10 = (bf16[128,256]{1,0:T(8,128)(2,1)S(1)}, bf16[128,256]{1,0:T(8,128)(2,1)}, u32[]{:S(2)}) copy-start(bf16[128,256]{1,0:T(8,128)(2,1)} %get-tuple-element.24) | copy-start | bytes 196612
  4.0 19.2 %copy-start.8 = (bf16[128,256]{1,0:T(8,128)(2,1)S(1)}, bf16[128,256]{1,0:T(8,128)(2,1)}, u32[]{:S(2)}) copy-start(bf16[128,256]{1,0:T(8,128)(2,1)} %get-tuple-element.25) | copy-start | bytes 196612
  4.0 30.4 %all-to-all-start = ((bf16[128,8,512]{2,1,0:T(8,128)(2,1)}), bf16[128,8,512]{2,1,0:T(8,128)(2,1)S(1)}, u32[]{:S(2)}, u32[]{:S(2)}) async-start(bf16[128,8,512]{2,1,0:T(8,128)(2,1)} %bitcast.15), calls=%async_computation | async-start | bytes 2097152 | tf_op jit(solution)/shard_map/all_to_all | solution.py:825
  15.5 16.1 %collective-permute-start = (bf16[32,256]{1,0:T(8,128)(2,1)S(1)}, bf16[32,256]{1,0:T(8,128)(2,1)S(1)}, u32[]{:S(2)}, u32[]{:S(2)}) collective-permute-start(bf16[32,256]{1,0:T(8,128)(2,1)S(1)} %copy-done.16), channel_id=1, source_target_pairs={{0,1},{1,2},{2,3},{3,4},{4,5},{5,6},{6,7},{7,8},{8,9},{9,10},{10,1... | collective-permute-start | bytes 49160 | tf_op jit(solution)/shard_map/ppermute | solution.py:785
  17.1 14.5 %collective-permute-start.1 = (bf16[32,256]{1,0:T(8,128)(2,1)S(1)}, bf16[32,256]{1,0:T(8,128)(2,1)S(1)}, u32[]{:S(2)}, u32[]{:S(2)}) collective-permute-start(bf16[32,256]{1,0:T(8,128)(2,1)S(1)} %copy-done.15), channel_id=1, source_target_pairs={{1,0},{2,1},{3,2},{4,3},{5,4},{6,5},{7,6},{8,7},{9,8},{10,9},{11,1... | collective-permute-start | bytes 49160 | tf_op jit(solution)/shard_map/ppermute | solution.py:786
  21.4 10.2 %collective-permute-start.2 = (bf16[128,256]{1,0:T(8,128)(2,1)S(1)}, bf16[128,256]{1,0:T(8,128)(2,1)S(1)}, u32[]{:S(2)}, u32[]{:S(2)}) collective-permute-start(bf16[128,256]{1,0:T(8,128)(2,1)S(1)} %copy-done.10), channel_id=1, source_target_pairs={{0,16},{16,32},{32,48},{48,64},{64,80},{80,96},{96,112},{112,0},{1... | collective-permute-start | bytes 196616 | tf_op jit(solution)/shard_map/ppermute | solution.py:793
  23.1 8.5 %collective-permute-start.3 = (bf16[128,256]{1,0:T(8,128)(2,1)S(1)}, bf16[128,256]{1,0:T(8,128)(2,1)S(1)}, u32[]{:S(2)}, u32[]{:S(2)}) collective-permute-start(bf16[128,256]{1,0:T(8,128)(2,1)S(1)} %copy-done.8), channel_id=1, source_target_pairs={{16,0},{32,16},{48,32},{64,48},{80,64},{96,80},{112,96},{0,112},{1... | collective-permute-start | bytes 196616 | tf_op jit(solution)/shard_map/ppermute | solution.py:794
  31.6 2.8 %copy-start.11 = (bf16[32,256]{1,0:T(8,128)(2,1)}, bf16[32,256]{1,0:T(8,128)(2,1)S(1)}, u32[]{:S(2)}) copy-start(bf16[32,256]{1,0:T(8,128)(2,1)S(1)} %collective-permute-done.left_hbm) | copy-start | bytes 49156
  31.6 2.8 %copy-start.12 = (bf16[32,256]{1,0:T(8,128)(2,1)}, bf16[32,256]{1,0:T(8,128)(2,1)S(1)}, u32[]{:S(2)}) copy-start(bf16[32,256]{1,0:T(8,128)(2,1)S(1)} %collective-permute-done.1.right_hbm) | copy-start | bytes 49156
  31.6 2.8 %copy-start.7 = (bf16[128,256]{1,0:T(8,128)(2,1)}, bf16[128,256]{1,0:T(8,128)(2,1)S(1)}, u32[]{:S(2)}) copy-start(bf16[128,256]{1,0:T(8,128)(2,1)S(1)} %collective-permute-done.2.north_hbm) | copy-start | bytes 196612
  31.7 2.8 %copy-start.9 = (bf16[128,256]{1,0:T(8,128)(2,1)}, bf16[128,256]{1,0:T(8,128)(2,1)S(1)}, u32[]{:S(2)}) copy-start(bf16[128,256]{1,0:T(8,128)(2,1)S(1)} %collective-permute-done.3.south_hbm) | copy-start | bytes 196612
  34.4 1.0 %copy-start.4 = (bf16[128,8,512]{2,1,0:T(8,128)(2,1)}, bf16[128,8,512]{2,1,0:T(8,128)(2,1)S(1)}, u32[]{:S(2)}) copy-start(bf16[128,8,512]{2,1,0:T(8,128)(2,1)S(1)} %all-to-all-done) | copy-start | bytes 3145732
  44.8 5.2 %copy-start.14 = (bf16[32,256]{1,0:T(8,128)(2,1)S(1)}, bf16[32,256]{1,0:T(8,128)(2,1)}, u32[]{:S(2)}) copy-start(bf16[32,256]{1,0:T(8,128)(2,1)} %get-tuple-element.30) | copy-start | bytes 49156
  44.8 6.9 %copy-start.13 = (bf16[32,256]{1,0:T(8,128)(2,1)S(1)}, bf16[32,256]{1,0:T(8,128)(2,1)}, u32[]{:S(2)}) copy-start(bf16[32,256]{1,0:T(8,128)(2,1)} %get-tuple-element.31) | copy-start | bytes 49156
  44.8 11.0 %copy-start.6 = (bf16[128,256]{1,0:T(8,128)(2,1)S(1)}, bf16[128,256]{1,0:T(8,128)(2,1)}, u32[]{:S(2)}) copy-start(bf16[128,256]{1,0:T(8,128)(2,1)} %get-tuple-element.32) | copy-start | bytes 196612
  44.8 12.7 %copy-start.5 = (bf16[128,256]{1,0:T(8,128)(2,1)S(1)}, bf16[128,256]{1,0:T(8,128)(2,1)}, u32[]{:S(2)}) copy-start(bf16[128,256]{1,0:T(8,128)(2,1)} %get-tuple-element.33) | copy-start | bytes 196612
  44.8 12.7 %copy-start = (bf16[3,3,256,256]{3,2,1,0:T(8,128)(2,1)S(1)}, bf16[3,3,256,256]{3,2,1,0:T(8,128)(2,1)}, u32[]{:S(2)}) copy-start(bf16[3,3,256,256]{3,2,1,0:T(8,128)(2,1)} %weight_hbm.3) | copy-start | bytes 3538948
  44.8 12.7 %copy-start.2 = (bf16[1024,256]{1,0:T(8,128)(2,1)S(1)}, bf16[1024,256]{1,0:T(8,128)(2,1)}, u32[]{:S(2)}) copy-start(bf16[1024,256]{1,0:T(8,128)(2,1)} %get-tuple-element.26.adjoint) | copy-start | bytes 1572868
  44.8 12.7 %copy-start.3 = (f32[16,1024]{1,0:T(8,128)S(1)}, f32[16,1024]{1,0:T(8,128)}, u32[]{:S(2)}) copy-start(f32[16,1024]{1,0:T(8,128)} %get-tuple-element.27.fields_ref) | copy-start | bytes 196612
  44.9 24.1 %all-to-all-start.1 = ((bf16[128,8,512]{2,1,0:T(8,128)(2,1)}), bf16[128,8,512]{2,1,0:T(8,128)(2,1)S(1)}, u32[]{:S(2)}, u32[]{:S(2)}) async-start(bf16[128,8,512]{2,1,0:T(8,128)(2,1)} %bitcast.14), calls=%async_computation.1 | async-start | bytes 2097152 | tf_op jit(solution)/shard_map/all_to_all | solution.py:825
  49.9 16.6 %collective-permute-start.4 = (bf16[32,256]{1,0:T(8,128)(2,1)S(1)}, bf16[32,256]{1,0:T(8,128)(2,1)S(1)}, u32[]{:S(2)}, u32[]{:S(2)}) collective-permute-start(bf16[32,256]{1,0:T(8,128)(2,1)S(1)} %copy-done.14), channel_id=1, source_target_pairs={{0,1},{1,2},{2,3},{3,4},{4,5},{5,6},{6,7},{7,8},{8,9},{9,10},{10,1... | collective-permute-start | bytes 49160 | tf_op jit(solution)/shard_map/ppermute | solution.py:785
  51.7 14.9 %collective-permute-start.5 = (bf16[32,256]{1,0:T(8,128)(2,1)S(1)}, bf16[32,256]{1,0:T(8,128)(2,1)S(1)}, u32[]{:S(2)}, u32[]{:S(2)}) collective-permute-start(bf16[32,256]{1,0:T(8,128)(2,1)S(1)} %copy-done.13), channel_id=1, source_target_pairs={{1,0},{2,1},{3,2},{4,3},{5,4},{6,5},{7,6},{8,7},{9,8},{10,9},{11,1... | collective-permute-start | bytes 49160 | tf_op jit(solution)/shard_map/ppermute | solution.py:786
  55.8 10.7 %collective-permute-start.6 = (bf16[128,256]{1,0:T(8,128)(2,1)S(1)}, bf16[128,256]{1,0:T(8,128)(2,1)S(1)}, u32[]{:S(2)}, u32[]{:S(2)}) collective-permute-start(bf16[128,256]{1,0:T(8,128)(2,1)S(1)} %copy-done.6), channel_id=1, source_target_pairs={{0,16},{16,32},{32,48},{48,64},{64,80},{80,96},{96,112},{112,0},{1... | collective-permute-start | bytes 196616 | tf_op jit(solution)/shard_map/ppermute | solution.py:793
  57.5 9.0 %collective-permute-start.7 = (bf16[128,256]{1,0:T(8,128)(2,1)S(1)}, bf16[128,256]{1,0:T(8,128)(2,1)S(1)}, u32[]{:S(2)}, u32[]{:S(2)}) collective-permute-start(bf16[128,256]{1,0:T(8,128)(2,1)S(1)} %copy-done.5), channel_id=1, source_target_pairs={{16,0},{32,16},{48,32},{64,48},{80,64},{96,80},{112,96},{0,112},{1... | collective-permute-start | bytes 196616 | tf_op jit(solution)/shard_map/ppermute | solution.py:794
  57.6 11.4 %copy-start.1 = (s32[1,512]{1,0:T(1,128)S(1)}, s32[1,512]{1,0:T(1,128)}, u32[]{:S(2)}) copy-start(s32[1,512]{1,0:T(1,128)} %get-tuple-element.28.slot_hbm) | copy-start | bytes 6148

commit v6 on v5

--- a/solution.py
+++ b/solution.py
@@ -88,12 +88,9 @@
     half = (iota((16, META), 0) // 8) * 8
     for index, (inside, first, own) in enumerate(diagonal_blocks(lat, lon, capacity)):
         lines = folded[8 * index : 8 * index + 8]
-        lines = jnp.where(half == own, jnp.concatenate([lines, lines], axis=0), 0.0)
-
-        @pl.when(inside)
-        def _():
-            which = pl.ds(first, 16)
-            box_ref[which, channels:] = (box_ref[which, channels:].astype(F32) + lines).astype(BF16)
+        lines = jnp.where((half == own) & inside, jnp.concatenate([lines, lines], axis=0), 0.0)
+        which = pl.ds(first, 16)
+        box_ref[which, channels:] = (box_ref[which, channels:].astype(F32) + lines).astype(BF16)
 
 
 def corners_in(box_ref, lat, lon, capacity, channels, width):
@@ -199,14 +196,14 @@
         leaving[-1].start()
     cells = (cells[0], cells[2], cells[1], cells[3])
     places = []
-    step = slots // 2
-    for index in range(2):
+    step = slots // 4
+    for index in range(4):
         part = slice(index * step, (index + 1) * step)
         places.append((iota((step, count), 0) + index * step == slot).astype(F32).astype(BF16))
         box_ref[part, channels:] = dot_nt(places[index], meta).astype(BF16)
     corners_out(cells, lat, lon, capacity, box_ref, channels)
     waiting[3].wait()
-    for index in range(2):
+    for index in range(4):
         part = slice(index * step, (index + 1) * step)
         box_ref[part, :channels] = dot_nn(places[index], radiance_ref[...]).astype(BF16)
         leaving.append(
@@ -851,7 +848,7 @@
             pltpu.VMEM((rows, channels), BF16),
             pltpu.VMEM((2, columns, channels), BF16),
             dma((8,)),
-            dma((7,)),
+            dma((9,)),
         ),
         flops=2 * slots * count * (bands + META),
         moved=2 * slots * (bands + META),

time: 72.7 us -> 72.7 us (level)
  no operation moved by 1% of the time
where the time goes in v6:
time: 72.7 us; the launch traced here: 72.3 us
  Pallas kernels  33.1 us (46%)
  starting transfers between devices  31.9 us (44%)
  waiting for transfers between devices  5.2 us (7%)
  between operations  1.11 us (2%)
  local copies, waits for them, and re-layouts  1.03 us (1%)
    all_to_all x2, starting transfers between devices, exchange(): lax.all_to_all(box.reshape(devices, capacity, -1), ('lat', 'lon'), split_...  16.6 us
    pallas_call x1, Pallas kernels, body(): kernel_call(functools.partial(observe_kernel, columns, capacity), (sds((s...  9.34 us
    pallas_call x1, Pallas kernels, body(): kernel_call(functools.partial(gradient_kernel, columns), (sds((cells, cha...  8.91 us
    ppermute x2, starting transfers between devices, beside(): lax.ppermute(west, 'lon', [(target, source) for source, target in onward])  8.48 us
    pallas_call x1, Pallas kernels, body(): kernel_call(functools.partial(forecast_kernel, columns), (sds((cells, cha...  8.43 us
    all_to_all x2, waiting for transfers between devices, exchange(): lax.all_to_all(box.reshape(devices, capacity, -1), ('lat', 'lon'), split_...  5.18 us
    ppermute x2, starting transfers between devices, over(): north = lax.ppermute(bottom, 'lat', down)  3.45 us
    ppermute x2, starting transfers between devices, beside(): left = lax.ppermute(east, 'lon', onward)  3.29 us
  transfers between devices with their start and end apart: 10, of which 2 were waited for; matrix products, arithmetic and copies ran while one was open for 0% of the time, Pallas kernels for 24%

profile of v6, /device:TPU:1, one launch (start us, length us, event | category | flops | bytes accessed | tf_op | source)
XLA Modules:
  0.0 72.3 jit_solution(4940890978579221625)
XLA Ops:
  0.6 3.2 %dispatch.1 = (bf16[1024,512]{1,0:T(8,128)(2,1)}, s32[1,512]{1,0:T(1,128)}, bf16[32,256]{1,0:T(8,128)(2,1)}, bf16[32,256]{1,0:T(8,128)(2,1)}, bf16[128,256]{1,0:T(8,128)(2,1)}, /*index=5*/bf16[128,256]{1,0:T(8,128)(2,1)}) custom-call(s32[1,512]{1,0:T(1,128)} %bitcast.17, s32[1,512]{1,0:T(1,128)} %bitcast.18, f32[2,512]{1,0:T(2,128)} %bitcast.16, ...), custom_call_target="tpu_custom_call" | custom-call | flops 536870912 | bytes 1048576 | tf_op jit(solution)/shard_map/dispatch/pallas_call | solution.py:826
  3.9 0.0 copy-start.16
  3.9 0.0 copy-start.15
  3.9 0.0 copy-start.10
  3.9 0.0 copy-start.8
  3.9 11.5 %all-to-all-start = ((bf16[128,8,512]{2,1,0:T(8,128)(2,1)}), bf16[128,8,512]{2,1,0:T(8,128)(2,1)S(1)}, u32[]{:S(2)}, u32[]{:S(2)}) async-start(bf16[128,8,512]{2,1,0:T(8,128)(2,1)} %bitcast.15), calls=%async_computation | async-start | bytes 2097152 | tf_op jit(solution)/shard_map/all_to_all | solution.py:822
  15.4 0.0 copy-done.16
  15.4 1.6 %collective-permute-start = (bf16[32,256]{1,0:T(8,128)(2,1)S(1)}, bf16[32,256]{1,0:T(8,128)(2,1)S(1)}, u32[]{:S(2)}, u32[]{:S(2)}) collective-permute-start(bf16[32,256]{1,0:T(8,128)(2,1)S(1)} %copy-done.16), channel_id=1, source_target_pairs={{0,1},{1,2},{2,3},{3,4},{4,5},{5,6},{6,7},{7,8},{8,9},{9,10},{10,1... | collective-permute-start | bytes 49160 | tf_op jit(solution)/shard_map/ppermute | solution.py:782
  17.0 0.0 copy-done.15
  17.0 4.3 %collective-permute-start.1 = (bf16[32,256]{1,0:T(8,128)(2,1)S(1)}, bf16[32,256]{1,0:T(8,128)(2,1)S(1)}, u32[]{:S(2)}, u32[]{:S(2)}) collective-permute-start(bf16[32,256]{1,0:T(8,128)(2,1)S(1)} %copy-done.15), channel_id=1, source_target_pairs={{1,0},{2,1},{3,2},{4,3},{5,4},{6,5},{7,6},{8,7},{9,8},{10,9},{11,1... | collective-permute-start | bytes 49160 | tf_op jit(solution)/shard_map/ppermute | solution.py:783
  21.4 0.0 copy-done.10
  21.4 1.7 %collective-permute-start.2 = (bf16[128,256]{1,0:T(8,128)(2,1)S(1)}, bf16[128,256]{1,0:T(8,128)(2,1)S(1)}, u32[]{:S(2)}, u32[]{:S(2)}) collective-permute-start(bf16[128,256]{1,0:T(8,128)(2,1)S(1)} %copy-done.10), channel_id=1, source_target_pairs={{0,16},{16,32},{32,48},{48,64},{64,80},{80,96},{96,112},{112,0},{1... | collective-permute-start | bytes 196616 | tf_op jit(solution)/shard_map/ppermute | solution.py:790
  23.1 0.0 copy-done.8
  23.1 0.0 collective-permute-start.3
  23.1 8.4 %forecast.1 = (bf16[4096,256]{1,0:T(8,128)(2,1)}, f32[384,256]{1,0:T(8,128)}) custom-call(bf16[4096,256]{1,0:T(8,128)(2,1)} %bitcast.12, bf16[4096,256]{1,0:T(8,128)(2,1)} %bitcast.19, bf16[3,3,256,256]{3,2,1,0:T(8,128)(2,1)} %weight_hbm.3), custom_call_target="tpu_custom_call" | custom-call | flops 4831838208 | bytes 6291456 | tf_op jit(solution)/shard_map/forecast/pallas_call | solution.py:871
  31.5 0.0 collective-permute-done.left_hbm
  31.5 0.0 copy-start.11
  31.6 0.0 collective-permute-done.1.right_hbm
  31.6 0.0 copy-start.12
  31.6 0.0 collective-permute-done.2.north_hbm
  31.6 0.0 copy-start.7
  31.6 0.0 collective-permute-done.3.south_hbm
  31.6 0.0 copy-start.9
  31.6 2.7 %all-to-all-done = bf16[128,8,512]{2,1,0:T(8,128)(2,1)S(1)} async-done(((bf16[128,8,512]{2,1,0:T(8,128)(2,1)}), bf16[128,8,512]{2,1,0:T(8,128)(2,1)S(1)}, u32[]{:S(2)}, u32[]{:S(2)}) %all-to-all-start) | async-done | bytes 1048608 | tf_op jit(solution)/shard_map/all_to_all | solution.py:822
  34.4 0.0 copy-start.4
  34.4 0.0 copy-done.11
  34.4 0.0 copy-done.12
  34.4 0.0 copy-done.7
  34.4 0.0 copy-done.9
  34.4 1.0 %copy-done.4 = bf16[128,8,512]{2,1,0:T(8,128)(2,1)} copy-done((bf16[128,8,512]{2,1,0:T(8,128)(2,1)}, bf16[128,8,512]{2,1,0:T(8,128)(2,1)S(1)}, u32[]{:S(2)}) %copy-start.4) | copy-done | bytes 1048600
  35.3 9.3 %observe.1 = (bf16[1024,512]{1,0:T(8,128)(2,1)}, bf16[1024,256]{1,0:T(8,128)(2,1)}, f32[16,1024]{1,0:T(8,128)}, bf16[32,256]{1,0:T(8,128)(2,1)}, bf16[32,256]{1,...) custom-call(bf16[1024,512]{1,0:T(8,128)(2,1)} %bitcast.13, ...), custom_call_target="tpu_custom_call" | custom-call | flops 4563402752 | bytes 2097152 | tf_op jit(solution)/shard_map/observe/pallas_call | solution.py:895
  44.7 0.0 copy-start.14
  44.7 0.0 copy-start.13
  44.7 0.0 copy-start.6
  44.7 0.0 copy-start.5
  44.7 0.0 copy-start
  44.7 0.0 copy-start.2
  44.7 0.0 copy-start.3
  44.7 5.1 %all-to-all-start.1 = ((bf16[128,8,512]{2,1,0:T(8,128)(2,1)}), bf16[128,8,512]{2,1,0:T(8,128)(2,1)S(1)}, u32[]{:S(2)}, u32[]{:S(2)}) async-start(bf16[128,8,512]{2,1,0:T(8,128)(2,1)} %bitcast.14), calls=%async_computation.1 | async-start | bytes 2097152 | tf_op jit(solution)/shard_map/all_to_all | solution.py:822
  49.9 0.0 copy-done.14
  49.9 1.7 %collective-permute-start.4 = (bf16[32,256]{1,0:T(8,128)(2,1)S(1)}, bf16[32,256]{1,0:T(8,128)(2,1)S(1)}, u32[]{:S(2)}, u32[]{:S(2)}) collective-permute-start(bf16[32,256]{1,0:T(8,128)(2,1)S(1)} %copy-done.14), channel_id=1, source_target_pairs={{0,1},{1,2},{2,3},{3,4},{4,5},{5,6},{6,7},{7,8},{8,9},{9,10},{10,1... | collective-permute-start | bytes 49160 | tf_op jit(solution)/shard_map/ppermute | solution.py:782
  51.6 0.0 copy-done.13
  51.6 4.2 %collective-permute-start.5 = (bf16[32,256]{1,0:T(8,128)(2,1)S(1)}, bf16[32,256]{1,0:T(8,128)(2,1)S(1)}, u32[]{:S(2)}, u32[]{:S(2)}) collective-permute-start(bf16[32,256]{1,0:T(8,128)(2,1)S(1)} %copy-done.13), channel_id=1, source_target_pairs={{1,0},{2,1},{3,2},{4,3},{5,4},{6,5},{7,6},{8,7},{9,8},{10,9},{11,1... | collective-permute-start | bytes 49160 | tf_op jit(solution)/shard_map/ppermute | solution.py:783
  55.8 0.0 copy-done.6
  55.8 1.7 %collective-permute-start.6 = (bf16[128,256]{1,0:T(8,128)(2,1)S(1)}, bf16[128,256]{1,0:T(8,128)(2,1)S(1)}, u32[]{:S(2)}, u32[]{:S(2)}) collective-permute-start(bf16[128,256]{1,0:T(8,128)(2,1)S(1)} %copy-done.6), channel_id=1, source_target_pairs={{0,16},{16,32},{32,48},{48,64},{64,80},{80,96},{96,112},{112,0},{1... | collective-permute-start | bytes 196616 | tf_op jit(solution)/shard_map/ppermute | solution.py:790
  57.5 0.0 copy-done.5
  57.5 0.0 collective-permute-start.7
  57.5 0.0 copy-done
  57.5 0.0 copy-done.2
  57.5 0.0 copy-done.3
  57.5 0.0 copy-start.1
  57.6 8.9 %gradient.1 = f32[4096,256]{1,0:T(8,128)} custom-call(bf16[1024,256]{1,0:T(8,128)(2,1)S(1)} %copy-done.2, f32[16,1024]{1,0:T(8,128)S(1)} %copy-done.3, bf16[4096,256]{1,0:T(8,128)(2,1)} %bitcast.21, bf16[3,3,256,256]{3,2,1,0:T(8,128)(2,1)S(1)} %copy-done), custom_call_target="tpu_custom_call" | custom-call | flops 6979321856 | bytes 4194304 | tf_op jit(solution)/shard_map/gradient/pallas_call | solution.py:950
  66.5 0.0 collective-permute-done.4.left_hbm
  66.5 0.0 collective-permute-done.5.right_hbm
  66.5 0.0 collective-permute-done.6.north_hbm
  66.5 0.0 collective-permute-done.7.south_hbm
  66.5 2.4 %all-to-all-done.1 = bf16[128,8,512]{2,1,0:T(8,128)(2,1)S(1)} async-done(((bf16[128,8,512]{2,1,0:T(8,128)(2,1)}), bf16[128,8,512]{2,1,0:T(8,128)(2,1)S(1)}, u32[]{:S(2)}, u32[]{:S(2)}) %all-to-all-start.1) | async-done | bytes 1048608 | tf_op jit(solution)/shard_map/all_to_all | solution.py:822
  69.0 0.0 copy-done.1
  69.0 3.2 %finish.1 = (f32[32,128,256]{2,1,0:T(8,128)}, f32[512,384]{1,0:T(8,128)}) custom-call(f32[32,128,256]{2,1,0:T(8,128)} %bitcast.11, s32[1,512]{1,0:T(1,128)S(1)} %copy-done.1, bf16[1024,512]{1,0:T(8,128)(2,1)S(1)} %bitcast.10, bf16[3,3,256,256]{3,2,1,0:T(8,128)(2,1)S(1)} %copy-done, ...), custom_call_target="tpu_custom_call", output_to_operand_aliasing={{0}: (0, {})} | custom-call | flops 402653184 | bytes 786432 | tf_op jit(solution)/shard_map/finish/pallas_call | solution.py:967
Async XLA Ops:
  3.9 11.6 %copy-start.16 = (bf16[32,256]{1,0:T(8,128)(2,1)S(1)}, bf16[32,256]{1,0:T(8,128)(2,1)}, u32[]{:S(2)}) copy-start(bf16[32,256]{1,0:T(8,128)(2,1)} %get-tuple-element.22) | copy-start | bytes 49156
  3.9 13.1 %copy-start.15 = (bf16[32,256]{1,0:T(8,128)(2,1)S(1)}, bf16[32,256]{1,0:T(8,128)(2,1)}, u32[]{:S(2)}) copy-start(bf16[32,256]{1,0:T(8,128)(2,1)} %get-tuple-element.23) | copy-start | bytes 49156
  3.9 17.5 %copy-start.10 = (bf16[128,256]{1,0:T(8,128)(2,1)S(1)}, bf16[128,256]{1,0:T(8,128)(2,1)}, u32[]{:S(2)}) copy-start(bf16[128,256]{1,0:T(8,128)(2,1)} %get-tuple-element.24) | copy-start | bytes 196612
  3.9 19.2 %copy-start.8 = (bf16[128,256]{1,0:T(8,128)(2,1)S(1)}, bf16[128,256]{1,0:T(8,128)(2,1)}, u32[]{:S(2)}) copy-start(bf16[128,256]{1,0:T(8,128)(2,1)} %get-tuple-element.25) | copy-start | bytes 196612
  3.9 30.4 %all-to-all-start = ((bf16[128,8,512]{2,1,0:T(8,128)(2,1)}), bf16[128,8,512]{2,1,0:T(8,128)(2,1)S(1)}, u32[]{:S(2)}, u32[]{:S(2)}) async-start(bf16[128,8,512]{2,1,0:T(8,128)(2,1)} %bitcast.15), calls=%async_computation | async-start | bytes 2097152 | tf_op jit(solution)/shard_map/all_to_all | solution.py:822
  15.4 16.1 %collective-permute-start = (bf16[32,256]{1,0:T(8,128)(2,1)S(1)}, bf16[32,256]{1,0:T(8,128)(2,1)S(1)}, u32[]{:S(2)}, u32[]{:S(2)}) collective-permute-start(bf16[32,256]{1,0:T(8,128)(2,1)S(1)} %copy-done.16), channel_id=1, source_target_pairs={{0,1},{1,2},{2,3},{3,4},{4,5},{5,6},{6,7},{7,8},{8,9},{9,10},{10,1... | collective-permute-start | bytes 49160 | tf_op jit(solution)/shard_map/ppermute | solution.py:782
  17.0 14.5 %collective-permute-start.1 = (bf16[32,256]{1,0:T(8,128)(2,1)S(1)}, bf16[32,256]{1,0:T(8,128)(2,1)S(1)}, u32[]{:S(2)}, u32[]{:S(2)}) collective-permute-start(bf16[32,256]{1,0:T(8,128)(2,1)S(1)} %copy-done.15), channel_id=1, source_target_pairs={{1,0},{2,1},{3,2},{4,3},{5,4},{6,5},{7,6},{8,7},{9,8},{10,9},{11,1... | collective-permute-start | bytes 49160 | tf_op jit(solution)/shard_map/ppermute | solution.py:783
  21.4 10.2 %collective-permute-start.2 = (bf16[128,256]{1,0:T(8,128)(2,1)S(1)}, bf16[128,256]{1,0:T(8,128)(2,1)S(1)}, u32[]{:S(2)}, u32[]{:S(2)}) collective-permute-start(bf16[128,256]{1,0:T(8,128)(2,1)S(1)} %copy-done.10), channel_id=1, source_target_pairs={{0,16},{16,32},{32,48},{48,64},{64,80},{80,96},{96,112},{112,0},{1... | collective-permute-start | bytes 196616 | tf_op jit(solution)/shard_map/ppermute | solution.py:790
  23.1 8.5 %collective-permute-start.3 = (bf16[128,256]{1,0:T(8,128)(2,1)S(1)}, bf16[128,256]{1,0:T(8,128)(2,1)S(1)}, u32[]{:S(2)}, u32[]{:S(2)}) collective-permute-start(bf16[128,256]{1,0:T(8,128)(2,1)S(1)} %copy-done.8), channel_id=1, source_target_pairs={{16,0},{32,16},{48,32},{64,48},{80,64},{96,80},{112,96},{0,112},{1... | collective-permute-start | bytes 196616 | tf_op jit(solution)/shard_map/ppermute | solution.py:791
  31.5 2.8 %copy-start.11 = (bf16[32,256]{1,0:T(8,128)(2,1)}, bf16[32,256]{1,0:T(8,128)(2,1)S(1)}, u32[]{:S(2)}) copy-start(bf16[32,256]{1,0:T(8,128)(2,1)S(1)} %collective-permute-done.left_hbm) | copy-start | bytes 49156
  31.6 2.8 %copy-start.12 = (bf16[32,256]{1,0:T(8,128)(2,1)}, bf16[32,256]{1,0:T(8,128)(2,1)S(1)}, u32[]{:S(2)}) copy-start(bf16[32,256]{1,0:T(8,128)(2,1)S(1)} %collective-permute-done.1.right_hbm) | copy-start | bytes 49156
  31.6 2.8 %copy-start.7 = (bf16[128,256]{1,0:T(8,128)(2,1)}, bf16[128,256]{1,0:T(8,128)(2,1)S(1)}, u32[]{:S(2)}) copy-start(bf16[128,256]{1,0:T(8,128)(2,1)S(1)} %collective-permute-done.2.north_hbm) | copy-start | bytes 196612
  31.6 2.8 %copy-start.9 = (bf16[128,256]{1,0:T(8,128)(2,1)}, bf16[128,256]{1,0:T(8,128)(2,1)S(1)}, u32[]{:S(2)}) copy-start(bf16[128,256]{1,0:T(8,128)(2,1)S(1)} %collective-permute-done.3.south_hbm) | copy-start | bytes 196612
  34.4 1.0 %copy-start.4 = (bf16[128,8,512]{2,1,0:T(8,128)(2,1)}, bf16[128,8,512]{2,1,0:T(8,128)(2,1)S(1)}, u32[]{:S(2)}) copy-start(bf16[128,8,512]{2,1,0:T(8,128)(2,1)S(1)} %all-to-all-done) | copy-start | bytes 3145732
  44.7 5.2 %copy-start.14 = (bf16[32,256]{1,0:T(8,128)(2,1)S(1)}, bf16[32,256]{1,0:T(8,128)(2,1)}, u32[]{:S(2)}) copy-start(bf16[32,256]{1,0:T(8,128)(2,1)} %get-tuple-element.30) | copy-start | bytes 49156
  44.7 6.9 %copy-start.13 = (bf16[32,256]{1,0:T(8,128)(2,1)S(1)}, bf16[32,256]{1,0:T(8,128)(2,1)}, u32[]{:S(2)}) copy-start(bf16[32,256]{1,0:T(8,128)(2,1)} %get-tuple-element.31) | copy-start | bytes 49156
  44.7 11.1 %copy-start.6 = (bf16[128,256]{1,0:T(8,128)(2,1)S(1)}, bf16[128,256]{1,0:T(8,128)(2,1)}, u32[]{:S(2)}) copy-start(bf16[128,256]{1,0:T(8,128)(2,1)} %get-tuple-element.32) | copy-start | bytes 196612
  44.7 12.8 %copy-start.5 = (bf16[128,256]{1,0:T(8,128)(2,1)S(1)}, bf16[128,256]{1,0:T(8,128)(2,1)}, u32[]{:S(2)}) copy-start(bf16[128,256]{1,0:T(8,128)(2,1)} %get-tuple-element.33) | copy-start | bytes 196612
  44.7 12.8 %copy-start = (bf16[3,3,256,256]{3,2,1,0:T(8,128)(2,1)S(1)}, bf16[3,3,256,256]{3,2,1,0:T(8,128)(2,1)}, u32[]{:S(2)}) copy-start(bf16[3,3,256,256]{3,2,1,0:T(8,128)(2,1)} %weight_hbm.3) | copy-start | bytes 3538948
  44.7 12.8 %copy-start.2 = (bf16[1024,256]{1,0:T(8,128)(2,1)S(1)}, bf16[1024,256]{1,0:T(8,128)(2,1)}, u32[]{:S(2)}) copy-start(bf16[1024,256]{1,0:T(8,128)(2,1)} %get-tuple-element.26.adjoint) | copy-start | bytes 1572868
  44.7 12.8 %copy-start.3 = (f32[16,1024]{1,0:T(8,128)S(1)}, f32[16,1024]{1,0:T(8,128)}, u32[]{:S(2)}) copy-start(f32[16,1024]{1,0:T(8,128)} %get-tuple-element.27.fields_ref) | copy-start | bytes 196612
  44.7 24.2 %all-to-all-start.1 = ((bf16[128,8,512]{2,1,0:T(8,128)(2,1)}), bf16[128,8,512]{2,1,0:T(8,128)(2,1)S(1)}, u32[]{:S(2)}, u32[]{:S(2)}) async-start(bf16[128,8,512]{2,1,0:T(8,128)(2,1)} %bitcast.14), calls=%async_computation.1 | async-start | bytes 2097152 | tf_op jit(solution)/shard_map/all_to_all | solution.py:822
  49.9 16.6 %collective-permute-start.4 = (bf16[32,256]{1,0:T(8,128)(2,1)S(1)}, bf16[32,256]{1,0:T(8,128)(2,1)S(1)}, u32[]{:S(2)}, u32[]{:S(2)}) collective-permute-start(bf16[32,256]{1,0:T(8,128)(2,1)S(1)} %copy-done.14), channel_id=1, source_target_pairs={{0,1},{1,2},{2,3},{3,4},{4,5},{5,6},{6,7},{7,8},{8,9},{9,10},{10,1... | collective-permute-start | bytes 49160 | tf_op jit(solution)/shard_map/ppermute | solution.py:782
  51.6 14.8 %collective-permute-start.5 = (bf16[32,256]{1,0:T(8,128)(2,1)S(1)}, bf16[32,256]{1,0:T(8,128)(2,1)S(1)}, u32[]{:S(2)}, u32[]{:S(2)}) collective-permute-start(bf16[32,256]{1,0:T(8,128)(2,1)S(1)} %copy-done.13), channel_id=1, source_target_pairs={{1,0},{2,1},{3,2},{4,3},{5,4},{6,5},{7,6},{8,7},{9,8},{10,9},{11,1... | collective-permute-start | bytes 49160 | tf_op jit(solution)/shard_map/ppermute | solution.py:783
  55.8 10.7 %collective-permute-start.6 = (bf16[128,256]{1,0:T(8,128)(2,1)S(1)}, bf16[128,256]{1,0:T(8,128)(2,1)S(1)}, u32[]{:S(2)}, u32[]{:S(2)}) collective-permute-start(bf16[128,256]{1,0:T(8,128)(2,1)S(1)} %copy-done.6), channel_id=1, source_target_pairs={{0,16},{16,32},{32,48},{48,64},{64,80},{80,96},{96,112},{112,0},{1... | collective-permute-start | bytes 196616 | tf_op jit(solution)/shard_map/ppermute | solution.py:790
  57.5 9.0 %collective-permute-start.7 = (bf16[128,256]{1,0:T(8,128)(2,1)S(1)}, bf16[128,256]{1,0:T(8,128)(2,1)S(1)}, u32[]{:S(2)}, u32[]{:S(2)}) collective-permute-start(bf16[128,256]{1,0:T(8,128)(2,1)S(1)} %copy-done.5), channel_id=1, source_target_pairs={{16,0},{32,16},{48,32},{64,48},{80,64},{96,80},{112,96},{0,112},{1... | collective-permute-start | bytes 196616 | tf_op jit(solution)/shard_map/ppermute | solution.py:791
  57.5 11.4 %copy-start.1 = (s32[1,512]{1,0:T(1,128)S(1)}, s32[1,512]{1,0:T(1,128)}, u32[]{:S(2)}) copy-start(s32[1,512]{1,0:T(1,128)} %get-tuple-element.28.slot_hbm) | copy-start | bytes 6148
